TPU v7x, 32 devices: a whole 2x2x4 slice. The times are simulated.
32 devices in a mesh: row: 8 (over y, x, core), col: 4 (over z).
Axes of the slice: x: 2, y: 2, z: 4, core: 2. Of those that a mesh axis runs over, the one named last changes fastest.
Arguments:
- a_vals: bfloat16 [8, 4, 2, 6, 5, 128, 128], P('row', 'col'), may hold values from -6 to 6
- a_cols: int32 [8, 4, 2, 6, 5], P('row', 'col'), may hold values from 0 to 5, as said below
- b_vals: bfloat16 [8, 4, 6, 8, 128, 128], P('row', 'col'), may hold values from -0.15625 to 0.15625
- b_cols: int32 [8, 4, 6, 8], P('row', 'col'), may hold values from 0 to 11, as said below
- c_cols: int32 [8, 4, 6, 6], P('row', 'col'), may hold values from 0 to 11, as said below
- panel_owner: int32 [8, 8], replicated, may hold values from 0 to 7, as said below
- atom_size: int32 [48], replicated, may hold values from 64 to 128
Outputs:
- product_blocks: bfloat16 [8, 4, 6, 6, 128, 128], P('row', 'col')
Inputs may be any that keep to these rules, and one draw needn't show every extreme that they name: `a_cols`: the 5 indices of one block row are distinct. `b_cols`: the 8 indices of one block row are distinct. `c_cols`: the 6 indices of one block row are distinct. `panel_owner`: each row is a permutation.
All inputs are finite; a program needn't handle non-finite values.
Results may differ from a plain program's by a relative error of at most 0.001.
Values may be sent and summed in bfloat16 or wider, within the bound.
No kernel may reach another device: no remote copies, remote signals or barrier semaphores. Data moves between devices by JAX's collectives and lax.ppermute only.
A program may use at most 128 MiB of HBM per device.

v0:
```python
import functools

import jax
import jax.numpy as jnp
from jax import lax
from jax.experimental import pallas as pl
from jax.experimental.pallas import tpu as pltpu
from jax.sharding import PartitionSpec as P

STEPS = 2
SHARES = (15, 21, 22, 22, 22, 18)
PIECES = len(SHARES)
NOTED = 1
NOTE = 16
MIB = 1024 * 1024

SMEM = pl.BlockSpec(memory_space=pltpu.SMEM)
VMEM = pl.BlockSpec(memory_space=pltpu.VMEM)
ANYWHERE = pl.BlockSpec(memory_space=pl.ANY)


def places_of(owner_ref):
    row_id, row_count = lax.axis_index("row"), lax.axis_size("row")
    panels = [lax.rem(row_id + t, row_count) for t in range(STEPS)]
    places = [owner_ref[row_id, k] for k in panels]
    return panels, [lax.div(p, 2) for p in places], [lax.rem(p, 2) for p in places]


def lag_of(hop, hops):
    return hop + (2 * hop >= hops)


def cut(rows, size):
    total = STEPS * rows * size
    pieces, at = [], 0
    for piece in range(PIECES):
        begin, end = at, total * sum(SHARES[: piece + 1]) // sum(SHARES)
        segments = []
        while at < end:
            unit, first = divmod(at, size)
            count = min(size - first, end - at)
            segments.append((unit % STEPS, unit // STEPS, first, count, at - begin))
            at += count
        if piece == NOTED:
            segments += [(t, -1, 0, NOTE, end - begin + t * NOTE) for t in range(STEPS)]
        pieces.append(tuple(segments))
    return pieces


def extent_of(segments):
    return max(offset + count for _, _, _, count, offset in segments)


def relay_kernel(roles, waits, owner, own, *refs):
    refs = list(refs)
    notes = refs.pop(0) if any(i < 0 for segments, _, _ in roles for _, i, _, _, _ in segments) else None
    arrivals = [refs.pop(0) if arrives else None for _, _, arrives in roles]
    del refs[:waits]
    onward, sem = refs
    _, holders, slots = places_of(owner)
    col_id, last = lax.axis_index("col"), lax.axis_size("col") - 1
    jobs = []
    for place, (segments, hop, _) in enumerate(roles):
        sends = (col_id == hop) | (col_id == last - hop)
        for n, (t, i, first, count, offset) in enumerate(segments):
            mine = sends if hop == 0 else sends & (holders[t] == col_id)
            src = notes.at[slots[t]] if i < 0 else own.at[slots[t], i, pl.ds(first, count)]
            jobs.append((mine, pltpu.make_async_copy(src, onward.at[pl.ds(offset, count)], sem.at[place, n])))
    for when, copy in jobs:
        pl.when(when)(copy.start)
    for (segments, hop, _), arrived in zip(roles, arrivals):
        if arrived is None:
            continue
        sends = (col_id == hop) | (col_id == last - hop)
        for t, _, _, count, offset in segments:

            @pl.when(sends & (holders[t] != col_id))
            def _():
                onward[offset : offset + count] = arrived[offset : offset + count]

    for when, copy in jobs:
        pl.when(when)(copy.wait)


def relay(owner, own, notes, roles, arrivals, after, limit, flops, name):
    noted = any(i < 0 for segments, _ in roles for _, i, _, _, _ in segments)
    size = max(extent_of(segments) for segments, _ in roles)
    given = [a for a in arrivals if a is not None]
    operands = [owner, own] + [notes] * noted + given + after
    specs = [SMEM, ANYWHERE] + [ANYWHERE] * noted + [VMEM] * len(given)
    specs += [pl.BlockSpec(memory_space=pltpu.HBM) if name == "lane0_1" else ANYWHERE] * len(after)
    roles = tuple((segments, hop, a is not None) for (segments, hop), a in zip(roles, arrivals))
    return pl.pallas_call(
        functools.partial(relay_kernel, roles, len(after)),
        out_shape=jax.ShapeDtypeStruct((size, own.shape[3]), own.dtype),
        in_specs=specs,
        out_specs=VMEM,
        scratch_shapes=[pltpu.SemaphoreType.DMA((2, max(len(segments) for segments, _, _ in roles)))],
        compiler_params=pltpu.CompilerParams(vmem_limit_bytes=limit),
        cost_estimate=pl.CostEstimate(flops=flops, bytes_accessed=1024, transcendentals=0),
        name=name,
    )(*operands)


def plan_kernel(nz, spots, owner, atoms, bcols0, bcols1, ccols, notes, *refs):
    arrivals, (plan, note_vm, ccols_vm) = refs[:-4], refs[-3:]
    panels, holders, slots = places_of(owner)
    row_id, col_id, col_count = lax.axis_index("row"), lax.axis_index("col"), lax.axis_size("col")
    panel_rows, nzb = bcols0.shape
    rows, kept = ccols.shape
    lanes = plan.shape[1]
    width = STEPS * nz
    sizes_at, row_at = kept * width, (kept + 1) * width
    for t in range(STEPS):
        hop = jnp.where(holders[t] < col_id, col_id - 1, col_count - 2 - col_id)
        mine = holders[t] == col_id

        @pl.when(mine)
        def _():
            note_vm[t] = notes[slots[t]]

        for h, arrived in enumerate(arrivals):

            @pl.when(jnp.logical_not(mine) & (hop == h))
            def _():
                note_vm[t] = arrived[spots[t] : spots[t] + NOTE]

    ccols_vm[...] = jnp.zeros_like(ccols_vm)
    ccols_vm[:rows, :kept] = ccols[...].astype(jnp.float32)

    source = lax.broadcasted_iota(jnp.int32, (lanes, lanes), 0)
    target = lax.broadcasted_iota(jnp.int32, (lanes, lanes), 1)

    def spread(values, hits):
        return jnp.dot(values, hits.astype(jnp.float32).astype(jnp.bfloat16), preferred_element_type=jnp.float32)

    lane = lax.broadcasted_iota(jnp.int32, plan.shape, 1)
    line = lax.broadcasted_iota(jnp.int32, plan.shape, 0)
    inner = jnp.zeros(plan.shape, jnp.float32)
    second = jnp.zeros(plan.shape, jnp.bool_)
    for t in range(STEPS):
        hits = source < 0
        for e in range(kept + 1):
            at = e * width + t * nz
            hits = hits | (target == source + at)
            if t:
                second = second | ((lane >= at) & (lane < at + nz))
        inner = inner + spread(note_vm[t], hits & (source < nz))
    inner = inner.astype(jnp.int32) + jnp.where(second, panel_rows, 0)
    hits = target == source + row_at + 1
    for e in range(kept):
        hits = hits | ((source == e) & (target >= e * width) & (target < (e + 1) * width))
    column = spread(ccols_vm[...].astype(jnp.bfloat16), hits & (source < kept)).astype(jnp.int32)

    block = jnp.full(plan.shape, -1, jnp.int32)
    size = jnp.zeros(plan.shape, jnp.int32)
    for t, bcols in enumerate((bcols0, bcols1)):
        for j in range(panel_rows):
            here = inner == t * panel_rows + j
            size = jnp.where(here, atoms[panels[t] * panel_rows + j], size)
            for n in range(nzb):
                block = jnp.where(here & (column == bcols[j, n]), j * nzb + n, block)
    col_size = jnp.zeros(plan.shape, jnp.int32)
    for c in range(2 * rows):
        col_size = jnp.where(column == c, atoms[col_id * 2 * rows + c], col_size)
    row_size = jnp.zeros(plan.shape, jnp.int32)
    for i in range(rows):
        row_size = jnp.where(line == i, atoms[row_id * panel_rows + i], row_size)
    tail = jnp.where(lane == row_at, row_size, col_size)
    plan[...] = jnp.where(lane < sizes_at, block, jnp.where(lane < row_at, size, tail))


def make_plan(owner, atoms, bcols0, bcols1, ccols, notes, arrivals, nz, spots, after):
    operands = [owner, atoms, bcols0, bcols1, ccols, notes, *arrivals, after]
    return pl.pallas_call(
        functools.partial(plan_kernel, nz, spots),
        out_shape=jax.ShapeDtypeStruct(notes.shape[1:], jnp.int32),
        in_specs=[SMEM] * 4 + [VMEM] * (2 + len(arrivals)) + [ANYWHERE],
        out_specs=VMEM,
        scratch_shapes=[pltpu.VMEM(notes.shape, notes.dtype), pltpu.VMEM(notes.shape[1:], jnp.float32)],
        compiler_params=pltpu.CompilerParams(vmem_limit_bytes=8 * MIB),
        cost_estimate=pl.CostEstimate(flops=10**9, bytes_accessed=1024, transcendentals=0),
        name="make_plan",
    )(*operands)


def rows_kernel(first, count, hops, sources, owner, plan, b0, b1, own, *refs):
    places = 1 + max(source[0] for source in sources)
    arrived = [refs[at * hops : (at + 1) * hops] for at in range(places)]
    out, a_vm, left_vm, o_vm, a_sem, o_sem = refs[-6:]
    kept, blk = o_vm.shape[1], o_vm.shape[-1]
    size = a_vm.shape[2]
    nz = size // blk
    width = STEPS * nz
    col_id, last = lax.axis_index("col"), lax.axis_size("col") - 1
    _, holders, slots = places_of(owner)
    copies = []
    for at in range(count):
        for t in range(STEPS):
            copy = pltpu.make_async_copy(own.at[slots[t], first + at], a_vm.at[at, t], a_sem.at[at, t])
            copies.append((holders[t] == col_id, copy))
    for when, copy in copies:
        pl.when(when)(copy.start)
    for t in range(STEPS):
        hop = jnp.where(holders[t] < col_id, col_id - 1, last - 1 - col_id)
        for h in range(hops):

            @pl.when((holders[t] != col_id) & (hop == h))
            def _():
                for place, step, i, start, lines, offset in sources:
                    if step == t:
                        a_vm[i - first, t, start : start + lines] = arrived[place][h][offset : offset + lines]

    for when, copy in copies:
        pl.when(when)(copy.wait)

    lane = lax.broadcasted_iota(jnp.int32, (blk, blk), 1)
    sub = lax.broadcasted_iota(jnp.int32, (blk, blk), 0)
    flat = [b.reshape(b.shape[0] * b.shape[1], blk, blk) for b in (b0, b1)]

    def one_row(at, carry):
        i = first + at
        for t in range(STEPS):
            for m in range(nz):
                q = t * nz + m
                left_vm[:, q * blk : (q + 1) * blk] = jnp.where(
                    lane < plan[i, kept * width + q],
                    a_vm[at, t, m * blk : (m + 1) * blk],
                    jnp.zeros((), a_vm.dtype),
                )
        row_size = plan[i, kept * width + width]

        for p in range(kept // 2):
            sides = []
            for e in range(2):
                parts = []
                for q in range(width):
                    n = plan[i, (2 * p + e) * width + q]
                    block = flat[q // nz][jnp.maximum(n, 0)]
                    parts.append(jnp.where(n >= 0, block, jnp.zeros((), block.dtype)))
                sides.append(jnp.concatenate(parts, axis=0))
            total = jnp.dot(
                left_vm[...], jnp.concatenate(sides, axis=1), preferred_element_type=jnp.float32
            )
            for e in range(2):
                col_size = plan[i, kept * width + width + 1 + 2 * p + e]
                inside = (sub < row_size) & (lane < col_size)
                part = total[:, e * blk : (e + 1) * blk]
                o_vm[at, 2 * p + e] = jnp.where(inside, part, 0.0).astype(o_vm.dtype)
        pltpu.make_async_copy(o_vm.at[at], out.at[i], o_sem.at[at]).start()
        return carry

    lax.fori_loop(0, count, one_row, 0)
    for at in range(count):
        pltpu.make_async_copy(o_vm.at[at], out.at[first + at], o_sem.at[at]).wait()


def multiply_rows(first, count, owner, plan, b_panels, own, pieces, arrived, kept, so_far):
    rows, size, blk = own.shape[1:]
    nz, hops = size // blk, len(arrived[0])
    operands = [owner, plan, *b_panels, own]
    sources, places = [], 0
    for piece, segments in enumerate(pieces):
        found = [segment for segment in segments if first <= segment[1] < first + count]
        if found:
            sources += [(places, *segment) for segment in found]
            operands += arrived[piece]
            places += 1
    specs = [SMEM] * 2 + [VMEM] * 2 + [ANYWHERE] + [VMEM] * (places * hops)
    aliases = {}
    if so_far is not None:
        aliases = {len(operands): 0}
        operands.append(so_far)
        specs.append(ANYWHERE)
    flops = 4 * count * blk * blk * blk * STEPS * nz * kept
    limit = (12 + places * hops // 2) * MIB
    return pl.pallas_call(
        functools.partial(rows_kernel, first, count, hops, tuple(sources)),
        out_shape=jax.ShapeDtypeStruct((rows, kept, blk, blk), jnp.bfloat16),
        in_specs=specs,
        out_specs=ANYWHERE,
        scratch_shapes=[
            pltpu.VMEM((count, STEPS, size, blk), jnp.bfloat16),
            pltpu.VMEM((blk, STEPS * size), jnp.bfloat16),
            pltpu.VMEM((count, kept, blk, blk), jnp.bfloat16),
            pltpu.SemaphoreType.DMA((count, STEPS)),
            pltpu.SemaphoreType.DMA((count,)),
        ],
        input_output_aliases=aliases,
        compiler_params=pltpu.CompilerParams(vmem_limit_bytes=limit),
        cost_estimate=pl.CostEstimate(flops=flops, bytes_accessed=4 * MIB, transcendentals=0),
        name="multiply_rows",
    )(*operands)


def local(a_vals, a_cols, b_vals, b_cols, c_cols, panel_owner, atom_size):
    row_count = lax.axis_size("row")
    col_count = lax.axis_size("col")
    stored_b, stored_bc = b_vals[0, 0], b_cols[0, 0]
    targets = c_cols[0, 0]
    slot_count, rows, nz, blk = a_vals.shape[2:6]
    own_a = a_vals.reshape(slot_count, rows, nz * blk, blk)
    notes = jnp.pad(
        a_cols[0, 0].astype(own_a.dtype), ((0, 0), (0, NOTE - rows), (0, blk - nz))
    )
    hops = col_count - 1
    from_next = [((i + 1) % row_count, i) for i in range(row_count)]

    pieces = cut(rows, nz * blk)
    spots = tuple(offset for _, i, _, _, offset in pieces[NOTED] if i < 0)
    arrived = [[None] * hops for _ in pieces]
    newest = plan = moved_b = moved_bc = None
    edges = {}
    last_slot = PIECES + lag_of(hops - 1, hops) - 1
    plan_slot = max(PIECES, NOTED + lag_of(hops - 1, hops) + 1)
    for slot in range(last_slot + 1):
        for lane in range((hops + 1) // 2):
            roles = []
            for hop in sorted({lane, hops - 1 - lane}):
                piece = slot - lag_of(hop, hops)
                if 0 <= piece < PIECES:
                    roles.append((piece, hop))
            if not roles:
                continue
            after = [newest] if slot > 1 else []
            if slot == lane == 1:
                after.append(moved_bc)
            if slot == PIECES and lane == 1:
                after.append(moved_b)
            before = slot - 2
            if lane == 0 and before > 0 and before in edges:
                after.append(edges[before])
            if slot == plan_slot and lane == 0:
                plan = make_plan(
                    panel_owner, atom_size, stored_bc, moved_bc[0, 0], targets, notes, arrived[NOTED], nz, spots, newest
                )
                after.append(plan)
            arrivals = [arrived[piece][hop - 1] if hop else None for piece, hop in roles]
            sent = [(pieces[piece], hop) for piece, hop in roles]
            flops = (3 - lane if slot == 2 else 2 if lane == 0 and slot == PIECES + 1 else 1) * 10**9
            limit = 62 * MIB if newest is None else 4 * MIB
            newest = relay(panel_owner, own_a, notes, sent, arrivals, after, limit, flops, f"lane{lane}_{slot}")
            if slot == 1 and lane == 0:
                behind_bc, newest = lax.optimization_barrier((b_cols, newest))
                moved_bc = lax.ppermute(behind_bc, "row", from_next)
                moved_bc, behind_b = lax.optimization_barrier((moved_bc, stored_b))
                moved_b = lax.ppermute(behind_b, "row", from_next)
            route = []
            for _, hop in roles:
                route += [(hop, hop + 1), (hops - hop, hops - hop - 1)]
            got = lax.ppermute(newest, "col", route)
            for piece, hop in roles:
                arrived[piece][hop] = got
            if lane == 0:
                edges[slot] = got

    result = None
    for first, count in ((0, rows - 2), (rows - 2, 2)):
        result = multiply_rows(
            first,
            count,
            panel_owner,
            plan,
            (stored_b, moved_b),
            own_a,
            pieces,
            arrived,
            targets.shape[1],
            result,
        )
    return result[None, None]


def solution(mesh):
    placed = (
        P("row", "col", None, None, None, None, None),
        P("row", "col", None, None, None),
        P("row", "col", None, None, None, None),
        P("row", "col", None, None),
        P("row", "col", None, None),
        P(),
        P(),
    )
    return jax.shard_map(
        local,
        mesh=mesh,
        in_specs=placed,
        out_specs=P("row", "col", None, None, None, None),
        check_vma=False,
    )
```

profile of v0, /device:TPU:0, one launch (start us, length us, event | category | flops | bytes accessed | tf_op | source)
XLA Modules:
  0.0 78.9 jit_solution(11512372321463707700)
XLA Ops:
  0.0 2.6 %lane0_0.1 = bf16[960,128]{1,0:T(8,128)(2,1)} custom-call(s32[8,8]{1,0:T(8,128)} %owner.35, bf16[2,6,640,128]{3,2,1,0:T(8,128)(2,1)} %bitcast.12), custom_call_target="tpu_custom_call" | custom-call | flops 1000000000 | bytes 1024 | tf_op jit(solution)/shard_map/lane0_0/pallas_call | solution.py:93
  2.6 4.0 %collective-permute-start.2 = (bf16[960,128]{1,0:T(8,128)(2,1)}, bf16[960,128]{1,0:T(8,128)(2,1)S(1)}, u32[]{:S(2)}, u32[]{:S(2)}) collective-permute-start(bf16[960,128]{1,0:T(8,128)(2,1)} %lane0_0.1), channel_id=1, source_target_pairs={{0,1},{3,2},{4,5},{7,6},{8,9},{11,10},{12,13},{15,14},{16,17},{19,... | collective-permute-start | bytes 737288 | tf_op jit(solution)/shard_map/ppermute | solution.py:351
  6.8 1.2 %lane0_1.1 = bf16[1376,128]{1,0:T(8,128)(2,1)S(1)} custom-call(s32[8,8]{1,0:T(8,128)S(1)} %copy-done.2, bf16[2,6,640,128]{3,2,1,0:T(8,128)(2,1)S(1)} %bitcast.13, bf16[2,16,128]{2,1,0:T(8,128)(2,1)S(1)} %pad.4.refs_0_.notes), custom_call_target="tpu_custom_call" | custom-call | flops 1000000000 | bytes 1024 | tf_op jit(solution)/shard_map/lane0_1/pallas_call | solution.py:93
  8.0 1.7 %collective-permute-start = (s32[1,1,6,8]{3,2,1,0:T(8,128)S(1)}, s32[1,1,6,8]{3,2,1,0:T(8,128)S(1)}, u32[]{:S(2)}, u32[]{:S(2)}) collective-permute-start(s32[1,1,6,8]{3,2,1,0:T(8,128)S(1)} %copy.10), channel_id=1, source_target_pairs={{4,0},{8,4},{12,8},{16,12},{20,16},{24,20},{28,24},{0,28},{5,1},{9... | collective-permute-start | bytes 584 | tf_op jit(solution)/shard_map/ppermute | solution.py:345
  9.6 1.3 %collective-permute-start.1 = (bf16[1376,128]{1,0:T(8,128)(2,1)S(1)}, bf16[1376,128]{1,0:T(8,128)(2,1)S(1)}, u32[]{:S(2)}, u32[]{:S(2)}) collective-permute-start(bf16[1376,128]{1,0:T(8,128)(2,1)S(1)} %lane0_1.1), channel_id=1, source_target_pairs={{0,1},{3,2},{4,5},{7,6},{8,9},{11,10},{12,13},{15,14},{16,17},{19,... | collective-permute-start | bytes 1056776 | tf_op jit(solution)/shard_map/ppermute | solution.py:351
  11.0 2.6 %collective-permute-start.9 = (bf16[6,8,128,128]{3,2,1,0:T(8,128)(2,1)S(1)}, bf16[6,8,128,128]{3,2,1,0:T(8,128)(2,1)S(1)}, u32[]{:S(2)}, u32[]{:S(2)}) collective-permute-start(bf16[6,8,128,128]{3,2,1,0:T(8,128)(2,1)S(1)} %bitcast.29), channel_id=1, source_target_pairs={{4,0},{8,4},{12,8},{16,12},{20,16},{24,20},{28,24},{0,28},{5,1},{9... | collective-permute-start | bytes 4718600 | tf_op jit(solution)/shard_map/ppermute | solution.py:347
  14.9 1.1 %lane0_2.1.refs_2_ = bf16[1408,128]{1,0:T(8,128)(2,1)S(1)} custom-call(s32[8,8]{1,0:T(8,128)S(1)} %copy-done.2, bf16[2,6,640,128]{3,2,1,0:T(8,128)(2,1)S(1)} %bitcast.15, bf16[960,128]{1,0:T(8,128)(2,1)S(1)} %lane1_1.1.refs_0_), custom_call_target="tpu_custom_call" | custom-call | flops 3000000000 | bytes 1024 | tf_op jit(solution)/shard_map/lane0_2/pallas_call | solution.py:93
  16.1 6.3 %collective-permute-start.4 = (bf16[1408,128]{1,0:T(8,128)(2,1)S(1)}, bf16[1408,128]{1,0:T(8,128)(2,1)S(1)}, u32[]{:S(2)}, u32[]{:S(2)}) collective-permute-start(bf16[1408,128]{1,0:T(8,128)(2,1)S(1)} %lane0_2.1.refs_2_), channel_id=1, source_target_pairs={{0,1},{3,2},{4,5},{7,6},{8,9},{11,10},{12,13},{15,14},{16,17},{19,... | collective-permute-start | bytes 1081352 | tf_op jit(solution)/shard_map/ppermute | solution.py:351
  23.9 1.2 %lane0_3.1.refs_1_ = bf16[1408,128]{1,0:T(8,128)(2,1)S(1)} custom-call(s32[8,8]{1,0:T(8,128)S(1)} %copy-done.2, bf16[2,6,640,128]{3,2,1,0:T(8,128)(2,1)S(1)} %bitcast.17, bf16[960,128]{1,0:T(8,128)(2,1)S(1)} %collective-permute-done.5.refs_0_.refs_1_, bf16[1376,128]{1,0:T(8,128)(2,1)S(1)} %lane1_2.1.refs_1_, ...), custom_call_target="tpu_custom_call" | custom-call | flops 1000000000 | bytes 1024 | tf_op jit(solution)/shard_map/lane0_3/pallas_call | solution.py:93
  25.0 2.9 %collective-permute-start.8 = (bf16[1408,128]{1,0:T(8,128)(2,1)S(1)}, bf16[1408,128]{1,0:T(8,128)(2,1)S(1)}, u32[]{:S(2)}, u32[]{:S(2)}) collective-permute-start(bf16[1408,128]{1,0:T(8,128)(2,1)S(1)} %lane0_3.1.refs_1_), channel_id=1, source_target_pairs={{0,1},{3,2},{2,3},{1,0},{4,5},{7,6},{6,7},{5,4},{8,9},{11,10},{10,... | collective-permute-start | bytes 1081352 | tf_op jit(solution)/shard_map/ppermute | solution.py:351
  28.0 2.0 %collective-permute-done.4.refs_0_.refs_3_.refs_6_ = bf16[1408,128]{1,0:T(8,128)(2,1)S(1)} collective-permute-done((bf16[1408,128]{1,0:T(8,128)(2,1)S(1)}, bf16[1408,128]{1,0:T(8,128)(2,1)S(1)}, u32[]{:S(2)}, u32[]{:S(2)}) %collective-permute-start.4) | collective-permute-done | bytes 360480 | tf_op jit(solution)/shard_map/ppermute | solution.py:351
  31.3 1.2 %lane0_4.1.refs_1_ = bf16[1408,128]{1,0:T(8,128)(2,1)S(1)} custom-call(s32[8,8]{1,0:T(8,128)S(1)} %copy-done.2, bf16[2,6,640,128]{3,2,1,0:T(8,128)(2,1)S(1)} %bitcast.19, bf16[2,16,128]{2,1,0:T(8,128)(2,1)S(1)} %pad.4.refs_0_.notes, bf16[1376,128]{1,0:T(8,128)(2,1)S(1)} %collective-permute-done.3.refs_1_.refs_4_, bf16[1408,128]{1,0:T(8,128)(2,1)S(1)} %lane1_3.1.refs_2_, ...), custom_call_target="tpu_custom_call" | custom-call | flops 1000000000 | bytes 1024 | tf_op jit(solution)/shard_map/lane0_4/pallas_call | solution.py:93
  32.6 5.0 %collective-permute-start.6 = (bf16[1408,128]{1,0:T(8,128)(2,1)S(1)}, bf16[1408,128]{1,0:T(8,128)(2,1)S(1)}, u32[]{:S(2)}, u32[]{:S(2)}) collective-permute-start(bf16[1408,128]{1,0:T(8,128)(2,1)S(1)} %lane0_4.1.refs_1_), channel_id=1, source_target_pairs={{0,1},{3,2},{2,3},{1,0},{4,5},{7,6},{6,7},{5,4},{8,9},{11,10},{10,... | collective-permute-start | bytes 1081352 | tf_op jit(solution)/shard_map/ppermute | solution.py:351
  39.1 1.1 %lane0_5.1.refs_1_ = bf16[1408,128]{1,0:T(8,128)(2,1)S(1)} custom-call(s32[8,8]{1,0:T(8,128)S(1)} %copy-done.2, bf16[2,6,640,128]{3,2,1,0:T(8,128)(2,1)S(1)} %bitcast.21, bf16[1408,128]{1,0:T(8,128)(2,1)S(1)} %collective-permute-done.7.refs_0_.refs_7_, bf16[1408,128]{1,0:T(8,128)(2,1)S(1)} %lane1_4.1.refs_1_, ...), custom_call_target="tpu_custom_call" | custom-call | flops 1000000000 | bytes 1024 | tf_op jit(solution)/shard_map/lane0_5/pallas_call | solution.py:93
  40.2 4.9 %collective-permute-start.11 = (bf16[1408,128]{1,0:T(8,128)(2,1)S(1)}, bf16[1408,128]{1,0:T(8,128)(2,1)S(1)}, u32[]{:S(2)}, u32[]{:S(2)}) collective-permute-start(bf16[1408,128]{1,0:T(8,128)(2,1)S(1)} %lane0_5.1.refs_1_), channel_id=1, source_target_pairs={{0,1},{3,2},{2,3},{1,0},{4,5},{7,6},{6,7},{5,4},{8,9},{11,10},{10,... | collective-permute-start | bytes 1081352 | tf_op jit(solution)/shard_map/ppermute | solution.py:351
  45.1 1.3 %collective-permute-done.6.refs_0_.refs_2_.refs_5_ = bf16[1408,128]{1,0:T(8,128)(2,1)S(1)} collective-permute-done((bf16[1408,128]{1,0:T(8,128)(2,1)S(1)}, bf16[1408,128]{1,0:T(8,128)(2,1)S(1)}, u32[]{:S(2)}, u32[]{:S(2)}) %collective-permute-start.6) | collective-permute-done | bytes 360480 | tf_op jit(solution)/shard_map/ppermute | solution.py:351
  47.9 1.1 %make_plan.1.refs_3_.plan = s32[16,128]{1,0:T(8,128)S(1)} custom-call(s32[8,8]{1,0:T(8,128)S(1)} %copy-done.2, s32[48]{0:T(128)S(1)} %copy-done.3, s32[6,8]{1,0:T(8,128)S(1)} %bitcast.32, s32[6,8]{1,0:T(8,128)S(1)} %bitcast.34, s32[6,6]{1,0:T(8,128)S(1)} %bitcast.33, bf16[2,16,128]{2,1,0:T(8,128)(2,1)S(1)} %pad.4.refs_0_.notes, ...), custom_call_target="tpu_custom_call" | custom-call | flops 1000000000 | bytes 1024 | tf_op jit(solution)/shard_map/make_plan/pallas_call | solution.py:175
  49.7 1.3 %collective-permute-start.15 = (bf16[1408,128]{1,0:T(8,128)(2,1)S(1)}, bf16[1408,128]{1,0:T(8,128)(2,1)S(1)}, u32[]{:S(2)}, u32[]{:S(2)}) collective-permute-start(bf16[1408,128]{1,0:T(8,128)(2,1)S(1)} %lane0_6.1.refs_1_), channel_id=1, source_target_pairs={{2,3},{1,0},{6,7},{5,4},{10,11},{9,8},{14,15},{13,12},{18,19},{17,... | collective-permute-start | bytes 1081352 | tf_op jit(solution)/shard_map/ppermute | solution.py:351
  53.4 1.3 %collective-permute-start.13 = (bf16[1408,128]{1,0:T(8,128)(2,1)S(1)}, bf16[1408,128]{1,0:T(8,128)(2,1)S(1)}, u32[]{:S(2)}, u32[]{:S(2)}) collective-permute-start(bf16[1408,128]{1,0:T(8,128)(2,1)S(1)} %lane0_7.1.refs_1_), channel_id=1, source_target_pairs={{2,3},{1,0},{6,7},{5,4},{10,11},{9,8},{14,15},{13,12},{18,19},{17,... | collective-permute-start | bytes 1081352 | tf_op jit(solution)/shard_map/ppermute | solution.py:351
  54.7 9.8 %collective-permute-done.15.refs_2_.refs_11_ = bf16[1408,128]{1,0:T(8,128)(2,1)S(1)} collective-permute-done((bf16[1408,128]{1,0:T(8,128)(2,1)S(1)}, bf16[1408,128]{1,0:T(8,128)(2,1)S(1)}, u32[]{:S(2)}, u32[]{:S(2)}) %collective-permute-start.15) | collective-permute-done | bytes 360480 | tf_op jit(solution)/shard_map/ppermute | solution.py:351
  65.2 1.3 %collective-permute-start.16 = (bf16[1152,128]{1,0:T(8,128)(2,1)S(1)}, bf16[1152,128]{1,0:T(8,128)(2,1)S(1)}, u32[]{:S(2)}, u32[]{:S(2)}) collective-permute-start(bf16[1152,128]{1,0:T(8,128)(2,1)S(1)} %lane0_8.1), channel_id=1, source_target_pairs={{2,3},{1,0},{6,7},{5,4},{10,11},{9,8},{14,15},{13,12},{18,19},{17,... | collective-permute-start | bytes 884744 | tf_op jit(solution)/shard_map/ppermute | solution.py:351
  66.5 5.1 %multiply_rows.2.refs_6_ = bf16[6,6,128,128]{3,2,1,0:T(8,128)(2,1)} custom-call(s32[8,8]{1,0:T(8,128)S(1)} %copy-done.2, s32[16,128]{1,0:T(8,128)S(1)} %make_plan.1.refs_3_.plan, bf16[6,8,128,128]{3,2,1,0:T(8,128)(2,1)S(1)} %bitcast.30, bf16[6,8,128,128]{3,2,1,0:T(8,128)(2,1)S(1)} %collective-permute-done.9.refs_2_.b1, ...), custom_call_target="tpu_custom_call" | custom-call | flops 2013265920 | bytes 4194304 | tf_op jit(solution)/shard_map/multiply_rows/pallas_call | solution.py:277
  72.4 3.2 %collective-permute-done.16.refs_5_ = bf16[1152,128]{1,0:T(8,128)(2,1)S(1)} collective-permute-done((bf16[1152,128]{1,0:T(8,128)(2,1)S(1)}, bf16[1152,128]{1,0:T(8,128)(2,1)S(1)}, u32[]{:S(2)}, u32[]{:S(2)}) %collective-permute-start.16) | collective-permute-done | bytes 294944 | tf_op jit(solution)/shard_map/ppermute | solution.py:351
  75.6 3.3 %multiply_rows.3 = bf16[6,6,128,128]{3,2,1,0:T(8,128)(2,1)} custom-call(s32[8,8]{1,0:T(8,128)S(1)} %copy-done.2, s32[16,128]{1,0:T(8,128)S(1)} %make_plan.1.refs_3_.plan, bf16[6,8,128,128]{3,2,1,0:T(8,128)(2,1)S(1)} %bitcast.31, bf16[6,8,128,128]{3,2,1,0:T(8,128)(2,1)S(1)} %collective-permute-done.9.refs_2_.b1, ...), custom_call_target="tpu_custom_call", output_to_operand_aliasing={{}: (11, {})} | custom-call | flops 1006632960 | bytes 4194304 | tf_op jit(solution)/shard_map/multiply_rows/pallas_call | solution.py:277
  (48 shorter events, 11.7 us)
Async XLA Ops:
  0.0 6.6 %copy-start.5 = (s32[1,1,2,6,5]{3,2,4,1,0:T(2,128)S(1)}, s32[1,1,2,6,5]{3,2,4,1,0:T(2,128)}, u32[]{:S(2)}) copy-start(s32[1,1,2,6,5]{3,2,4,1,0:T(2,128)} %param.8) | copy-start | bytes 724
  0.0 6.7 %copy-start = (bf16[1,1,2,6,5,128,128]{6,5,4,3,2,1,0:T(8,128)(2,1)S(1)}, bf16[1,1,2,6,5,128,128]{6,5,4,3,2,1,0:T(8,128)(2,1)}, u32[]{:S(2)}) copy-start(bf16[1,1,2,6,5,128,128]{6,5,4,3,2,1,0:T(8,128)(2,1)} %param.7) | copy-start | bytes 5898244
  0.0 6.7 %copy-start.2 = (s32[8,8]{1,0:T(8,128)S(1)}, s32[8,8]{1,0:T(8,128)}, u32[]{:S(2)}) copy-start(s32[8,8]{1,0:T(8,128)} %owner.35) | copy-start | bytes 772
  2.6 11.0 %collective-permute-start.2 = (bf16[960,128]{1,0:T(8,128)(2,1)}, bf16[960,128]{1,0:T(8,128)(2,1)S(1)}, u32[]{:S(2)}, u32[]{:S(2)}) collective-permute-start(bf16[960,128]{1,0:T(8,128)(2,1)} %lane0_0.1), channel_id=1, source_target_pairs={{0,1},{3,2},{4,5},{7,6},{8,9},{11,10},{12,13},{15,14},{16,17},{19,... | collective-permute-start | bytes 737288 | tf_op jit(solution)/shard_map/ppermute | solution.py:351
  6.7 1.2 %copy-start.4 = (s32[1,1,6,8]{3,1,2,0:T(1,128)S(1)}, s32[1,1,6,8]{3,1,2,0:T(1,128)}, u32[]{:S(2)}) copy-start(s32[1,1,6,8]{3,1,2,0:T(1,128)} %param.10) | copy-start | bytes 580
  6.7 4.2 %copy-start.1 = (bf16[1,1,6,8,128,128]{5,4,3,2,1,0:T(8,128)(2,1)S(1)}, bf16[1,1,6,8,128,128]{5,4,3,2,1,0:T(8,128)(2,1)}, u32[]{:S(2)}) copy-start(bf16[1,1,6,8,128,128]{5,4,3,2,1,0:T(8,128)(2,1)} %param.9) | copy-start | bytes 4718596
  8.0 3.0 %collective-permute-start = (s32[1,1,6,8]{3,2,1,0:T(8,128)S(1)}, s32[1,1,6,8]{3,2,1,0:T(8,128)S(1)}, u32[]{:S(2)}, u32[]{:S(2)}) collective-permute-start(s32[1,1,6,8]{3,2,1,0:T(8,128)S(1)} %copy.10), channel_id=1, source_target_pairs={{4,0},{8,4},{12,8},{16,12},{20,16},{24,20},{28,24},{0,28},{5,1},{9... | collective-permute-start | bytes 584 | tf_op jit(solution)/shard_map/ppermute | solution.py:345
  9.6 12.8 %collective-permute-start.1 = (bf16[1376,128]{1,0:T(8,128)(2,1)S(1)}, bf16[1376,128]{1,0:T(8,128)(2,1)S(1)}, u32[]{:S(2)}, u32[]{:S(2)}) collective-permute-start(bf16[1376,128]{1,0:T(8,128)(2,1)S(1)} %lane0_1.1), channel_id=1, source_target_pairs={{0,1},{3,2},{4,5},{7,6},{8,9},{11,10},{12,13},{15,14},{16,17},{19,... | collective-permute-start | bytes 1056776 | tf_op jit(solution)/shard_map/ppermute | solution.py:351
  11.0 40.3 %collective-permute-start.9 = (bf16[6,8,128,128]{3,2,1,0:T(8,128)(2,1)S(1)}, bf16[6,8,128,128]{3,2,1,0:T(8,128)(2,1)S(1)}, u32[]{:S(2)}, u32[]{:S(2)}) collective-permute-start(bf16[6,8,128,128]{3,2,1,0:T(8,128)(2,1)S(1)} %bitcast.29), channel_id=1, source_target_pairs={{4,0},{8,4},{12,8},{16,12},{20,16},{24,20},{28,24},{0,28},{5,1},{9... | collective-permute-start | bytes 4718600 | tf_op jit(solution)/shard_map/ppermute | solution.py:347
  14.2 9.6 %collective-permute-start.5 = (bf16[960,128]{1,0:T(8,128)(2,1)S(1)}, bf16[960,128]{1,0:T(8,128)(2,1)S(1)}, u32[]{:S(2)}, u32[]{:S(2)}) collective-permute-start(bf16[960,128]{1,0:T(8,128)(2,1)S(1)} %lane1_1.1.refs_0_), channel_id=1, source_target_pairs={{1,2},{2,1},{5,6},{6,5},{9,10},{10,9},{13,14},{14,13},{17,18},{18,... | collective-permute-start | bytes 737288 | tf_op jit(solution)/shard_map/ppermute | solution.py:351
  16.1 13.8 %collective-permute-start.4 = (bf16[1408,128]{1,0:T(8,128)(2,1)S(1)}, bf16[1408,128]{1,0:T(8,128)(2,1)S(1)}, u32[]{:S(2)}, u32[]{:S(2)}) collective-permute-start(bf16[1408,128]{1,0:T(8,128)(2,1)S(1)} %lane0_2.1.refs_2_), channel_id=1, source_target_pairs={{0,1},{3,2},{4,5},{7,6},{8,9},{11,10},{12,13},{15,14},{16,17},{19,... | collective-permute-start | bytes 1081352 | tf_op jit(solution)/shard_map/ppermute | solution.py:351
  23.2 8.2 %collective-permute-start.3 = (bf16[1376,128]{1,0:T(8,128)(2,1)S(1)}, bf16[1376,128]{1,0:T(8,128)(2,1)S(1)}, u32[]{:S(2)}, u32[]{:S(2)}) collective-permute-start(bf16[1376,128]{1,0:T(8,128)(2,1)S(1)} %lane1_2.1.refs_1_), channel_id=1, source_target_pairs={{1,2},{2,1},{5,6},{6,5},{9,10},{10,9},{13,14},{14,13},{17,18},{18,... | collective-permute-start | bytes 1056776 | tf_op jit(solution)/shard_map/ppermute | solution.py:351
  25.0 12.6 %collective-permute-start.8 = (bf16[1408,128]{1,0:T(8,128)(2,1)S(1)}, bf16[1408,128]{1,0:T(8,128)(2,1)S(1)}, u32[]{:S(2)}, u32[]{:S(2)}) collective-permute-start(bf16[1408,128]{1,0:T(8,128)(2,1)S(1)} %lane0_3.1.refs_1_), channel_id=1, source_target_pairs={{0,1},{3,2},{2,3},{1,0},{4,5},{7,6},{6,7},{5,4},{8,9},{11,10},{10,... | collective-permute-start | bytes 1081352 | tf_op jit(solution)/shard_map/ppermute | solution.py:351
  30.6 8.4 %collective-permute-start.7 = (bf16[1408,128]{1,0:T(8,128)(2,1)S(1)}, bf16[1408,128]{1,0:T(8,128)(2,1)S(1)}, u32[]{:S(2)}, u32[]{:S(2)}) collective-permute-start(bf16[1408,128]{1,0:T(8,128)(2,1)S(1)} %lane1_3.1.refs_2_), channel_id=1, source_target_pairs={{1,2},{2,1},{5,6},{6,5},{9,10},{10,9},{13,14},{14,13},{17,18},{18,... | collective-permute-start | bytes 1081352 | tf_op jit(solution)/shard_map/ppermute | solution.py:351
  32.6 13.9 %collective-permute-start.6 = (bf16[1408,128]{1,0:T(8,128)(2,1)S(1)}, bf16[1408,128]{1,0:T(8,128)(2,1)S(1)}, u32[]{:S(2)}, u32[]{:S(2)}) collective-permute-start(bf16[1408,128]{1,0:T(8,128)(2,1)S(1)} %lane0_4.1.refs_1_), channel_id=1, source_target_pairs={{0,1},{3,2},{2,3},{1,0},{4,5},{7,6},{6,7},{5,4},{8,9},{11,10},{10,... | collective-permute-start | bytes 1081352 | tf_op jit(solution)/shard_map/ppermute | solution.py:351
  38.4 6.8 %copy-start.6 = (s32[1,1,6,6]{3,1,2,0:T(1,128)S(1)}, s32[1,1,6,6]{3,1,2,0:T(1,128)}, u32[]{:S(2)}) copy-start(s32[1,1,6,6]{3,1,2,0:T(1,128)} %param.11) | copy-start | bytes 436
  38.4 10.6 %collective-permute-start.12 = (bf16[1408,128]{1,0:T(8,128)(2,1)S(1)}, bf16[1408,128]{1,0:T(8,128)(2,1)S(1)}, u32[]{:S(2)}, u32[]{:S(2)}) collective-permute-start(bf16[1408,128]{1,0:T(8,128)(2,1)S(1)} %lane1_4.1.refs_1_), channel_id=1, source_target_pairs={{1,2},{2,1},{5,6},{6,5},{9,10},{10,9},{13,14},{14,13},{17,18},{18,... | collective-permute-start | bytes 1081352 | tf_op jit(solution)/shard_map/ppermute | solution.py:351
  40.2 11.1 %collective-permute-start.11 = (bf16[1408,128]{1,0:T(8,128)(2,1)S(1)}, bf16[1408,128]{1,0:T(8,128)(2,1)S(1)}, u32[]{:S(2)}, u32[]{:S(2)}) collective-permute-start(bf16[1408,128]{1,0:T(8,128)(2,1)S(1)} %lane0_5.1.refs_1_), channel_id=1, source_target_pairs={{0,1},{3,2},{2,3},{1,0},{4,5},{7,6},{6,7},{5,4},{8,9},{11,10},{10,... | collective-permute-start | bytes 1081352 | tf_op jit(solution)/shard_map/ppermute | solution.py:351
  45.1 2.7 %copy-start.3 = (s32[48]{0:T(128)S(1)}, s32[48]{0:T(128)}, u32[]{:S(2)}) copy-start(s32[48]{0:T(128)} %atoms.1) | copy-start | bytes 580
  47.2 5.5 %collective-permute-start.10 = (bf16[1408,128]{1,0:T(8,128)(2,1)S(1)}, bf16[1408,128]{1,0:T(8,128)(2,1)S(1)}, u32[]{:S(2)}, u32[]{:S(2)}) collective-permute-start(bf16[1408,128]{1,0:T(8,128)(2,1)S(1)} %lane1_5.1.refs_3_.refs_1_), channel_id=1, source_target_pairs={{1,2},{2,1},{5,6},{6,5},{9,10},{10,9},{13,14},{14,13},{17,18},{18,... | collective-permute-start | bytes 1081352 | tf_op jit(solution)/shard_map/ppermute | solution.py:351
  49.7 14.8 %collective-permute-start.15 = (bf16[1408,128]{1,0:T(8,128)(2,1)S(1)}, bf16[1408,128]{1,0:T(8,128)(2,1)S(1)}, u32[]{:S(2)}, u32[]{:S(2)}) collective-permute-start(bf16[1408,128]{1,0:T(8,128)(2,1)S(1)} %lane0_6.1.refs_1_), channel_id=1, source_target_pairs={{2,3},{1,0},{6,7},{5,4},{10,11},{9,8},{14,15},{13,12},{18,19},{17,... | collective-permute-start | bytes 1081352 | tf_op jit(solution)/shard_map/ppermute | solution.py:351
  52.0 12.6 %collective-permute-start.14 = (bf16[1152,128]{1,0:T(8,128)(2,1)S(1)}, bf16[1152,128]{1,0:T(8,128)(2,1)S(1)}, u32[]{:S(2)}, u32[]{:S(2)}) collective-permute-start(bf16[1152,128]{1,0:T(8,128)(2,1)S(1)} %lane1_6.1.refs_1_), channel_id=1, source_target_pairs={{1,2},{2,1},{5,6},{6,5},{9,10},{10,9},{13,14},{14,13},{17,18},{18,... | collective-permute-start | bytes 884744 | tf_op jit(solution)/shard_map/ppermute | solution.py:351
  53.4 19.0 %collective-permute-start.13 = (bf16[1408,128]{1,0:T(8,128)(2,1)S(1)}, bf16[1408,128]{1,0:T(8,128)(2,1)S(1)}, u32[]{:S(2)}, u32[]{:S(2)}) collective-permute-start(bf16[1408,128]{1,0:T(8,128)(2,1)S(1)} %lane0_7.1.refs_1_), channel_id=1, source_target_pairs={{2,3},{1,0},{6,7},{5,4},{10,11},{9,8},{14,15},{13,12},{18,19},{17,... | collective-permute-start | bytes 1081352 | tf_op jit(solution)/shard_map/ppermute | solution.py:351
  65.2 10.4 %collective-permute-start.16 = (bf16[1152,128]{1,0:T(8,128)(2,1)S(1)}, bf16[1152,128]{1,0:T(8,128)(2,1)S(1)}, u32[]{:S(2)}, u32[]{:S(2)}) collective-permute-start(bf16[1152,128]{1,0:T(8,128)(2,1)S(1)} %lane0_8.1), channel_id=1, source_target_pairs={{2,3},{1,0},{6,7},{5,4},{10,11},{9,8},{14,15},{13,12},{18,19},{17,... | collective-permute-start | bytes 884744 | tf_op jit(solution)/shard_map/ppermute | solution.py:351
where the time goes:
time: 79.2 us; the launch traced here: 78.9 us
  starting transfers between devices  36.7 us (46%)
  Pallas kernels  24.3 us (31%)
  waiting for transfers between devices  17.4 us (22%)
    ppermute x15, starting transfers between devices, local(): got = lax.ppermute(newest, 'col', route)  32.4 us
    ppermute x15, waiting for transfers between devices, local(): got = lax.ppermute(newest, 'col', route)  17.4 us
    pallas_call x15, Pallas kernels, relay(): pl.pallas_call(functools.partial(relay_kernel, roles, len(after)), out_sh...  14.7 us
    pallas_call x2, Pallas kernels, multiply_rows(): pl.pallas_call(functools.partial(rows_kernel, first, count, hops, tuple(s...  8.47 us
    ppermute x1, starting transfers between devices, local(): moved_b = lax.ppermute(behind_b, 'row', from_next)  2.6 us
    ppermute x1, starting transfers between devices, local(): moved_bc = lax.ppermute(behind_bc, 'row', from_next)  1.66 us
  transfers between devices with their start and end apart: 17, of which 7 were waited for; matrix products, arithmetic and copies ran while one was open for 0% of the time, Pallas kernels for 23%

commit v1 on v0

--- a/solution.py
+++ b/solution.py
@@ -8,7 +8,7 @@
 from jax.sharding import PartitionSpec as P
 
 STEPS = 2
-SHARES = (15, 21, 22, 22, 22, 18)
+SHARES = (1, 1, 1, 1, 1, 1)
 PIECES = len(SHARES)
 NOTED = 1
 NOTE = 16
@@ -346,7 +346,7 @@
                 moved_bc, behind_b = lax.optimization_barrier((moved_bc, stored_b))
                 moved_b = lax.ppermute(behind_b, "row", from_next)
             route = []
-            for _, hop in roles:
+            for hop in sorted({lane, hops - 1 - lane}):
                 route += [(hop, hop + 1), (hops - hop, hops - hop - 1)]
             got = lax.ppermute(newest, "col", route)
             for piece, hop in roles:
@@ -355,7 +355,7 @@
                 edges[slot] = got
 
     result = None
-    for first, count in ((0, rows - 2), (rows - 2, 2)):
+    for first, count in ((0, rows - 2), (rows - 2, 1), (rows - 1, 1)):
         result = multiply_rows(
             first,
             count,

time: 79.2 us -> 72.3 us (0.913)
  waiting for transfers between devices: 17.4 us -> 2.24 us
  starting transfers between devices: 36.7 us -> 45.1 us
    ppermute x15, waiting for transfers between devices: 17.4 us -> 1.91 us  [local(): got = lax.ppermute(newest, 'col', route)]
    ppermute x15, starting transfers between devices: 32.4 us -> 40.9 us  [local(): got = lax.ppermute(newest, 'col', route)]
    pallas_call x2 -> x3, Pallas kernels: 8.47 us -> 8.6 us  [multiply_rows(): pl.pallas_call(functools.partial(rows_kernel, first, count, hops, tuple(s...]
  transfers between devices with their start and end apart: 17 -> 17, of which waited for: 7 -> 3; matrix products, arithmetic and copies ran while one was open for 0% -> 0% of each run, Pallas kernels for 23% -> 27%
where the time goes in v1:
time: 72.3 us; the launch traced here: 72 us
  starting transfers between devices  45.1 us (62%)
  Pallas kernels  24.1 us (33%)
  waiting for transfers between devices  2.24 us (3%)
    ppermute x15, starting transfers between devices, local(): got = lax.ppermute(newest, 'col', route)  40.9 us
    pallas_call x15, Pallas kernels, relay(): pl.pallas_call(functools.partial(relay_kernel, roles, len(after)), out_sh...  14.4 us
    pallas_call x3, Pallas kernels, multiply_rows(): pl.pallas_call(functools.partial(rows_kernel, first, count, hops, tuple(s...  8.6 us
    ppermute x1, starting transfers between devices, local(): moved_b = lax.ppermute(behind_b, 'row', from_next)  2.6 us
    ppermute x15, waiting for transfers between devices, local(): got = lax.ppermute(newest, 'col', route)  1.91 us
    ppermute x1, starting transfers between devices, local(): moved_bc = lax.ppermute(behind_bc, 'row', from_next)  1.66 us
  transfers between devices with their start and end apart: 17, of which 3 were waited for; matrix products, arithmetic and copies ran while one was open for 0% of the time, Pallas kernels for 27%

profile of v1, /device:TPU:0, one launch (start us, length us, event | category | flops | bytes accessed | tf_op | source)
XLA Modules:
  0.0 72.0 jit_solution(10585899353440164042)
XLA Ops:
  0.0 2.6 %lane0_0.1 = bf16[1280,128]{1,0:T(8,128)(2,1)} custom-call(s32[8,8]{1,0:T(8,128)} %owner.37, bf16[2,6,640,128]{3,2,1,0:T(8,128)(2,1)} %bitcast.12), custom_call_target="tpu_custom_call" | custom-call | flops 1000000000 | bytes 1024 | tf_op jit(solution)/shard_map/lane0_0/pallas_call | solution.py:93
  2.6 2.1 %collective-permute-start.2 = (bf16[1280,128]{1,0:T(8,128)(2,1)}, bf16[1280,128]{1,0:T(8,128)(2,1)S(1)}, u32[]{:S(2)}, u32[]{:S(2)}) collective-permute-start(bf16[1280,128]{1,0:T(8,128)(2,1)} %lane0_0.1), channel_id=1, source_target_pairs={{0,1},{3,2},{2,3},{1,0},{4,5},{7,6},{6,7},{5,4},{8,9},{11,10},{10,... | collective-permute-start | bytes 983048 | tf_op jit(solution)/shard_map/ppermute | solution.py:351
  4.9 1.1 %lane0_1.1 = bf16[1312,128]{1,0:T(8,128)(2,1)S(1)} custom-call(s32[8,8]{1,0:T(8,128)S(1)} %copy-done.2, bf16[2,6,640,128]{3,2,1,0:T(8,128)(2,1)S(1)} %bitcast.13, bf16[2,16,128]{2,1,0:T(8,128)(2,1)S(1)} %pad.4.refs_0_.notes), custom_call_target="tpu_custom_call" | custom-call | flops 1000000000 | bytes 1024 | tf_op jit(solution)/shard_map/lane0_1/pallas_call | solution.py:93
  6.1 1.7 %collective-permute-start = (s32[1,1,6,8]{3,2,1,0:T(8,128)S(1)}, s32[1,1,6,8]{3,2,1,0:T(8,128)S(1)}, u32[]{:S(2)}, u32[]{:S(2)}) collective-permute-start(s32[1,1,6,8]{3,2,1,0:T(8,128)S(1)} %copy.11), channel_id=1, source_target_pairs={{4,0},{8,4},{12,8},{16,12},{20,16},{24,20},{28,24},{0,28},{5,1},{9... | collective-permute-start | bytes 584 | tf_op jit(solution)/shard_map/ppermute | solution.py:345
  7.7 1.0 %collective-permute-start.1 = (bf16[1312,128]{1,0:T(8,128)(2,1)S(1)}, bf16[1312,128]{1,0:T(8,128)(2,1)S(1)}, u32[]{:S(2)}, u32[]{:S(2)}) collective-permute-start(bf16[1312,128]{1,0:T(8,128)(2,1)S(1)} %lane0_1.1), channel_id=1, source_target_pairs={{0,1},{3,2},{2,3},{1,0},{4,5},{7,6},{6,7},{5,4},{8,9},{11,10},{10,... | collective-permute-start | bytes 1007624 | tf_op jit(solution)/shard_map/ppermute | solution.py:351
  9.1 2.6 %collective-permute-start.9 = (bf16[6,8,128,128]{3,2,1,0:T(8,128)(2,1)S(1)}, bf16[6,8,128,128]{3,2,1,0:T(8,128)(2,1)S(1)}, u32[]{:S(2)}, u32[]{:S(2)}) collective-permute-start(bf16[6,8,128,128]{3,2,1,0:T(8,128)(2,1)S(1)} %bitcast.30), channel_id=1, source_target_pairs={{4,0},{8,4},{12,8},{16,12},{20,16},{24,20},{28,24},{0,28},{5,1},{9... | collective-permute-start | bytes 4718600 | tf_op jit(solution)/shard_map/ppermute | solution.py:347
  11.7 1.8 %collective-permute-done.2.refs_0_ = bf16[1280,128]{1,0:T(8,128)(2,1)S(1)} collective-permute-done((bf16[1280,128]{1,0:T(8,128)(2,1)}, bf16[1280,128]{1,0:T(8,128)(2,1)S(1)}, u32[]{:S(2)}, u32[]{:S(2)}) %collective-permute-start.2) | collective-permute-done | bytes 327712 | tf_op jit(solution)/shard_map/ppermute | solution.py:351
  14.8 1.1 %lane0_2.1.refs_2_ = bf16[1280,128]{1,0:T(8,128)(2,1)S(1)} custom-call(s32[8,8]{1,0:T(8,128)S(1)} %copy-done.2, bf16[2,6,640,128]{3,2,1,0:T(8,128)(2,1)S(1)} %bitcast.15, bf16[1280,128]{1,0:T(8,128)(2,1)S(1)} %lane1_1.1.refs_0_), custom_call_target="tpu_custom_call" | custom-call | flops 3000000000 | bytes 1024 | tf_op jit(solution)/shard_map/lane0_2/pallas_call | solution.py:93
  15.9 5.1 %collective-permute-start.4 = (bf16[1280,128]{1,0:T(8,128)(2,1)S(1)}, bf16[1280,128]{1,0:T(8,128)(2,1)S(1)}, u32[]{:S(2)}, u32[]{:S(2)}) collective-permute-start(bf16[1280,128]{1,0:T(8,128)(2,1)S(1)} %lane0_2.1.refs_2_), channel_id=1, source_target_pairs={{0,1},{3,2},{2,3},{1,0},{4,5},{7,6},{6,7},{5,4},{8,9},{11,10},{10,... | collective-permute-start | bytes 983048 | tf_op jit(solution)/shard_map/ppermute | solution.py:351
  21.0 0.7 %lane1_2.1.refs_1_ = bf16[1312,128]{1,0:T(8,128)(2,1)S(1)} custom-call(s32[8,8]{1,0:T(8,128)S(1)} %copy-done.2, bf16[2,6,640,128]{3,2,1,0:T(8,128)(2,1)S(1)} %bitcast.16, bf16[2,16,128]{2,1,0:T(8,128)(2,1)S(1)} %pad.4.refs_0_.notes, bf16[1312,128]{1,0:T(8,128)(2,1)S(1)} %collective-permute-done.1.refs_1_.refs_2_.refs_0_.refs_3_, ...), custom_call_target="tpu_custom_call" | custom-call | flops 2000000000 | bytes 1024 | tf_op jit(solution)/shard_map/lane1_2/pallas_call | solution.py:93
  21.7 0.7 collective-permute-start.3
  22.4 1.1 %lane0_3.1.refs_1_ = bf16[1280,128]{1,0:T(8,128)(2,1)S(1)} custom-call(s32[8,8]{1,0:T(8,128)S(1)} %copy-done.2, bf16[2,6,640,128]{3,2,1,0:T(8,128)(2,1)S(1)} %bitcast.17, bf16[1280,128]{1,0:T(8,128)(2,1)S(1)} %collective-permute-done.5.refs_0_.refs_1_, bf16[1312,128]{1,0:T(8,128)(2,1)S(1)} %lane1_2.1.refs_1_, ...), custom_call_target="tpu_custom_call" | custom-call | flops 1000000000 | bytes 1024 | tf_op jit(solution)/shard_map/lane0_3/pallas_call | solution.py:93
  23.5 4.9 %collective-permute-start.8 = (bf16[1280,128]{1,0:T(8,128)(2,1)S(1)}, bf16[1280,128]{1,0:T(8,128)(2,1)S(1)}, u32[]{:S(2)}, u32[]{:S(2)}) collective-permute-start(bf16[1280,128]{1,0:T(8,128)(2,1)S(1)} %lane0_3.1.refs_1_), channel_id=1, source_target_pairs={{0,1},{3,2},{2,3},{1,0},{4,5},{7,6},{6,7},{5,4},{8,9},{11,10},{10,... | collective-permute-start | bytes 983048 | tf_op jit(solution)/shard_map/ppermute | solution.py:351
  29.9 1.2 %lane0_4.1.refs_1_ = bf16[1312,128]{1,0:T(8,128)(2,1)S(1)} custom-call(s32[8,8]{1,0:T(8,128)S(1)} %copy-done.2, bf16[2,6,640,128]{3,2,1,0:T(8,128)(2,1)S(1)} %bitcast.19, bf16[2,16,128]{2,1,0:T(8,128)(2,1)S(1)} %pad.4.refs_0_.notes, bf16[1312,128]{1,0:T(8,128)(2,1)S(1)} %collective-permute-done.3.refs_1_.refs_4_, bf16[1280,128]{1,0:T(8,128)(2,1)S(1)} %lane1_3.1.refs_2_, ...), custom_call_target="tpu_custom_call" | custom-call | flops 1000000000 | bytes 1024 | tf_op jit(solution)/shard_map/lane0_4/pallas_call | solution.py:93
  31.0 4.5 %collective-permute-start.6 = (bf16[1312,128]{1,0:T(8,128)(2,1)S(1)}, bf16[1312,128]{1,0:T(8,128)(2,1)S(1)}, u32[]{:S(2)}, u32[]{:S(2)}) collective-permute-start(bf16[1312,128]{1,0:T(8,128)(2,1)S(1)} %lane0_4.1.refs_1_), channel_id=1, source_target_pairs={{0,1},{3,2},{2,3},{1,0},{4,5},{7,6},{6,7},{5,4},{8,9},{11,10},{10,... | collective-permute-start | bytes 1007624 | tf_op jit(solution)/shard_map/ppermute | solution.py:351
  36.9 1.1 %lane0_5.1.refs_1_ = bf16[1280,128]{1,0:T(8,128)(2,1)S(1)} custom-call(s32[8,8]{1,0:T(8,128)S(1)} %copy-done.2, bf16[2,6,640,128]{3,2,1,0:T(8,128)(2,1)S(1)} %bitcast.21, bf16[1280,128]{1,0:T(8,128)(2,1)S(1)} %collective-permute-done.7.refs_0_.refs_7_, bf16[1280,128]{1,0:T(8,128)(2,1)S(1)} %lane1_4.1.refs_1_, ...), custom_call_target="tpu_custom_call" | custom-call | flops 1000000000 | bytes 1024 | tf_op jit(solution)/shard_map/lane0_5/pallas_call | solution.py:93
  38.0 5.3 %collective-permute-start.10 = (bf16[1280,128]{1,0:T(8,128)(2,1)S(1)}, bf16[1280,128]{1,0:T(8,128)(2,1)S(1)}, u32[]{:S(2)}, u32[]{:S(2)}) collective-permute-start(bf16[1280,128]{1,0:T(8,128)(2,1)S(1)} %lane0_5.1.refs_1_), channel_id=1, source_target_pairs={{0,1},{3,2},{2,3},{1,0},{4,5},{7,6},{6,7},{5,4},{8,9},{11,10},{10,... | collective-permute-start | bytes 983048 | tf_op jit(solution)/shard_map/ppermute | solution.py:351
  44.8 1.1 %make_plan.1.refs_3_.plan = s32[16,128]{1,0:T(8,128)S(1)} custom-call(s32[8,8]{1,0:T(8,128)S(1)} %copy-done.2, s32[48]{0:T(128)S(1)} %copy-done.3, s32[6,8]{1,0:T(8,128)S(1)} %bitcast.34, s32[6,8]{1,0:T(8,128)S(1)} %bitcast.36, s32[6,6]{1,0:T(8,128)S(1)} %bitcast.35, bf16[2,16,128]{2,1,0:T(8,128)(2,1)S(1)} %pad.4.refs_0_.notes, ...), custom_call_target="tpu_custom_call" | custom-call | flops 1000000000 | bytes 1024 | tf_op jit(solution)/shard_map/make_plan/pallas_call | solution.py:175
  46.6 4.1 %collective-permute-start.14 = (bf16[1280,128]{1,0:T(8,128)(2,1)S(1)}, bf16[1280,128]{1,0:T(8,128)(2,1)S(1)}, u32[]{:S(2)}, u32[]{:S(2)}) collective-permute-start(bf16[1280,128]{1,0:T(8,128)(2,1)S(1)} %lane0_6.1.refs_1_), channel_id=1, source_target_pairs={{0,1},{3,2},{2,3},{1,0},{4,5},{7,6},{6,7},{5,4},{8,9},{11,10},{10,... | collective-permute-start | bytes 983048 | tf_op jit(solution)/shard_map/ppermute | solution.py:351
  52.7 4.9 %collective-permute-start.16 = (bf16[1280,128]{1,0:T(8,128)(2,1)S(1)}, bf16[1280,128]{1,0:T(8,128)(2,1)S(1)}, u32[]{:S(2)}, u32[]{:S(2)}) collective-permute-start(bf16[1280,128]{1,0:T(8,128)(2,1)S(1)} %lane0_7.1.refs_1_), channel_id=1, source_target_pairs={{0,1},{3,2},{2,3},{1,0},{4,5},{7,6},{6,7},{5,4},{8,9},{11,10},{10,... | collective-permute-start | bytes 983048 | tf_op jit(solution)/shard_map/ppermute | solution.py:351
  58.4 4.9 %collective-permute-start.15 = (bf16[1280,128]{1,0:T(8,128)(2,1)S(1)}, bf16[1280,128]{1,0:T(8,128)(2,1)S(1)}, u32[]{:S(2)}, u32[]{:S(2)}) collective-permute-start(bf16[1280,128]{1,0:T(8,128)(2,1)S(1)} %lane0_8.1), channel_id=1, source_target_pairs={{0,1},{3,2},{2,3},{1,0},{4,5},{7,6},{6,7},{5,4},{8,9},{11,10},{10,... | collective-permute-start | bytes 983048 | tf_op jit(solution)/shard_map/ppermute | solution.py:351
  63.3 4.3 %multiply_rows.3.refs_3_ = bf16[6,6,128,128]{3,2,1,0:T(8,128)(2,1)} custom-call(s32[8,8]{1,0:T(8,128)S(1)} %copy-done.2, s32[16,128]{1,0:T(8,128)S(1)} %make_plan.1.refs_3_.plan, bf16[6,8,128,128]{3,2,1,0:T(8,128)(2,1)S(1)} %bitcast.31, bf16[6,8,128,128]{3,2,1,0:T(8,128)(2,1)S(1)} %collective-permute-done.9.refs_2_.b1, ...), custom_call_target="tpu_custom_call" | custom-call | flops 2013265920 | bytes 4194304 | tf_op jit(solution)/shard_map/multiply_rows/pallas_call | solution.py:277
  67.6 2.2 %multiply_rows.4.refs_3_ = bf16[6,6,128,128]{3,2,1,0:T(8,128)(2,1)} custom-call(s32[8,8]{1,0:T(8,128)S(1)} %copy-done.2, s32[16,128]{1,0:T(8,128)S(1)} %make_plan.1.refs_3_.plan, bf16[6,8,128,128]{3,2,1,0:T(8,128)(2,1)S(1)} %bitcast.32, bf16[6,8,128,128]{3,2,1,0:T(8,128)(2,1)S(1)} %collective-permute-done.9.refs_2_.b1, ...), custom_call_target="tpu_custom_call", output_to_operand_aliasing={{}: (8, {})} | custom-call | flops 503316480 | bytes 4194304 | tf_op jit(solution)/shard_map/multiply_rows/pallas_call | solution.py:277
  69.8 2.1 %multiply_rows.5 = bf16[6,6,128,128]{3,2,1,0:T(8,128)(2,1)} custom-call(s32[8,8]{1,0:T(8,128)S(1)} %copy-done.2, s32[16,128]{1,0:T(8,128)S(1)} %make_plan.1.refs_3_.plan, bf16[6,8,128,128]{3,2,1,0:T(8,128)(2,1)S(1)} %bitcast.33, bf16[6,8,128,128]{3,2,1,0:T(8,128)(2,1)S(1)} %collective-permute-done.9.refs_2_.b1, ...), custom_call_target="tpu_custom_call", output_to_operand_aliasing={{}: (8, {})} | custom-call | flops 503316480 | bytes 4194304 | tf_op jit(solution)/shard_map/multiply_rows/pallas_call | solution.py:277
  (49 shorter events, 9.5 us)
Async XLA Ops:
  0.0 4.7 %copy-start.5 = (s32[1,1,2,6,5]{3,2,4,1,0:T(2,128)S(1)}, s32[1,1,2,6,5]{3,2,4,1,0:T(2,128)}, u32[]{:S(2)}) copy-start(s32[1,1,2,6,5]{3,2,4,1,0:T(2,128)} %param.8) | copy-start | bytes 724
  0.0 4.9 %copy-start = (bf16[1,1,2,6,5,128,128]{6,5,4,3,2,1,0:T(8,128)(2,1)S(1)}, bf16[1,1,2,6,5,128,128]{6,5,4,3,2,1,0:T(8,128)(2,1)}, u32[]{:S(2)}) copy-start(bf16[1,1,2,6,5,128,128]{6,5,4,3,2,1,0:T(8,128)(2,1)} %param.7) | copy-start | bytes 5898244
  0.0 4.9 %copy-start.2 = (s32[8,8]{1,0:T(8,128)S(1)}, s32[8,8]{1,0:T(8,128)}, u32[]{:S(2)}) copy-start(s32[8,8]{1,0:T(8,128)} %owner.37) | copy-start | bytes 772
  2.6 10.8 %collective-permute-start.2 = (bf16[1280,128]{1,0:T(8,128)(2,1)}, bf16[1280,128]{1,0:T(8,128)(2,1)S(1)}, u32[]{:S(2)}, u32[]{:S(2)}) collective-permute-start(bf16[1280,128]{1,0:T(8,128)(2,1)} %lane0_0.1), channel_id=1, source_target_pairs={{0,1},{3,2},{2,3},{1,0},{4,5},{7,6},{6,7},{5,4},{8,9},{11,10},{10,... | collective-permute-start | bytes 983048 | tf_op jit(solution)/shard_map/ppermute | solution.py:351
  4.9 1.2 %copy-start.4 = (s32[1,1,6,8]{3,1,2,0:T(1,128)S(1)}, s32[1,1,6,8]{3,1,2,0:T(1,128)}, u32[]{:S(2)}) copy-start(s32[1,1,6,8]{3,1,2,0:T(1,128)} %param.10) | copy-start | bytes 580
  4.9 4.2 %copy-start.1 = (bf16[1,1,6,8,128,128]{5,4,3,2,1,0:T(8,128)(2,1)S(1)}, bf16[1,1,6,8,128,128]{5,4,3,2,1,0:T(8,128)(2,1)}, u32[]{:S(2)}) copy-start(bf16[1,1,6,8,128,128]{5,4,3,2,1,0:T(8,128)(2,1)} %param.9) | copy-start | bytes 4718596
  6.1 3.0 %collective-permute-start = (s32[1,1,6,8]{3,2,1,0:T(8,128)S(1)}, s32[1,1,6,8]{3,2,1,0:T(8,128)S(1)}, u32[]{:S(2)}, u32[]{:S(2)}) collective-permute-start(s32[1,1,6,8]{3,2,1,0:T(8,128)S(1)} %copy.11), channel_id=1, source_target_pairs={{4,0},{8,4},{12,8},{16,12},{20,16},{24,20},{28,24},{0,28},{5,1},{9... | collective-permute-start | bytes 584 | tf_op jit(solution)/shard_map/ppermute | solution.py:345
  7.7 13.2 %collective-permute-start.1 = (bf16[1312,128]{1,0:T(8,128)(2,1)S(1)}, bf16[1312,128]{1,0:T(8,128)(2,1)S(1)}, u32[]{:S(2)}, u32[]{:S(2)}) collective-permute-start(bf16[1312,128]{1,0:T(8,128)(2,1)S(1)} %lane0_1.1), channel_id=1, source_target_pairs={{0,1},{3,2},{2,3},{1,0},{4,5},{7,6},{6,7},{5,4},{8,9},{11,10},{10,... | collective-permute-start | bytes 1007624 | tf_op jit(solution)/shard_map/ppermute | solution.py:351
  9.1 41.6 %collective-permute-start.9 = (bf16[6,8,128,128]{3,2,1,0:T(8,128)(2,1)S(1)}, bf16[6,8,128,128]{3,2,1,0:T(8,128)(2,1)S(1)}, u32[]{:S(2)}, u32[]{:S(2)}) collective-permute-start(bf16[6,8,128,128]{3,2,1,0:T(8,128)(2,1)S(1)} %bitcast.30), channel_id=1, source_target_pairs={{4,0},{8,4},{12,8},{16,12},{20,16},{24,20},{28,24},{0,28},{5,1},{9... | collective-permute-start | bytes 4718600 | tf_op jit(solution)/shard_map/ppermute | solution.py:347
  14.1 8.3 %collective-permute-start.5 = (bf16[1280,128]{1,0:T(8,128)(2,1)S(1)}, bf16[1280,128]{1,0:T(8,128)(2,1)S(1)}, u32[]{:S(2)}, u32[]{:S(2)}) collective-permute-start(bf16[1280,128]{1,0:T(8,128)(2,1)S(1)} %lane1_1.1.refs_0_), channel_id=1, source_target_pairs={{1,2},{2,1},{5,6},{6,5},{9,10},{10,9},{13,14},{14,13},{17,18},{18,... | collective-permute-start | bytes 983048 | tf_op jit(solution)/shard_map/ppermute | solution.py:351
  15.9 12.6 %collective-permute-start.4 = (bf16[1280,128]{1,0:T(8,128)(2,1)S(1)}, bf16[1280,128]{1,0:T(8,128)(2,1)S(1)}, u32[]{:S(2)}, u32[]{:S(2)}) collective-permute-start(bf16[1280,128]{1,0:T(8,128)(2,1)S(1)} %lane0_2.1.refs_2_), channel_id=1, source_target_pairs={{0,1},{3,2},{2,3},{1,0},{4,5},{7,6},{6,7},{5,4},{8,9},{11,10},{10,... | collective-permute-start | bytes 983048 | tf_op jit(solution)/shard_map/ppermute | solution.py:351
  21.7 8.1 %collective-permute-start.3 = (bf16[1312,128]{1,0:T(8,128)(2,1)S(1)}, bf16[1312,128]{1,0:T(8,128)(2,1)S(1)}, u32[]{:S(2)}, u32[]{:S(2)}) collective-permute-start(bf16[1312,128]{1,0:T(8,128)(2,1)S(1)} %lane1_2.1.refs_1_), channel_id=1, source_target_pairs={{1,2},{2,1},{5,6},{6,5},{9,10},{10,9},{13,14},{14,13},{17,18},{18,... | collective-permute-start | bytes 1007624 | tf_op jit(solution)/shard_map/ppermute | solution.py:351
  23.5 12.0 %collective-permute-start.8 = (bf16[1280,128]{1,0:T(8,128)(2,1)S(1)}, bf16[1280,128]{1,0:T(8,128)(2,1)S(1)}, u32[]{:S(2)}, u32[]{:S(2)}) collective-permute-start(bf16[1280,128]{1,0:T(8,128)(2,1)S(1)} %lane0_3.1.refs_1_), channel_id=1, source_target_pairs={{0,1},{3,2},{2,3},{1,0},{4,5},{7,6},{6,7},{5,4},{8,9},{11,10},{10,... | collective-permute-start | bytes 983048 | tf_op jit(solution)/shard_map/ppermute | solution.py:351
  29.2 7.7 %collective-permute-start.7 = (bf16[1280,128]{1,0:T(8,128)(2,1)S(1)}, bf16[1280,128]{1,0:T(8,128)(2,1)S(1)}, u32[]{:S(2)}, u32[]{:S(2)}) collective-permute-start(bf16[1280,128]{1,0:T(8,128)(2,1)S(1)} %lane1_3.1.refs_2_), channel_id=1, source_target_pairs={{1,2},{2,1},{5,6},{6,5},{9,10},{10,9},{13,14},{14,13},{17,18},{18,... | collective-permute-start | bytes 983048 | tf_op jit(solution)/shard_map/ppermute | solution.py:351
  31.0 12.4 %collective-permute-start.6 = (bf16[1312,128]{1,0:T(8,128)(2,1)S(1)}, bf16[1312,128]{1,0:T(8,128)(2,1)S(1)}, u32[]{:S(2)}, u32[]{:S(2)}) collective-permute-start(bf16[1312,128]{1,0:T(8,128)(2,1)S(1)} %lane0_4.1.refs_1_), channel_id=1, source_target_pairs={{0,1},{3,2},{2,3},{1,0},{4,5},{7,6},{6,7},{5,4},{8,9},{11,10},{10,... | collective-permute-start | bytes 1007624 | tf_op jit(solution)/shard_map/ppermute | solution.py:351
  36.2 7.2 %copy-start.6 = (s32[1,1,6,6]{3,1,2,0:T(1,128)S(1)}, s32[1,1,6,6]{3,1,2,0:T(1,128)}, u32[]{:S(2)}) copy-start(s32[1,1,6,6]{3,1,2,0:T(1,128)} %param.11) | copy-start | bytes 436
  36.2 9.7 %collective-permute-start.11 = (bf16[1280,128]{1,0:T(8,128)(2,1)S(1)}, bf16[1280,128]{1,0:T(8,128)(2,1)S(1)}, u32[]{:S(2)}, u32[]{:S(2)}) collective-permute-start(bf16[1280,128]{1,0:T(8,128)(2,1)S(1)} %lane1_4.1.refs_1_), channel_id=1, source_target_pairs={{1,2},{2,1},{5,6},{6,5},{9,10},{10,9},{13,14},{14,13},{17,18},{18,... | collective-permute-start | bytes 983048 | tf_op jit(solution)/shard_map/ppermute | solution.py:351
  38.0 12.6 %collective-permute-start.10 = (bf16[1280,128]{1,0:T(8,128)(2,1)S(1)}, bf16[1280,128]{1,0:T(8,128)(2,1)S(1)}, u32[]{:S(2)}, u32[]{:S(2)}) collective-permute-start(bf16[1280,128]{1,0:T(8,128)(2,1)S(1)} %lane0_5.1.refs_1_), channel_id=1, source_target_pairs={{0,1},{3,2},{2,3},{1,0},{4,5},{7,6},{6,7},{5,4},{8,9},{11,10},{10,... | collective-permute-start | bytes 983048 | tf_op jit(solution)/shard_map/ppermute | solution.py:351
  43.4 1.4 %copy-start.3 = (s32[48]{0:T(128)S(1)}, s32[48]{0:T(128)}, u32[]{:S(2)}) copy-start(s32[48]{0:T(128)} %atoms.1) | copy-start | bytes 580
  44.1 7.9 %collective-permute-start.13 = (bf16[1280,128]{1,0:T(8,128)(2,1)S(1)}, bf16[1280,128]{1,0:T(8,128)(2,1)S(1)}, u32[]{:S(2)}, u32[]{:S(2)}) collective-permute-start(bf16[1280,128]{1,0:T(8,128)(2,1)S(1)} %lane1_5.1.refs_3_.refs_1_), channel_id=1, source_target_pairs={{1,2},{2,1},{5,6},{6,5},{9,10},{10,9},{13,14},{14,13},{17,18},{18,... | collective-permute-start | bytes 983048 | tf_op jit(solution)/shard_map/ppermute | solution.py:351
  46.6 11.1 %collective-permute-start.14 = (bf16[1280,128]{1,0:T(8,128)(2,1)S(1)}, bf16[1280,128]{1,0:T(8,128)(2,1)S(1)}, u32[]{:S(2)}, u32[]{:S(2)}) collective-permute-start(bf16[1280,128]{1,0:T(8,128)(2,1)S(1)} %lane0_6.1.refs_1_), channel_id=1, source_target_pairs={{0,1},{3,2},{2,3},{1,0},{4,5},{7,6},{6,7},{5,4},{8,9},{11,10},{10,... | collective-permute-start | bytes 983048 | tf_op jit(solution)/shard_map/ppermute | solution.py:351
  51.3 6.3 %collective-permute-start.12 = (bf16[1280,128]{1,0:T(8,128)(2,1)S(1)}, bf16[1280,128]{1,0:T(8,128)(2,1)S(1)}, u32[]{:S(2)}, u32[]{:S(2)}) collective-permute-start(bf16[1280,128]{1,0:T(8,128)(2,1)S(1)} %lane1_6.1.refs_1_), channel_id=1, source_target_pairs={{1,2},{2,1},{5,6},{6,5},{9,10},{10,9},{13,14},{14,13},{17,18},{18,... | collective-permute-start | bytes 983048 | tf_op jit(solution)/shard_map/ppermute | solution.py:351
  52.7 14.8 %collective-permute-start.16 = (bf16[1280,128]{1,0:T(8,128)(2,1)S(1)}, bf16[1280,128]{1,0:T(8,128)(2,1)S(1)}, u32[]{:S(2)}, u32[]{:S(2)}) collective-permute-start(bf16[1280,128]{1,0:T(8,128)(2,1)S(1)} %lane0_7.1.refs_1_), channel_id=1, source_target_pairs={{0,1},{3,2},{2,3},{1,0},{4,5},{7,6},{6,7},{5,4},{8,9},{11,10},{10,... | collective-permute-start | bytes 983048 | tf_op jit(solution)/shard_map/ppermute | solution.py:351
  58.4 11.4 %collective-permute-start.15 = (bf16[1280,128]{1,0:T(8,128)(2,1)S(1)}, bf16[1280,128]{1,0:T(8,128)(2,1)S(1)}, u32[]{:S(2)}, u32[]{:S(2)}) collective-permute-start(bf16[1280,128]{1,0:T(8,128)(2,1)S(1)} %lane0_8.1), channel_id=1, source_target_pairs={{0,1},{3,2},{2,3},{1,0},{4,5},{7,6},{6,7},{5,4},{8,9},{11,10},{10,... | collective-permute-start | bytes 983048 | tf_op jit(solution)/shard_map/ppermute | solution.py:351

commit v2 on v1

--- a/solution.py
+++ b/solution.py
@@ -337,7 +337,7 @@
                 after.append(plan)
             arrivals = [arrived[piece][hop - 1] if hop else None for piece, hop in roles]
             sent = [(pieces[piece], hop) for piece, hop in roles]
-            flops = (3 - lane if slot == 2 else 2 if lane == 0 and slot == PIECES + 1 else 1) * 10**9
+            flops = (2 if lane == 0 and slot == PIECES + 1 else 1) * 10**9
             limit = 62 * MIB if newest is None else 4 * MIB
             newest = relay(panel_owner, own_a, notes, sent, arrivals, after, limit, flops, f"lane{lane}_{slot}")
             if slot == 1 and lane == 0:
@@ -348,6 +348,7 @@
             route = []
             for hop in sorted({lane, hops - 1 - lane}):
                 route += [(hop, hop + 1), (hops - hop, hops - hop - 1)]
+            route += [(i, i) for i in range(col_count) if i not in dict(route)]
             got = lax.ppermute(newest, "col", route)
             for piece, hop in roles:
                 arrived[piece][hop] = got

time: 72.3 us -> 74.2 us (1.026)
  waiting for transfers between devices: 2.24 us -> 3.59 us
    ppermute x1, waiting for transfers between devices: 0.33 us -> 1.33 us  [local(): moved_bc = lax.ppermute(behind_bc, 'row', from_next)]
  transfers between devices with their start and end apart: 17 -> 17, of which waited for: 3 -> 4; matrix products, arithmetic and copies ran while one was open for 0% -> 0% of each run, Pallas kernels for 27% -> 26%
where the time goes in v2:
time: 74.2 us; the launch traced here: 73.8 us
  starting transfers between devices  45.6 us (61%)
  Pallas kernels  24.1 us (32%)
  waiting for transfers between devices  3.59 us (5%)
    ppermute x15, starting transfers between devices, local(): got = lax.ppermute(newest, 'col', route)  41.4 us
    pallas_call x15, Pallas kernels, relay(): pl.pallas_call(functools.partial(relay_kernel, roles, len(after)), out_sh...  14.4 us
    pallas_call x3, Pallas kernels, multiply_rows(): pl.pallas_call(functools.partial(rows_kernel, first, count, hops, tuple(s...  8.61 us
    ppermute x1, starting transfers between devices, local(): moved_b = lax.ppermute(behind_b, 'row', from_next)  2.6 us
    ppermute x15, waiting for transfers between devices, local(): got = lax.ppermute(newest, 'col', route)  2.26 us
    ppermute x1, starting transfers between devices, local(): moved_bc = lax.ppermute(behind_bc, 'row', from_next)  1.66 us
  transfers between devices with their start and end apart: 17, of which 4 were waited for; matrix products, arithmetic and copies ran while one was open for 0% of the time, Pallas kernels for 26%

profile of v2, /device:TPU:0, one launch (start us, length us, event | category | flops | bytes accessed | tf_op | source)
XLA Modules:
  0.0 73.8 jit_solution(8650272262740400767)
XLA Ops:
  0.0 2.6 %lane0_0.1 = bf16[1280,128]{1,0:T(8,128)(2,1)} custom-call(s32[8,8]{1,0:T(8,128)} %owner.37, bf16[2,6,640,128]{3,2,1,0:T(8,128)(2,1)} %bitcast.12), custom_call_target="tpu_custom_call" | custom-call | flops 1000000000 | bytes 1024 | tf_op jit(solution)/shard_map/lane0_0/pallas_call | solution.py:93
  2.6 2.1 %collective-permute-start.2 = (bf16[1280,128]{1,0:T(8,128)(2,1)}, bf16[1280,128]{1,0:T(8,128)(2,1)S(1)}, u32[]{:S(2)}, u32[]{:S(2)}) collective-permute-start(bf16[1280,128]{1,0:T(8,128)(2,1)} %lane0_0.1), channel_id=1, source_target_pairs={{0,1},{3,2},{2,3},{1,0},{4,5},{7,6},{6,7},{5,4},{8,9},{11,10},{10,... | collective-permute-start | bytes 983048 | tf_op jit(solution)/shard_map/ppermute | solution.py:352
  4.9 1.1 %lane0_1.1 = bf16[1312,128]{1,0:T(8,128)(2,1)S(1)} custom-call(s32[8,8]{1,0:T(8,128)S(1)} %copy-done.2, bf16[2,6,640,128]{3,2,1,0:T(8,128)(2,1)S(1)} %bitcast.13, bf16[2,16,128]{2,1,0:T(8,128)(2,1)S(1)} %pad.4.refs_0_.notes), custom_call_target="tpu_custom_call" | custom-call | flops 1000000000 | bytes 1024 | tf_op jit(solution)/shard_map/lane0_1/pallas_call | solution.py:93
  6.1 1.7 %collective-permute-start = (s32[1,1,6,8]{3,2,1,0:T(8,128)S(1)}, s32[1,1,6,8]{3,2,1,0:T(8,128)S(1)}, u32[]{:S(2)}, u32[]{:S(2)}) collective-permute-start(s32[1,1,6,8]{3,2,1,0:T(8,128)S(1)} %copy.11), channel_id=1, source_target_pairs={{4,0},{8,4},{12,8},{16,12},{20,16},{24,20},{28,24},{0,28},{5,1},{9... | collective-permute-start | bytes 584 | tf_op jit(solution)/shard_map/ppermute | solution.py:345
  7.7 1.3 %collective-permute-done.refs_1_ = s32[1,1,6,8]{3,2,1,0:T(8,128)S(1)} collective-permute-done((s32[1,1,6,8]{3,2,1,0:T(8,128)S(1)}, s32[1,1,6,8]{3,2,1,0:T(8,128)S(1)}, u32[]{:S(2)}, u32[]{:S(2)}) %collective-permute-start) | collective-permute-done | bytes 224 | tf_op jit(solution)/shard_map/ppermute | solution.py:345
  9.1 2.6 %collective-permute-start.9 = (bf16[6,8,128,128]{3,2,1,0:T(8,128)(2,1)S(1)}, bf16[6,8,128,128]{3,2,1,0:T(8,128)(2,1)S(1)}, u32[]{:S(2)}, u32[]{:S(2)}) collective-permute-start(bf16[6,8,128,128]{3,2,1,0:T(8,128)(2,1)S(1)} %bitcast.30), channel_id=1, source_target_pairs={{4,0},{8,4},{12,8},{16,12},{20,16},{24,20},{28,24},{0,28},{5,1},{9... | collective-permute-start | bytes 4718600 | tf_op jit(solution)/shard_map/ppermute | solution.py:347
  11.7 1.0 %collective-permute-start.1 = (bf16[1312,128]{1,0:T(8,128)(2,1)S(1)}, bf16[1312,128]{1,0:T(8,128)(2,1)S(1)}, u32[]{:S(2)}, u32[]{:S(2)}) collective-permute-start(bf16[1312,128]{1,0:T(8,128)(2,1)S(1)} %lane0_1.1), channel_id=1, source_target_pairs={{0,1},{3,2},{2,3},{1,0},{4,5},{7,6},{6,7},{5,4},{8,9},{11,10},{10,... | collective-permute-start | bytes 1007624 | tf_op jit(solution)/shard_map/ppermute | solution.py:352
  12.7 0.8 %collective-permute-done.2.refs_0_ = bf16[1280,128]{1,0:T(8,128)(2,1)S(1)} collective-permute-done((bf16[1280,128]{1,0:T(8,128)(2,1)}, bf16[1280,128]{1,0:T(8,128)(2,1)S(1)}, u32[]{:S(2)}, u32[]{:S(2)}) %collective-permute-start.2) | collective-permute-done | bytes 327712 | tf_op jit(solution)/shard_map/ppermute | solution.py:352
  14.8 1.1 %lane0_2.1.refs_2_ = bf16[1280,128]{1,0:T(8,128)(2,1)S(1)} custom-call(s32[8,8]{1,0:T(8,128)S(1)} %copy-done.2, bf16[2,6,640,128]{3,2,1,0:T(8,128)(2,1)S(1)} %bitcast.15, bf16[1280,128]{1,0:T(8,128)(2,1)S(1)} %lane1_1.1.refs_0_), custom_call_target="tpu_custom_call" | custom-call | flops 1000000000 | bytes 1024 | tf_op jit(solution)/shard_map/lane0_2/pallas_call | solution.py:93
  15.9 5.3 %collective-permute-start.4 = (bf16[1280,128]{1,0:T(8,128)(2,1)S(1)}, bf16[1280,128]{1,0:T(8,128)(2,1)S(1)}, u32[]{:S(2)}, u32[]{:S(2)}) collective-permute-start(bf16[1280,128]{1,0:T(8,128)(2,1)S(1)} %lane0_2.1.refs_2_), channel_id=1, source_target_pairs={{0,1},{3,2},{2,3},{1,0},{4,5},{7,6},{6,7},{5,4},{8,9},{11,10},{10,... | collective-permute-start | bytes 983048 | tf_op jit(solution)/shard_map/ppermute | solution.py:352
  22.6 1.1 %lane0_3.1.refs_1_ = bf16[1280,128]{1,0:T(8,128)(2,1)S(1)} custom-call(s32[8,8]{1,0:T(8,128)S(1)} %copy-done.2, bf16[2,6,640,128]{3,2,1,0:T(8,128)(2,1)S(1)} %bitcast.17, bf16[1280,128]{1,0:T(8,128)(2,1)S(1)} %collective-permute-done.5.refs_0_.refs_1_, bf16[1312,128]{1,0:T(8,128)(2,1)S(1)} %lane1_2.1.refs_1_, ...), custom_call_target="tpu_custom_call" | custom-call | flops 1000000000 | bytes 1024 | tf_op jit(solution)/shard_map/lane0_3/pallas_call | solution.py:93
  23.7 6.0 %collective-permute-start.8 = (bf16[1280,128]{1,0:T(8,128)(2,1)S(1)}, bf16[1280,128]{1,0:T(8,128)(2,1)S(1)}, u32[]{:S(2)}, u32[]{:S(2)}) collective-permute-start(bf16[1280,128]{1,0:T(8,128)(2,1)S(1)} %lane0_3.1.refs_1_), channel_id=1, source_target_pairs={{0,1},{3,2},{2,3},{1,0},{4,5},{7,6},{6,7},{5,4},{8,9},{11,10},{10,... | collective-permute-start | bytes 983048 | tf_op jit(solution)/shard_map/ppermute | solution.py:352
  31.1 1.2 %lane0_4.1.refs_1_ = bf16[1312,128]{1,0:T(8,128)(2,1)S(1)} custom-call(s32[8,8]{1,0:T(8,128)S(1)} %copy-done.2, bf16[2,6,640,128]{3,2,1,0:T(8,128)(2,1)S(1)} %bitcast.19, bf16[2,16,128]{2,1,0:T(8,128)(2,1)S(1)} %pad.4.refs_0_.notes, bf16[1312,128]{1,0:T(8,128)(2,1)S(1)} %collective-permute-done.3.refs_1_.refs_4_, bf16[1280,128]{1,0:T(8,128)(2,1)S(1)} %lane1_3.1.refs_2_, ...), custom_call_target="tpu_custom_call" | custom-call | flops 1000000000 | bytes 1024 | tf_op jit(solution)/shard_map/lane0_4/pallas_call | solution.py:93
  32.3 4.5 %collective-permute-start.6 = (bf16[1312,128]{1,0:T(8,128)(2,1)S(1)}, bf16[1312,128]{1,0:T(8,128)(2,1)S(1)}, u32[]{:S(2)}, u32[]{:S(2)}) collective-permute-start(bf16[1312,128]{1,0:T(8,128)(2,1)S(1)} %lane0_4.1.refs_1_), channel_id=1, source_target_pairs={{0,1},{3,2},{2,3},{1,0},{4,5},{7,6},{6,7},{5,4},{8,9},{11,10},{10,... | collective-permute-start | bytes 1007624 | tf_op jit(solution)/shard_map/ppermute | solution.py:352
  38.2 1.1 %lane0_5.1.refs_1_ = bf16[1280,128]{1,0:T(8,128)(2,1)S(1)} custom-call(s32[8,8]{1,0:T(8,128)S(1)} %copy-done.2, bf16[2,6,640,128]{3,2,1,0:T(8,128)(2,1)S(1)} %bitcast.21, bf16[1280,128]{1,0:T(8,128)(2,1)S(1)} %collective-permute-done.7.refs_0_.refs_7_, bf16[1280,128]{1,0:T(8,128)(2,1)S(1)} %lane1_4.1.refs_1_, ...), custom_call_target="tpu_custom_call" | custom-call | flops 1000000000 | bytes 1024 | tf_op jit(solution)/shard_map/lane0_5/pallas_call | solution.py:93
  39.3 5.1 %collective-permute-start.10 = (bf16[1280,128]{1,0:T(8,128)(2,1)S(1)}, bf16[1280,128]{1,0:T(8,128)(2,1)S(1)}, u32[]{:S(2)}, u32[]{:S(2)}) collective-permute-start(bf16[1280,128]{1,0:T(8,128)(2,1)S(1)} %lane0_5.1.refs_1_), channel_id=1, source_target_pairs={{0,1},{3,2},{2,3},{1,0},{4,5},{7,6},{6,7},{5,4},{8,9},{11,10},{10,... | collective-permute-start | bytes 983048 | tf_op jit(solution)/shard_map/ppermute | solution.py:352
  45.8 1.1 %make_plan.1.refs_3_.plan = s32[16,128]{1,0:T(8,128)S(1)} custom-call(s32[8,8]{1,0:T(8,128)S(1)} %copy-done.2, s32[48]{0:T(128)S(1)} %copy-done.3, s32[6,8]{1,0:T(8,128)S(1)} %bitcast.34, s32[6,8]{1,0:T(8,128)S(1)} %bitcast.36, s32[6,6]{1,0:T(8,128)S(1)} %bitcast.35, bf16[2,16,128]{2,1,0:T(8,128)(2,1)S(1)} %pad.4.refs_0_.notes, ...), custom_call_target="tpu_custom_call" | custom-call | flops 1000000000 | bytes 1024 | tf_op jit(solution)/shard_map/make_plan/pallas_call | solution.py:175
  47.6 5.3 %collective-permute-start.14 = (bf16[1280,128]{1,0:T(8,128)(2,1)S(1)}, bf16[1280,128]{1,0:T(8,128)(2,1)S(1)}, u32[]{:S(2)}, u32[]{:S(2)}) collective-permute-start(bf16[1280,128]{1,0:T(8,128)(2,1)S(1)} %lane0_6.1.refs_1_), channel_id=1, source_target_pairs={{0,1},{3,2},{2,3},{1,0},{4,5},{7,6},{6,7},{5,4},{8,9},{11,10},{10,... | collective-permute-start | bytes 983048 | tf_op jit(solution)/shard_map/ppermute | solution.py:352
  55.0 4.9 %collective-permute-start.16 = (bf16[1280,128]{1,0:T(8,128)(2,1)S(1)}, bf16[1280,128]{1,0:T(8,128)(2,1)S(1)}, u32[]{:S(2)}, u32[]{:S(2)}) collective-permute-start(bf16[1280,128]{1,0:T(8,128)(2,1)S(1)} %lane0_7.1.refs_1_), channel_id=1, source_target_pairs={{0,1},{3,2},{2,3},{1,0},{4,5},{7,6},{6,7},{5,4},{8,9},{11,10},{10,... | collective-permute-start | bytes 983048 | tf_op jit(solution)/shard_map/ppermute | solution.py:352
  59.9 0.8 %collective-permute-done.14.refs_2_.refs_11_ = bf16[1280,128]{1,0:T(8,128)(2,1)S(1)} collective-permute-done((bf16[1280,128]{1,0:T(8,128)(2,1)S(1)}, bf16[1280,128]{1,0:T(8,128)(2,1)S(1)}, u32[]{:S(2)}, u32[]{:S(2)}) %collective-permute-start.14) | collective-permute-done | bytes 327712 | tf_op jit(solution)/shard_map/ppermute | solution.py:352
  61.4 3.1 %collective-permute-start.15 = (bf16[1280,128]{1,0:T(8,128)(2,1)S(1)}, bf16[1280,128]{1,0:T(8,128)(2,1)S(1)}, u32[]{:S(2)}, u32[]{:S(2)}) collective-permute-start(bf16[1280,128]{1,0:T(8,128)(2,1)S(1)} %lane0_8.1), channel_id=1, source_target_pairs={{0,1},{3,2},{2,3},{1,0},{4,5},{7,6},{6,7},{5,4},{8,9},{11,10},{10,... | collective-permute-start | bytes 983048 | tf_op jit(solution)/shard_map/ppermute | solution.py:352
  64.6 4.3 %multiply_rows.3.refs_3_ = bf16[6,6,128,128]{3,2,1,0:T(8,128)(2,1)} custom-call(s32[8,8]{1,0:T(8,128)S(1)} %copy-done.2, s32[16,128]{1,0:T(8,128)S(1)} %make_plan.1.refs_3_.plan, bf16[6,8,128,128]{3,2,1,0:T(8,128)(2,1)S(1)} %bitcast.31, bf16[6,8,128,128]{3,2,1,0:T(8,128)(2,1)S(1)} %collective-permute-done.9.refs_2_.b1, ...), custom_call_target="tpu_custom_call" | custom-call | flops 2013265920 | bytes 4194304 | tf_op jit(solution)/shard_map/multiply_rows/pallas_call | solution.py:277
  68.9 2.2 %multiply_rows.4.refs_3_ = bf16[6,6,128,128]{3,2,1,0:T(8,128)(2,1)} custom-call(s32[8,8]{1,0:T(8,128)S(1)} %copy-done.2, s32[16,128]{1,0:T(8,128)S(1)} %make_plan.1.refs_3_.plan, bf16[6,8,128,128]{3,2,1,0:T(8,128)(2,1)S(1)} %bitcast.32, bf16[6,8,128,128]{3,2,1,0:T(8,128)(2,1)S(1)} %collective-permute-done.9.refs_2_.b1, ...), custom_call_target="tpu_custom_call", output_to_operand_aliasing={{}: (8, {})} | custom-call | flops 503316480 | bytes 4194304 | tf_op jit(solution)/shard_map/multiply_rows/pallas_call | solution.py:277
  71.7 2.1 %multiply_rows.5 = bf16[6,6,128,128]{3,2,1,0:T(8,128)(2,1)} custom-call(s32[8,8]{1,0:T(8,128)S(1)} %copy-done.2, s32[16,128]{1,0:T(8,128)S(1)} %make_plan.1.refs_3_.plan, bf16[6,8,128,128]{3,2,1,0:T(8,128)(2,1)S(1)} %bitcast.33, bf16[6,8,128,128]{3,2,1,0:T(8,128)(2,1)S(1)} %collective-permute-done.9.refs_2_.b1, ...), custom_call_target="tpu_custom_call", output_to_operand_aliasing={{}: (8, {})} | custom-call | flops 503316480 | bytes 4194304 | tf_op jit(solution)/shard_map/multiply_rows/pallas_call | solution.py:277
  (49 shorter events, 11.1 us)
Async XLA Ops:
  0.0 4.7 %copy-start.5 = (s32[1,1,2,6,5]{3,2,4,1,0:T(2,128)S(1)}, s32[1,1,2,6,5]{3,2,4,1,0:T(2,128)}, u32[]{:S(2)}) copy-start(s32[1,1,2,6,5]{3,2,4,1,0:T(2,128)} %param.8) | copy-start | bytes 724
  0.0 4.9 %copy-start = (bf16[1,1,2,6,5,128,128]{6,5,4,3,2,1,0:T(8,128)(2,1)S(1)}, bf16[1,1,2,6,5,128,128]{6,5,4,3,2,1,0:T(8,128)(2,1)}, u32[]{:S(2)}) copy-start(bf16[1,1,2,6,5,128,128]{6,5,4,3,2,1,0:T(8,128)(2,1)} %param.7) | copy-start | bytes 5898244
  0.0 4.9 %copy-start.2 = (s32[8,8]{1,0:T(8,128)S(1)}, s32[8,8]{1,0:T(8,128)}, u32[]{:S(2)}) copy-start(s32[8,8]{1,0:T(8,128)} %owner.37) | copy-start | bytes 772
  2.6 10.8 %collective-permute-start.2 = (bf16[1280,128]{1,0:T(8,128)(2,1)}, bf16[1280,128]{1,0:T(8,128)(2,1)S(1)}, u32[]{:S(2)}, u32[]{:S(2)}) collective-permute-start(bf16[1280,128]{1,0:T(8,128)(2,1)} %lane0_0.1), channel_id=1, source_target_pairs={{0,1},{3,2},{2,3},{1,0},{4,5},{7,6},{6,7},{5,4},{8,9},{11,10},{10,... | collective-permute-start | bytes 983048 | tf_op jit(solution)/shard_map/ppermute | solution.py:352
  4.9 1.2 %copy-start.4 = (s32[1,1,6,8]{3,1,2,0:T(1,128)S(1)}, s32[1,1,6,8]{3,1,2,0:T(1,128)}, u32[]{:S(2)}) copy-start(s32[1,1,6,8]{3,1,2,0:T(1,128)} %param.10) | copy-start | bytes 580
  4.9 4.2 %copy-start.1 = (bf16[1,1,6,8,128,128]{5,4,3,2,1,0:T(8,128)(2,1)S(1)}, bf16[1,1,6,8,128,128]{5,4,3,2,1,0:T(8,128)(2,1)}, u32[]{:S(2)}) copy-start(bf16[1,1,6,8,128,128]{5,4,3,2,1,0:T(8,128)(2,1)} %param.9) | copy-start | bytes 4718596
  6.1 3.0 %collective-permute-start = (s32[1,1,6,8]{3,2,1,0:T(8,128)S(1)}, s32[1,1,6,8]{3,2,1,0:T(8,128)S(1)}, u32[]{:S(2)}, u32[]{:S(2)}) collective-permute-start(s32[1,1,6,8]{3,2,1,0:T(8,128)S(1)} %copy.11), channel_id=1, source_target_pairs={{4,0},{8,4},{12,8},{16,12},{20,16},{24,20},{28,24},{0,28},{5,1},{9... | collective-permute-start | bytes 584 | tf_op jit(solution)/shard_map/ppermute | solution.py:345
  9.1 43.9 %collective-permute-start.9 = (bf16[6,8,128,128]{3,2,1,0:T(8,128)(2,1)S(1)}, bf16[6,8,128,128]{3,2,1,0:T(8,128)(2,1)S(1)}, u32[]{:S(2)}, u32[]{:S(2)}) collective-permute-start(bf16[6,8,128,128]{3,2,1,0:T(8,128)(2,1)S(1)} %bitcast.30), channel_id=1, source_target_pairs={{4,0},{8,4},{12,8},{16,12},{20,16},{24,20},{28,24},{0,28},{5,1},{9... | collective-permute-start | bytes 4718600 | tf_op jit(solution)/shard_map/ppermute | solution.py:347
  11.7 9.5 %collective-permute-start.1 = (bf16[1312,128]{1,0:T(8,128)(2,1)S(1)}, bf16[1312,128]{1,0:T(8,128)(2,1)S(1)}, u32[]{:S(2)}, u32[]{:S(2)}) collective-permute-start(bf16[1312,128]{1,0:T(8,128)(2,1)S(1)} %lane0_1.1), channel_id=1, source_target_pairs={{0,1},{3,2},{2,3},{1,0},{4,5},{7,6},{6,7},{5,4},{8,9},{11,10},{10,... | collective-permute-start | bytes 1007624 | tf_op jit(solution)/shard_map/ppermute | solution.py:352
  14.1 8.5 %collective-permute-start.5 = (bf16[1280,128]{1,0:T(8,128)(2,1)S(1)}, bf16[1280,128]{1,0:T(8,128)(2,1)S(1)}, u32[]{:S(2)}, u32[]{:S(2)}) collective-permute-start(bf16[1280,128]{1,0:T(8,128)(2,1)S(1)} %lane1_1.1.refs_0_), channel_id=1, source_target_pairs={{1,2},{2,1},{0,0},{3,3},{5,6},{6,5},{4,4},{7,7},{9,10},{10,9},{8,8... | collective-permute-start | bytes 983048 | tf_op jit(solution)/shard_map/ppermute | solution.py:352
  15.9 13.8 %collective-permute-start.4 = (bf16[1280,128]{1,0:T(8,128)(2,1)S(1)}, bf16[1280,128]{1,0:T(8,128)(2,1)S(1)}, u32[]{:S(2)}, u32[]{:S(2)}) collective-permute-start(bf16[1280,128]{1,0:T(8,128)(2,1)S(1)} %lane0_2.1.refs_2_), channel_id=1, source_target_pairs={{0,1},{3,2},{2,3},{1,0},{4,5},{7,6},{6,7},{5,4},{8,9},{11,10},{10,... | collective-permute-start | bytes 983048 | tf_op jit(solution)/shard_map/ppermute | solution.py:352
  21.9 9.2 %collective-permute-start.3 = (bf16[1312,128]{1,0:T(8,128)(2,1)S(1)}, bf16[1312,128]{1,0:T(8,128)(2,1)S(1)}, u32[]{:S(2)}, u32[]{:S(2)}) collective-permute-start(bf16[1312,128]{1,0:T(8,128)(2,1)S(1)} %lane1_2.1.refs_1_), channel_id=1, source_target_pairs={{1,2},{2,1},{0,0},{3,3},{5,6},{6,5},{4,4},{7,7},{9,10},{10,9},{8,8... | collective-permute-start | bytes 1007624 | tf_op jit(solution)/shard_map/ppermute | solution.py:352
  23.7 13.0 %collective-permute-start.8 = (bf16[1280,128]{1,0:T(8,128)(2,1)S(1)}, bf16[1280,128]{1,0:T(8,128)(2,1)S(1)}, u32[]{:S(2)}, u32[]{:S(2)}) collective-permute-start(bf16[1280,128]{1,0:T(8,128)(2,1)S(1)} %lane0_3.1.refs_1_), channel_id=1, source_target_pairs={{0,1},{3,2},{2,3},{1,0},{4,5},{7,6},{6,7},{5,4},{8,9},{11,10},{10,... | collective-permute-start | bytes 983048 | tf_op jit(solution)/shard_map/ppermute | solution.py:352
  30.4 7.7 %collective-permute-start.7 = (bf16[1280,128]{1,0:T(8,128)(2,1)S(1)}, bf16[1280,128]{1,0:T(8,128)(2,1)S(1)}, u32[]{:S(2)}, u32[]{:S(2)}) collective-permute-start(bf16[1280,128]{1,0:T(8,128)(2,1)S(1)} %lane1_3.1.refs_2_), channel_id=1, source_target_pairs={{1,2},{2,1},{0,0},{3,3},{5,6},{6,5},{4,4},{7,7},{9,10},{10,9},{8,8... | collective-permute-start | bytes 983048 | tf_op jit(solution)/shard_map/ppermute | solution.py:352
  32.3 12.1 %collective-permute-start.6 = (bf16[1312,128]{1,0:T(8,128)(2,1)S(1)}, bf16[1312,128]{1,0:T(8,128)(2,1)S(1)}, u32[]{:S(2)}, u32[]{:S(2)}) collective-permute-start(bf16[1312,128]{1,0:T(8,128)(2,1)S(1)} %lane0_4.1.refs_1_), channel_id=1, source_target_pairs={{0,1},{3,2},{2,3},{1,0},{4,5},{7,6},{6,7},{5,4},{8,9},{11,10},{10,... | collective-permute-start | bytes 1007624 | tf_op jit(solution)/shard_map/ppermute | solution.py:352
  37.5 7.0 %copy-start.6 = (s32[1,1,6,6]{3,1,2,0:T(1,128)S(1)}, s32[1,1,6,6]{3,1,2,0:T(1,128)}, u32[]{:S(2)}) copy-start(s32[1,1,6,6]{3,1,2,0:T(1,128)} %param.11) | copy-start | bytes 436
  37.5 9.5 %collective-permute-start.11 = (bf16[1280,128]{1,0:T(8,128)(2,1)S(1)}, bf16[1280,128]{1,0:T(8,128)(2,1)S(1)}, u32[]{:S(2)}, u32[]{:S(2)}) collective-permute-start(bf16[1280,128]{1,0:T(8,128)(2,1)S(1)} %lane1_4.1.refs_1_), channel_id=1, source_target_pairs={{1,2},{2,1},{0,0},{3,3},{5,6},{6,5},{4,4},{7,7},{9,10},{10,9},{8,8... | collective-permute-start | bytes 983048 | tf_op jit(solution)/shard_map/ppermute | solution.py:352
  39.3 13.6 %collective-permute-start.10 = (bf16[1280,128]{1,0:T(8,128)(2,1)S(1)}, bf16[1280,128]{1,0:T(8,128)(2,1)S(1)}, u32[]{:S(2)}, u32[]{:S(2)}) collective-permute-start(bf16[1280,128]{1,0:T(8,128)(2,1)S(1)} %lane0_5.1.refs_1_), channel_id=1, source_target_pairs={{0,1},{3,2},{2,3},{1,0},{4,5},{7,6},{6,7},{5,4},{8,9},{11,10},{10,... | collective-permute-start | bytes 983048 | tf_op jit(solution)/shard_map/ppermute | solution.py:352
  44.4 1.4 %copy-start.3 = (s32[48]{0:T(128)S(1)}, s32[48]{0:T(128)}, u32[]{:S(2)}) copy-start(s32[48]{0:T(128)} %atoms.1) | copy-start | bytes 580
  45.1 9.2 %collective-permute-start.13 = (bf16[1280,128]{1,0:T(8,128)(2,1)S(1)}, bf16[1280,128]{1,0:T(8,128)(2,1)S(1)}, u32[]{:S(2)}, u32[]{:S(2)}) collective-permute-start(bf16[1280,128]{1,0:T(8,128)(2,1)S(1)} %lane1_5.1.refs_3_.refs_1_), channel_id=1, source_target_pairs={{1,2},{2,1},{0,0},{3,3},{5,6},{6,5},{4,4},{7,7},{9,10},{10,9},{8,8... | collective-permute-start | bytes 983048 | tf_op jit(solution)/shard_map/ppermute | solution.py:352
  47.6 13.1 %collective-permute-start.14 = (bf16[1280,128]{1,0:T(8,128)(2,1)S(1)}, bf16[1280,128]{1,0:T(8,128)(2,1)S(1)}, u32[]{:S(2)}, u32[]{:S(2)}) collective-permute-start(bf16[1280,128]{1,0:T(8,128)(2,1)S(1)} %lane0_6.1.refs_1_), channel_id=1, source_target_pairs={{0,1},{3,2},{2,3},{1,0},{4,5},{7,6},{6,7},{5,4},{8,9},{11,10},{10,... | collective-permute-start | bytes 983048 | tf_op jit(solution)/shard_map/ppermute | solution.py:352
  53.6 7.1 %collective-permute-start.12 = (bf16[1280,128]{1,0:T(8,128)(2,1)S(1)}, bf16[1280,128]{1,0:T(8,128)(2,1)S(1)}, u32[]{:S(2)}, u32[]{:S(2)}) collective-permute-start(bf16[1280,128]{1,0:T(8,128)(2,1)S(1)} %lane1_6.1.refs_1_), channel_id=1, source_target_pairs={{1,2},{2,1},{0,0},{3,3},{5,6},{6,5},{4,4},{7,7},{9,10},{10,9},{8,8... | collective-permute-start | bytes 983048 | tf_op jit(solution)/shard_map/ppermute | solution.py:352
  55.0 13.9 %collective-permute-start.16 = (bf16[1280,128]{1,0:T(8,128)(2,1)S(1)}, bf16[1280,128]{1,0:T(8,128)(2,1)S(1)}, u32[]{:S(2)}, u32[]{:S(2)}) collective-permute-start(bf16[1280,128]{1,0:T(8,128)(2,1)S(1)} %lane0_7.1.refs_1_), channel_id=1, source_target_pairs={{0,1},{3,2},{2,3},{1,0},{4,5},{7,6},{6,7},{5,4},{8,9},{11,10},{10,... | collective-permute-start | bytes 983048 | tf_op jit(solution)/shard_map/ppermute | solution.py:352
  61.4 10.2 %collective-permute-start.15 = (bf16[1280,128]{1,0:T(8,128)(2,1)S(1)}, bf16[1280,128]{1,0:T(8,128)(2,1)S(1)}, u32[]{:S(2)}, u32[]{:S(2)}) collective-permute-start(bf16[1280,128]{1,0:T(8,128)(2,1)S(1)} %lane0_8.1), channel_id=1, source_target_pairs={{0,1},{3,2},{2,3},{1,0},{4,5},{7,6},{6,7},{5,4},{8,9},{11,10},{10,... | collective-permute-start | bytes 983048 | tf_op jit(solution)/shard_map/ppermute | solution.py:352

commit v3 on v1

--- a/solution.py
+++ b/solution.py
@@ -8,7 +8,7 @@
 from jax.sharding import PartitionSpec as P
 
 STEPS = 2
-SHARES = (1, 1, 1, 1, 1, 1)
+SHARES = (1, 1, 1, 1, 1, 1, 1, 1)
 PIECES = len(SHARES)
 NOTED = 1
 NOTE = 16

time: 72.3 us -> 78.1 us (1.080); the launches traced: 72 us -> 77 us
  Pallas kernels: 24.1 us -> 28.1 us
  starting transfers between devices: 45.1 us -> 47.9 us
  waiting for transfers between devices: 2.24 us -> 0.44 us
    pallas_call x15 -> x19, Pallas kernels: 14.4 us -> 17.2 us  [relay(): pl.pallas_call(functools.partial(relay_kernel, roles, len(after)), out_sh...]
    ppermute x15 -> x19, starting transfers between devices: 40.9 us -> 43.6 us  [local(): got = lax.ppermute(newest, 'col', route)]
    ppermute x15 -> x19, waiting for transfers between devices: 1.91 us -> 0.18 us  [local(): got = lax.ppermute(newest, 'col', route)]
    pallas_call x3, Pallas kernels: 8.6 us -> 9.85 us  [multiply_rows(): pl.pallas_call(functools.partial(rows_kernel, first, count, hops, tuple(s...]
  transfers between devices with their start and end apart: 17 -> 21, of which waited for: 3 -> 2; matrix products, arithmetic and copies ran while one was open for 0% -> 0% of each run, Pallas kernels for 27% -> 30%
where the time goes in v3:
time: 78.1 us; the launch traced here: 77 us
  starting transfers between devices  47.9 us (61%)
  Pallas kernels  28.1 us (36%)
    ppermute x19, starting transfers between devices, local(): got = lax.ppermute(newest, 'col', route)  43.6 us
    pallas_call x19, Pallas kernels, relay(): pl.pallas_call(functools.partial(relay_kernel, roles, len(after)), out_sh...  17.2 us
    pallas_call x3, Pallas kernels, multiply_rows(): pl.pallas_call(functools.partial(rows_kernel, first, count, hops, tuple(s...  9.85 us
    ppermute x1, starting transfers between devices, local(): moved_b = lax.ppermute(behind_b, 'row', from_next)  2.6 us
    ppermute x1, starting transfers between devices, local(): moved_bc = lax.ppermute(behind_bc, 'row', from_next)  1.66 us
  transfers between devices with their start and end apart: 21, of which 2 were waited for; matrix products, arithmetic and copies ran while one was open for 0% of the time, Pallas kernels for 30%

profile of v3, /device:TPU:0, one launch (start us, length us, event | category | flops | bytes accessed | tf_op | source)
XLA Modules:
  0.0 77.0 jit_solution(16019398036436291267)
XLA Ops:
  0.0 2.6 %lane0_0.1 = bf16[960,128]{1,0:T(8,128)(2,1)} custom-call(s32[8,8]{1,0:T(8,128)} %owner.45, bf16[2,6,640,128]{3,2,1,0:T(8,128)(2,1)} %bitcast.12), custom_call_target="tpu_custom_call" | custom-call | flops 1000000000 | bytes 1024 | tf_op jit(solution)/shard_map/lane0_0/pallas_call | solution.py:93
  2.6 2.1 %collective-permute-start.2 = (bf16[960,128]{1,0:T(8,128)(2,1)}, bf16[960,128]{1,0:T(8,128)(2,1)S(1)}, u32[]{:S(2)}, u32[]{:S(2)}) collective-permute-start(bf16[960,128]{1,0:T(8,128)(2,1)} %lane0_0.1), channel_id=1, source_target_pairs={{0,1},{3,2},{2,3},{1,0},{4,5},{7,6},{6,7},{5,4},{8,9},{11,10},{10,... | collective-permute-start | bytes 737288 | tf_op jit(solution)/shard_map/ppermute | solution.py:351
  4.9 1.0 %lane0_1.1 = bf16[992,128]{1,0:T(8,128)(2,1)S(1)} custom-call(s32[8,8]{1,0:T(8,128)S(1)} %copy-done.2, bf16[2,6,640,128]{3,2,1,0:T(8,128)(2,1)S(1)} %bitcast.13, bf16[2,16,128]{2,1,0:T(8,128)(2,1)S(1)} %pad.4.refs_0_.notes), custom_call_target="tpu_custom_call" | custom-call | flops 1000000000 | bytes 1024 | tf_op jit(solution)/shard_map/lane0_1/pallas_call | solution.py:93
  5.9 1.7 %collective-permute-start = (s32[1,1,6,8]{3,2,1,0:T(8,128)S(1)}, s32[1,1,6,8]{3,2,1,0:T(8,128)S(1)}, u32[]{:S(2)}, u32[]{:S(2)}) collective-permute-start(s32[1,1,6,8]{3,2,1,0:T(8,128)S(1)} %copy.11), channel_id=1, source_target_pairs={{4,0},{8,4},{12,8},{16,12},{20,16},{24,20},{28,24},{0,28},{5,1},{9... | collective-permute-start | bytes 584 | tf_op jit(solution)/shard_map/ppermute | solution.py:345
  7.6 1.1 %collective-permute-start.1 = (bf16[992,128]{1,0:T(8,128)(2,1)S(1)}, bf16[992,128]{1,0:T(8,128)(2,1)S(1)}, u32[]{:S(2)}, u32[]{:S(2)}) collective-permute-start(bf16[992,128]{1,0:T(8,128)(2,1)S(1)} %lane0_1.1), channel_id=1, source_target_pairs={{0,1},{3,2},{2,3},{1,0},{4,5},{7,6},{6,7},{5,4},{8,9},{11,10},{10,... | collective-permute-start | bytes 761864 | tf_op jit(solution)/shard_map/ppermute | solution.py:351
  8.9 2.6 %collective-permute-start.13 = (bf16[6,8,128,128]{3,2,1,0:T(8,128)(2,1)S(1)}, bf16[6,8,128,128]{3,2,1,0:T(8,128)(2,1)S(1)}, u32[]{:S(2)}, u32[]{:S(2)}) collective-permute-start(bf16[6,8,128,128]{3,2,1,0:T(8,128)(2,1)S(1)} %bitcast.34), channel_id=1, source_target_pairs={{4,0},{8,4},{12,8},{16,12},{20,16},{24,20},{28,24},{0,28},{5,1},{9... | collective-permute-start | bytes 4718600 | tf_op jit(solution)/shard_map/ppermute | solution.py:347
  14.0 5.1 %collective-permute-start.4 = (bf16[960,128]{1,0:T(8,128)(2,1)S(1)}, bf16[960,128]{1,0:T(8,128)(2,1)S(1)}, u32[]{:S(2)}, u32[]{:S(2)}) collective-permute-start(bf16[960,128]{1,0:T(8,128)(2,1)S(1)} %lane0_2.1.refs_2_), channel_id=1, source_target_pairs={{0,1},{3,2},{2,3},{1,0},{4,5},{7,6},{6,7},{5,4},{8,9},{11,10},{10,... | collective-permute-start | bytes 737288 | tf_op jit(solution)/shard_map/ppermute | solution.py:351
  20.6 1.0 %lane0_3.1.refs_1_ = bf16[960,128]{1,0:T(8,128)(2,1)S(1)} custom-call(s32[8,8]{1,0:T(8,128)S(1)} %copy-done.2, bf16[2,6,640,128]{3,2,1,0:T(8,128)(2,1)S(1)} %bitcast.17, bf16[960,128]{1,0:T(8,128)(2,1)S(1)} %collective-permute-done.5.refs_0_.refs_1_, bf16[992,128]{1,0:T(8,128)(2,1)S(1)} %lane1_2.1.refs_1_, ...), custom_call_target="tpu_custom_call" | custom-call | flops 1000000000 | bytes 1024 | tf_op jit(solution)/shard_map/lane0_3/pallas_call | solution.py:93
  21.6 2.7 %collective-permute-start.7 = (bf16[960,128]{1,0:T(8,128)(2,1)S(1)}, bf16[960,128]{1,0:T(8,128)(2,1)S(1)}, u32[]{:S(2)}, u32[]{:S(2)}) collective-permute-start(bf16[960,128]{1,0:T(8,128)(2,1)S(1)} %lane0_3.1.refs_1_), channel_id=1, source_target_pairs={{0,1},{3,2},{2,3},{1,0},{4,5},{7,6},{6,7},{5,4},{8,9},{11,10},{10,... | collective-permute-start | bytes 737288 | tf_op jit(solution)/shard_map/ppermute | solution.py:351
  25.7 1.0 %lane0_4.1.refs_1_ = bf16[992,128]{1,0:T(8,128)(2,1)S(1)} custom-call(s32[8,8]{1,0:T(8,128)S(1)} %copy-done.2, bf16[2,6,640,128]{3,2,1,0:T(8,128)(2,1)S(1)} %bitcast.19, bf16[2,16,128]{2,1,0:T(8,128)(2,1)S(1)} %pad.4.refs_0_.notes, bf16[992,128]{1,0:T(8,128)(2,1)S(1)} %collective-permute-done.3.refs_1_.refs_4_, bf16[960,128]{1,0:T(8,128)(2,1)S(1)} %lane1_3.1.refs_2_, ...), custom_call_target="tpu_custom_call" | custom-call | flops 1000000000 | bytes 1024 | tf_op jit(solution)/shard_map/lane0_4/pallas_call | solution.py:93
  26.7 3.8 %collective-permute-start.6 = (bf16[992,128]{1,0:T(8,128)(2,1)S(1)}, bf16[992,128]{1,0:T(8,128)(2,1)S(1)}, u32[]{:S(2)}, u32[]{:S(2)}) collective-permute-start(bf16[992,128]{1,0:T(8,128)(2,1)S(1)} %lane0_4.1.refs_1_), channel_id=1, source_target_pairs={{0,1},{3,2},{2,3},{1,0},{4,5},{7,6},{6,7},{5,4},{8,9},{11,10},{10,... | collective-permute-start | bytes 761864 | tf_op jit(solution)/shard_map/ppermute | solution.py:351
  31.9 1.0 %lane0_5.1.refs_1_ = bf16[960,128]{1,0:T(8,128)(2,1)S(1)} custom-call(s32[8,8]{1,0:T(8,128)S(1)} %copy-done.2, bf16[2,6,640,128]{3,2,1,0:T(8,128)(2,1)S(1)} %bitcast.21, bf16[960,128]{1,0:T(8,128)(2,1)S(1)} %collective-permute-done.9.refs_0_.refs_7_, bf16[960,128]{1,0:T(8,128)(2,1)S(1)} %lane1_4.1.refs_1_, ...), custom_call_target="tpu_custom_call" | custom-call | flops 1000000000 | bytes 1024 | tf_op jit(solution)/shard_map/lane0_5/pallas_call | solution.py:93
  32.9 3.5 %collective-permute-start.12 = (bf16[960,128]{1,0:T(8,128)(2,1)S(1)}, bf16[960,128]{1,0:T(8,128)(2,1)S(1)}, u32[]{:S(2)}, u32[]{:S(2)}) collective-permute-start(bf16[960,128]{1,0:T(8,128)(2,1)S(1)} %lane0_5.1.refs_1_), channel_id=1, source_target_pairs={{0,1},{3,2},{2,3},{1,0},{4,5},{7,6},{6,7},{5,4},{8,9},{11,10},{10,... | collective-permute-start | bytes 737288 | tf_op jit(solution)/shard_map/ppermute | solution.py:351
  37.8 1.0 %lane0_6.1.refs_1_ = bf16[960,128]{1,0:T(8,128)(2,1)S(1)} custom-call(s32[8,8]{1,0:T(8,128)S(1)} %copy-done.2, bf16[2,6,640,128]{3,2,1,0:T(8,128)(2,1)S(1)} %bitcast.23, bf16[960,128]{1,0:T(8,128)(2,1)S(1)} %collective-permute-done.8.refs_0_.refs_10_, bf16[960,128]{1,0:T(8,128)(2,1)S(1)} %lane1_5.1.refs_1_, ...), custom_call_target="tpu_custom_call" | custom-call | flops 1000000000 | bytes 1024 | tf_op jit(solution)/shard_map/lane0_6/pallas_call | solution.py:93
  38.8 5.3 %collective-permute-start.10 = (bf16[960,128]{1,0:T(8,128)(2,1)S(1)}, bf16[960,128]{1,0:T(8,128)(2,1)S(1)}, u32[]{:S(2)}, u32[]{:S(2)}) collective-permute-start(bf16[960,128]{1,0:T(8,128)(2,1)S(1)} %lane0_6.1.refs_1_), channel_id=1, source_target_pairs={{0,1},{3,2},{2,3},{1,0},{4,5},{7,6},{6,7},{5,4},{8,9},{11,10},{10,... | collective-permute-start | bytes 737288 | tf_op jit(solution)/shard_map/ppermute | solution.py:351
  45.5 1.0 %lane0_7.1.refs_1_ = bf16[960,128]{1,0:T(8,128)(2,1)S(1)} custom-call(s32[8,8]{1,0:T(8,128)S(1)} %copy-done.2, bf16[2,6,640,128]{3,2,1,0:T(8,128)(2,1)S(1)} %bitcast.25, bf16[960,128]{1,0:T(8,128)(2,1)S(1)} %collective-permute-done.11.refs_0_.refs_13_, bf16[960,128]{1,0:T(8,128)(2,1)S(1)} %lane1_6.1.refs_1_, ...), custom_call_target="tpu_custom_call" | custom-call | flops 1000000000 | bytes 1024 | tf_op jit(solution)/shard_map/lane0_7/pallas_call | solution.py:93
  46.5 3.1 %collective-permute-start.15 = (bf16[960,128]{1,0:T(8,128)(2,1)S(1)}, bf16[960,128]{1,0:T(8,128)(2,1)S(1)}, u32[]{:S(2)}, u32[]{:S(2)}) collective-permute-start(bf16[960,128]{1,0:T(8,128)(2,1)S(1)} %lane0_7.1.refs_1_), channel_id=1, source_target_pairs={{0,1},{3,2},{2,3},{1,0},{4,5},{7,6},{6,7},{5,4},{8,9},{11,10},{10,... | collective-permute-start | bytes 737288 | tf_op jit(solution)/shard_map/ppermute | solution.py:351
  51.0 1.1 %make_plan.1.refs_3_.plan = s32[16,128]{1,0:T(8,128)S(1)} custom-call(s32[8,8]{1,0:T(8,128)S(1)} %copy-done.2, s32[48]{0:T(128)S(1)} %copy-done.3, s32[6,8]{1,0:T(8,128)S(1)} %bitcast.38, s32[6,8]{1,0:T(8,128)S(1)} %bitcast.40, s32[6,6]{1,0:T(8,128)S(1)} %bitcast.39, bf16[2,16,128]{2,1,0:T(8,128)(2,1)S(1)} %pad.4.refs_0_.notes, ...), custom_call_target="tpu_custom_call" | custom-call | flops 1000000000 | bytes 1024 | tf_op jit(solution)/shard_map/make_plan/pallas_call | solution.py:175
  52.8 3.3 %collective-permute-start.19 = (bf16[960,128]{1,0:T(8,128)(2,1)S(1)}, bf16[960,128]{1,0:T(8,128)(2,1)S(1)}, u32[]{:S(2)}, u32[]{:S(2)}) collective-permute-start(bf16[960,128]{1,0:T(8,128)(2,1)S(1)} %lane0_8.1.refs_1_), channel_id=1, source_target_pairs={{0,1},{3,2},{2,3},{1,0},{4,5},{7,6},{6,7},{5,4},{8,9},{11,10},{10,... | collective-permute-start | bytes 737288 | tf_op jit(solution)/shard_map/ppermute | solution.py:351
  58.2 5.2 %collective-permute-start.17 = (bf16[960,128]{1,0:T(8,128)(2,1)S(1)}, bf16[960,128]{1,0:T(8,128)(2,1)S(1)}, u32[]{:S(2)}, u32[]{:S(2)}) collective-permute-start(bf16[960,128]{1,0:T(8,128)(2,1)S(1)} %lane0_9.1.refs_1_), channel_id=1, source_target_pairs={{0,1},{3,2},{2,3},{1,0},{4,5},{7,6},{6,7},{5,4},{8,9},{11,10},{10,... | collective-permute-start | bytes 737288 | tf_op jit(solution)/shard_map/ppermute | solution.py:351
  64.1 2.9 %collective-permute-start.20 = (bf16[960,128]{1,0:T(8,128)(2,1)S(1)}, bf16[960,128]{1,0:T(8,128)(2,1)S(1)}, u32[]{:S(2)}, u32[]{:S(2)}) collective-permute-start(bf16[960,128]{1,0:T(8,128)(2,1)S(1)} %lane0_10.1), channel_id=1, source_target_pairs={{0,1},{3,2},{2,3},{1,0},{4,5},{7,6},{6,7},{5,4},{8,9},{11,10},{10,... | collective-permute-start | bytes 737288 | tf_op jit(solution)/shard_map/ppermute | solution.py:351
  67.1 5.1 %multiply_rows.3.refs_6_ = bf16[6,6,128,128]{3,2,1,0:T(8,128)(2,1)} custom-call(s32[8,8]{1,0:T(8,128)S(1)} %copy-done.2, s32[16,128]{1,0:T(8,128)S(1)} %make_plan.1.refs_3_.plan, bf16[6,8,128,128]{3,2,1,0:T(8,128)(2,1)S(1)} %bitcast.35, bf16[6,8,128,128]{3,2,1,0:T(8,128)(2,1)S(1)} %collective-permute-done.13.refs_2_.b1, ...), custom_call_target="tpu_custom_call" | custom-call | flops 2013265920 | bytes 4194304 | tf_op jit(solution)/shard_map/multiply_rows/pallas_call | solution.py:277
  72.2 2.4 %multiply_rows.4.refs_6_ = bf16[6,6,128,128]{3,2,1,0:T(8,128)(2,1)} custom-call(s32[8,8]{1,0:T(8,128)S(1)} %copy-done.2, s32[16,128]{1,0:T(8,128)S(1)} %make_plan.1.refs_3_.plan, bf16[6,8,128,128]{3,2,1,0:T(8,128)(2,1)S(1)} %bitcast.36, bf16[6,8,128,128]{3,2,1,0:T(8,128)(2,1)S(1)} %collective-permute-done.13.refs_2_.b1, ...), custom_call_target="tpu_custom_call", output_to_operand_aliasing={{}: (11, {})} | custom-call | flops 503316480 | bytes 4194304 | tf_op jit(solution)/shard_map/multiply_rows/pallas_call | solution.py:277
  74.6 2.4 %multiply_rows.5 = bf16[6,6,128,128]{3,2,1,0:T(8,128)(2,1)} custom-call(s32[8,8]{1,0:T(8,128)S(1)} %copy-done.2, s32[16,128]{1,0:T(8,128)S(1)} %make_plan.1.refs_3_.plan, bf16[6,8,128,128]{3,2,1,0:T(8,128)(2,1)S(1)} %bitcast.37, bf16[6,8,128,128]{3,2,1,0:T(8,128)(2,1)S(1)} %collective-permute-done.13.refs_2_.b1, ...), custom_call_target="tpu_custom_call", output_to_operand_aliasing={{}: (11, {})} | custom-call | flops 503316480 | bytes 4194304 | tf_op jit(solution)/shard_map/multiply_rows/pallas_call | solution.py:277
  (61 shorter events, 14.5 us)
Async XLA Ops:
  0.0 4.8 %copy-start = (bf16[1,1,2,6,5,128,128]{6,5,4,3,2,1,0:T(8,128)(2,1)S(1)}, bf16[1,1,2,6,5,128,128]{6,5,4,3,2,1,0:T(8,128)(2,1)}, u32[]{:S(2)}) copy-start(bf16[1,1,2,6,5,128,128]{6,5,4,3,2,1,0:T(8,128)(2,1)} %param.7) | copy-start | bytes 5898244
  0.0 4.8 %copy-start.2 = (s32[8,8]{1,0:T(8,128)S(1)}, s32[8,8]{1,0:T(8,128)}, u32[]{:S(2)}) copy-start(s32[8,8]{1,0:T(8,128)} %owner.45) | copy-start | bytes 772
  2.6 9.1 %collective-permute-start.2 = (bf16[960,128]{1,0:T(8,128)(2,1)}, bf16[960,128]{1,0:T(8,128)(2,1)S(1)}, u32[]{:S(2)}, u32[]{:S(2)}) collective-permute-start(bf16[960,128]{1,0:T(8,128)(2,1)} %lane0_0.1), channel_id=1, source_target_pairs={{0,1},{3,2},{2,3},{1,0},{4,5},{7,6},{6,7},{5,4},{8,9},{11,10},{10,... | collective-permute-start | bytes 737288 | tf_op jit(solution)/shard_map/ppermute | solution.py:351
  5.9 3.0 %collective-permute-start = (s32[1,1,6,8]{3,2,1,0:T(8,128)S(1)}, s32[1,1,6,8]{3,2,1,0:T(8,128)S(1)}, u32[]{:S(2)}, u32[]{:S(2)}) collective-permute-start(s32[1,1,6,8]{3,2,1,0:T(8,128)S(1)} %copy.11), channel_id=1, source_target_pairs={{4,0},{8,4},{12,8},{16,12},{20,16},{24,20},{28,24},{0,28},{5,1},{9... | collective-permute-start | bytes 584 | tf_op jit(solution)/shard_map/ppermute | solution.py:345
  7.6 11.6 %collective-permute-start.1 = (bf16[992,128]{1,0:T(8,128)(2,1)S(1)}, bf16[992,128]{1,0:T(8,128)(2,1)S(1)}, u32[]{:S(2)}, u32[]{:S(2)}) collective-permute-start(bf16[992,128]{1,0:T(8,128)(2,1)S(1)} %lane0_1.1), channel_id=1, source_target_pairs={{0,1},{3,2},{2,3},{1,0},{4,5},{7,6},{6,7},{5,4},{8,9},{11,10},{10,... | collective-permute-start | bytes 761864 | tf_op jit(solution)/shard_map/ppermute | solution.py:351
  8.9 47.2 %collective-permute-start.13 = (bf16[6,8,128,128]{3,2,1,0:T(8,128)(2,1)S(1)}, bf16[6,8,128,128]{3,2,1,0:T(8,128)(2,1)S(1)}, u32[]{:S(2)}, u32[]{:S(2)}) collective-permute-start(bf16[6,8,128,128]{3,2,1,0:T(8,128)(2,1)S(1)} %bitcast.34), channel_id=1, source_target_pairs={{4,0},{8,4},{12,8},{16,12},{20,16},{24,20},{28,24},{0,28},{5,1},{9... | collective-permute-start | bytes 4718600 | tf_op jit(solution)/shard_map/ppermute | solution.py:347
  12.4 8.2 %collective-permute-start.5 = (bf16[960,128]{1,0:T(8,128)(2,1)S(1)}, bf16[960,128]{1,0:T(8,128)(2,1)S(1)}, u32[]{:S(2)}, u32[]{:S(2)}) collective-permute-start(bf16[960,128]{1,0:T(8,128)(2,1)S(1)} %lane1_1.1.refs_0_), channel_id=1, source_target_pairs={{1,2},{2,1},{5,6},{6,5},{9,10},{10,9},{13,14},{14,13},{17,18},{18,... | collective-permute-start | bytes 737288 | tf_op jit(solution)/shard_map/ppermute | solution.py:351
  14.0 10.2 %collective-permute-start.4 = (bf16[960,128]{1,0:T(8,128)(2,1)S(1)}, bf16[960,128]{1,0:T(8,128)(2,1)S(1)}, u32[]{:S(2)}, u32[]{:S(2)}) collective-permute-start(bf16[960,128]{1,0:T(8,128)(2,1)S(1)} %lane0_2.1.refs_2_), channel_id=1, source_target_pairs={{0,1},{3,2},{2,3},{1,0},{4,5},{7,6},{6,7},{5,4},{8,9},{11,10},{10,... | collective-permute-start | bytes 737288 | tf_op jit(solution)/shard_map/ppermute | solution.py:351
  19.9 5.8 %collective-permute-start.3 = (bf16[992,128]{1,0:T(8,128)(2,1)S(1)}, bf16[992,128]{1,0:T(8,128)(2,1)S(1)}, u32[]{:S(2)}, u32[]{:S(2)}) collective-permute-start(bf16[992,128]{1,0:T(8,128)(2,1)S(1)} %lane1_2.1.refs_1_), channel_id=1, source_target_pairs={{1,2},{2,1},{5,6},{6,5},{9,10},{10,9},{13,14},{14,13},{17,18},{18,... | collective-permute-start | bytes 761864 | tf_op jit(solution)/shard_map/ppermute | solution.py:351
  21.6 8.9 %collective-permute-start.7 = (bf16[960,128]{1,0:T(8,128)(2,1)S(1)}, bf16[960,128]{1,0:T(8,128)(2,1)S(1)}, u32[]{:S(2)}, u32[]{:S(2)}) collective-permute-start(bf16[960,128]{1,0:T(8,128)(2,1)S(1)} %lane0_3.1.refs_1_), channel_id=1, source_target_pairs={{0,1},{3,2},{2,3},{1,0},{4,5},{7,6},{6,7},{5,4},{8,9},{11,10},{10,... | collective-permute-start | bytes 737288 | tf_op jit(solution)/shard_map/ppermute | solution.py:351
  25.0 6.9 %collective-permute-start.9 = (bf16[960,128]{1,0:T(8,128)(2,1)S(1)}, bf16[960,128]{1,0:T(8,128)(2,1)S(1)}, u32[]{:S(2)}, u32[]{:S(2)}) collective-permute-start(bf16[960,128]{1,0:T(8,128)(2,1)S(1)} %lane1_3.1.refs_2_), channel_id=1, source_target_pairs={{1,2},{2,1},{5,6},{6,5},{9,10},{10,9},{13,14},{14,13},{17,18},{18,... | collective-permute-start | bytes 737288 | tf_op jit(solution)/shard_map/ppermute | solution.py:351
  26.7 9.7 %collective-permute-start.6 = (bf16[992,128]{1,0:T(8,128)(2,1)S(1)}, bf16[992,128]{1,0:T(8,128)(2,1)S(1)}, u32[]{:S(2)}, u32[]{:S(2)}) collective-permute-start(bf16[992,128]{1,0:T(8,128)(2,1)S(1)} %lane0_4.1.refs_1_), channel_id=1, source_target_pairs={{0,1},{3,2},{2,3},{1,0},{4,5},{7,6},{6,7},{5,4},{8,9},{11,10},{10,... | collective-permute-start | bytes 761864 | tf_op jit(solution)/shard_map/ppermute | solution.py:351
  31.2 6.6 %collective-permute-start.8 = (bf16[960,128]{1,0:T(8,128)(2,1)S(1)}, bf16[960,128]{1,0:T(8,128)(2,1)S(1)}, u32[]{:S(2)}, u32[]{:S(2)}) collective-permute-start(bf16[960,128]{1,0:T(8,128)(2,1)S(1)} %lane1_4.1.refs_1_), channel_id=1, source_target_pairs={{1,2},{2,1},{5,6},{6,5},{9,10},{10,9},{13,14},{14,13},{17,18},{18,... | collective-permute-start | bytes 737288 | tf_op jit(solution)/shard_map/ppermute | solution.py:351
  32.9 11.2 %collective-permute-start.12 = (bf16[960,128]{1,0:T(8,128)(2,1)S(1)}, bf16[960,128]{1,0:T(8,128)(2,1)S(1)}, u32[]{:S(2)}, u32[]{:S(2)}) collective-permute-start(bf16[960,128]{1,0:T(8,128)(2,1)S(1)} %lane0_5.1.refs_1_), channel_id=1, source_target_pairs={{0,1},{3,2},{2,3},{1,0},{4,5},{7,6},{6,7},{5,4},{8,9},{11,10},{10,... | collective-permute-start | bytes 737288 | tf_op jit(solution)/shard_map/ppermute | solution.py:351
  37.1 7.0 %copy-start.6 = (s32[1,1,6,6]{3,1,2,0:T(1,128)S(1)}, s32[1,1,6,6]{3,1,2,0:T(1,128)}, u32[]{:S(2)}) copy-start(s32[1,1,6,6]{3,1,2,0:T(1,128)} %param.11) | copy-start | bytes 436
  37.1 8.4 %collective-permute-start.11 = (bf16[960,128]{1,0:T(8,128)(2,1)S(1)}, bf16[960,128]{1,0:T(8,128)(2,1)S(1)}, u32[]{:S(2)}, u32[]{:S(2)}) collective-permute-start(bf16[960,128]{1,0:T(8,128)(2,1)S(1)} %lane1_5.1.refs_1_), channel_id=1, source_target_pairs={{1,2},{2,1},{5,6},{6,5},{9,10},{10,9},{13,14},{14,13},{17,18},{18,... | collective-permute-start | bytes 737288 | tf_op jit(solution)/shard_map/ppermute | solution.py:351
  38.8 10.8 %collective-permute-start.10 = (bf16[960,128]{1,0:T(8,128)(2,1)S(1)}, bf16[960,128]{1,0:T(8,128)(2,1)S(1)}, u32[]{:S(2)}, u32[]{:S(2)}) collective-permute-start(bf16[960,128]{1,0:T(8,128)(2,1)S(1)} %lane0_6.1.refs_1_), channel_id=1, source_target_pairs={{0,1},{3,2},{2,3},{1,0},{4,5},{7,6},{6,7},{5,4},{8,9},{11,10},{10,... | collective-permute-start | bytes 737288 | tf_op jit(solution)/shard_map/ppermute | solution.py:351
  44.8 7.3 %collective-permute-start.16 = (bf16[960,128]{1,0:T(8,128)(2,1)S(1)}, bf16[960,128]{1,0:T(8,128)(2,1)S(1)}, u32[]{:S(2)}, u32[]{:S(2)}) collective-permute-start(bf16[960,128]{1,0:T(8,128)(2,1)S(1)} %lane1_6.1.refs_1_), channel_id=1, source_target_pairs={{1,2},{2,1},{5,6},{6,5},{9,10},{10,9},{13,14},{14,13},{17,18},{18,... | collective-permute-start | bytes 737288 | tf_op jit(solution)/shard_map/ppermute | solution.py:351
  46.5 9.7 %collective-permute-start.15 = (bf16[960,128]{1,0:T(8,128)(2,1)S(1)}, bf16[960,128]{1,0:T(8,128)(2,1)S(1)}, u32[]{:S(2)}, u32[]{:S(2)}) collective-permute-start(bf16[960,128]{1,0:T(8,128)(2,1)S(1)} %lane0_7.1.refs_1_), channel_id=1, source_target_pairs={{0,1},{3,2},{2,3},{1,0},{4,5},{7,6},{6,7},{5,4},{8,9},{11,10},{10,... | collective-permute-start | bytes 737288 | tf_op jit(solution)/shard_map/ppermute | solution.py:351
  50.3 7.2 %collective-permute-start.14 = (bf16[960,128]{1,0:T(8,128)(2,1)S(1)}, bf16[960,128]{1,0:T(8,128)(2,1)S(1)}, u32[]{:S(2)}, u32[]{:S(2)}) collective-permute-start(bf16[960,128]{1,0:T(8,128)(2,1)S(1)} %lane1_7.1.refs_3_.refs_1_), channel_id=1, source_target_pairs={{1,2},{2,1},{5,6},{6,5},{9,10},{10,9},{13,14},{14,13},{17,18},{18,... | collective-permute-start | bytes 737288 | tf_op jit(solution)/shard_map/ppermute | solution.py:351
  52.8 10.6 %collective-permute-start.19 = (bf16[960,128]{1,0:T(8,128)(2,1)S(1)}, bf16[960,128]{1,0:T(8,128)(2,1)S(1)}, u32[]{:S(2)}, u32[]{:S(2)}) collective-permute-start(bf16[960,128]{1,0:T(8,128)(2,1)S(1)} %lane0_8.1.refs_1_), channel_id=1, source_target_pairs={{0,1},{3,2},{2,3},{1,0},{4,5},{7,6},{6,7},{5,4},{8,9},{11,10},{10,... | collective-permute-start | bytes 737288 | tf_op jit(solution)/shard_map/ppermute | solution.py:351
  56.8 6.6 %collective-permute-start.18 = (bf16[960,128]{1,0:T(8,128)(2,1)S(1)}, bf16[960,128]{1,0:T(8,128)(2,1)S(1)}, u32[]{:S(2)}, u32[]{:S(2)}) collective-permute-start(bf16[960,128]{1,0:T(8,128)(2,1)S(1)} %lane1_8.1.refs_1_), channel_id=1, source_target_pairs={{1,2},{2,1},{5,6},{6,5},{9,10},{10,9},{13,14},{14,13},{17,18},{18,... | collective-permute-start | bytes 737288 | tf_op jit(solution)/shard_map/ppermute | solution.py:351
  58.2 14.0 %collective-permute-start.17 = (bf16[960,128]{1,0:T(8,128)(2,1)S(1)}, bf16[960,128]{1,0:T(8,128)(2,1)S(1)}, u32[]{:S(2)}, u32[]{:S(2)}) collective-permute-start(bf16[960,128]{1,0:T(8,128)(2,1)S(1)} %lane0_9.1.refs_1_), channel_id=1, source_target_pairs={{0,1},{3,2},{2,3},{1,0},{4,5},{7,6},{6,7},{5,4},{8,9},{11,10},{10,... | collective-permute-start | bytes 737288 | tf_op jit(solution)/shard_map/ppermute | solution.py:351
  64.1 10.5 %collective-permute-start.20 = (bf16[960,128]{1,0:T(8,128)(2,1)S(1)}, bf16[960,128]{1,0:T(8,128)(2,1)S(1)}, u32[]{:S(2)}, u32[]{:S(2)}) collective-permute-start(bf16[960,128]{1,0:T(8,128)(2,1)S(1)} %lane0_10.1), channel_id=1, source_target_pairs={{0,1},{3,2},{2,3},{1,0},{4,5},{7,6},{6,7},{5,4},{8,9},{11,10},{10,... | collective-permute-start | bytes 737288 | tf_op jit(solution)/shard_map/ppermute | solution.py:351
  (4 other events, 14.4 us)

commit v4 on v3

--- a/solution.py
+++ b/solution.py
@@ -8,7 +8,7 @@
 from jax.sharding import PartitionSpec as P
 
 STEPS = 2
-SHARES = (1, 1, 1, 1, 1, 1, 1, 1)
+SHARES = (16, 21, 21, 22, 20, 20)
 PIECES = len(SHARES)
 NOTED = 1
 NOTE = 16

time: 78.1 us -> 74.1 us (0.949); the launches traced: 77 us -> 74 us
  Pallas kernels: 28.1 us -> 24.4 us
  waiting for transfers between devices: 0.44 us -> 4 us
  starting transfers between devices: 47.9 us -> 45.1 us
    ppermute x19 -> x15, waiting for transfers between devices: 0.18 us -> 3.62 us  [local(): got = lax.ppermute(newest, 'col', route)]
    ppermute x19 -> x15, starting transfers between devices: 43.6 us -> 40.8 us  [local(): got = lax.ppermute(newest, 'col', route)]
    pallas_call x19 -> x15, Pallas kernels: 17.2 us -> 14.7 us  [relay(): pl.pallas_call(functools.partial(relay_kernel, roles, len(after)), out_sh...]
    pallas_call x3, Pallas kernels: 9.85 us -> 8.6 us  [multiply_rows(): pl.pallas_call(functools.partial(rows_kernel, first, count, hops, tuple(s...]
  transfers between devices with their start and end apart: 21 -> 17, of which waited for: 2 -> 4; matrix products, arithmetic and copies ran while one was open for 0% -> 0% of each run, Pallas kernels for 30% -> 27%
where the time goes in v4:
time: 74.1 us; the launch traced here: 74 us
  starting transfers between devices  45.1 us (61%)
  Pallas kernels  24.4 us (33%)
  waiting for transfers between devices  4 us (5%)
    ppermute x15, starting transfers between devices, local(): got = lax.ppermute(newest, 'col', route)  40.8 us
    pallas_call x15, Pallas kernels, relay(): pl.pallas_call(functools.partial(relay_kernel, roles, len(after)), out_sh...  14.7 us
    pallas_call x3, Pallas kernels, multiply_rows(): pl.pallas_call(functools.partial(rows_kernel, first, count, hops, tuple(s...  8.6 us
    ppermute x15, waiting for transfers between devices, local(): got = lax.ppermute(newest, 'col', route)  3.62 us
    ppermute x1, starting transfers between devices, local(): moved_b = lax.ppermute(behind_b, 'row', from_next)  2.6 us
    ppermute x1, starting transfers between devices, local(): moved_bc = lax.ppermute(behind_bc, 'row', from_next)  1.66 us
  transfers between devices with their start and end apart: 17, of which 4 were waited for; matrix products, arithmetic and copies ran while one was open for 0% of the time, Pallas kernels for 27%

profile of v4, /device:TPU:0, one launch (start us, length us, event | category | flops | bytes accessed | tf_op | source)
XLA Modules:
  0.0 74.0 jit_solution(17941442189318233254)
XLA Ops:
  0.0 2.6 %lane0_0.1 = bf16[1024,128]{1,0:T(8,128)(2,1)} custom-call(s32[8,8]{1,0:T(8,128)} %owner.37, bf16[2,6,640,128]{3,2,1,0:T(8,128)(2,1)} %bitcast.12), custom_call_target="tpu_custom_call" | custom-call | flops 1000000000 | bytes 1024 | tf_op jit(solution)/shard_map/lane0_0/pallas_call | solution.py:93
  2.6 2.1 %collective-permute-start.2 = (bf16[1024,128]{1,0:T(8,128)(2,1)}, bf16[1024,128]{1,0:T(8,128)(2,1)S(1)}, u32[]{:S(2)}, u32[]{:S(2)}) collective-permute-start(bf16[1024,128]{1,0:T(8,128)(2,1)} %lane0_0.1), channel_id=1, source_target_pairs={{0,1},{3,2},{2,3},{1,0},{4,5},{7,6},{6,7},{5,4},{8,9},{11,10},{10,... | collective-permute-start | bytes 786440 | tf_op jit(solution)/shard_map/ppermute | solution.py:351
  4.9 1.2 %lane0_1.1 = bf16[1376,128]{1,0:T(8,128)(2,1)S(1)} custom-call(s32[8,8]{1,0:T(8,128)S(1)} %copy-done.2, bf16[2,6,640,128]{3,2,1,0:T(8,128)(2,1)S(1)} %bitcast.13, bf16[2,16,128]{2,1,0:T(8,128)(2,1)S(1)} %pad.4.refs_0_.notes), custom_call_target="tpu_custom_call" | custom-call | flops 1000000000 | bytes 1024 | tf_op jit(solution)/shard_map/lane0_1/pallas_call | solution.py:93
  6.1 1.7 %collective-permute-start = (s32[1,1,6,8]{3,2,1,0:T(8,128)S(1)}, s32[1,1,6,8]{3,2,1,0:T(8,128)S(1)}, u32[]{:S(2)}, u32[]{:S(2)}) collective-permute-start(s32[1,1,6,8]{3,2,1,0:T(8,128)S(1)} %copy.11), channel_id=1, source_target_pairs={{4,0},{8,4},{12,8},{16,12},{20,16},{24,20},{28,24},{0,28},{5,1},{9... | collective-permute-start | bytes 584 | tf_op jit(solution)/shard_map/ppermute | solution.py:345
  7.8 0.9 %collective-permute-start.1 = (bf16[1376,128]{1,0:T(8,128)(2,1)S(1)}, bf16[1376,128]{1,0:T(8,128)(2,1)S(1)}, u32[]{:S(2)}, u32[]{:S(2)}) collective-permute-start(bf16[1376,128]{1,0:T(8,128)(2,1)S(1)} %lane0_1.1), channel_id=1, source_target_pairs={{0,1},{3,2},{2,3},{1,0},{4,5},{7,6},{6,7},{5,4},{8,9},{11,10},{10,... | collective-permute-start | bytes 1056776 | tf_op jit(solution)/shard_map/ppermute | solution.py:351
  9.1 2.6 %collective-permute-start.9 = (bf16[6,8,128,128]{3,2,1,0:T(8,128)(2,1)S(1)}, bf16[6,8,128,128]{3,2,1,0:T(8,128)(2,1)S(1)}, u32[]{:S(2)}, u32[]{:S(2)}) collective-permute-start(bf16[6,8,128,128]{3,2,1,0:T(8,128)(2,1)S(1)} %bitcast.30), channel_id=1, source_target_pairs={{4,0},{8,4},{12,8},{16,12},{20,16},{24,20},{28,24},{0,28},{5,1},{9... | collective-permute-start | bytes 4718600 | tf_op jit(solution)/shard_map/ppermute | solution.py:347
  13.4 1.1 %lane0_2.1.refs_2_ = bf16[1344,128]{1,0:T(8,128)(2,1)S(1)} custom-call(s32[8,8]{1,0:T(8,128)S(1)} %copy-done.2, bf16[2,6,640,128]{3,2,1,0:T(8,128)(2,1)S(1)} %bitcast.15, bf16[1024,128]{1,0:T(8,128)(2,1)S(1)} %lane1_1.1.refs_0_), custom_call_target="tpu_custom_call" | custom-call | flops 3000000000 | bytes 1024 | tf_op jit(solution)/shard_map/lane0_2/pallas_call | solution.py:93
  14.5 5.2 %collective-permute-start.4 = (bf16[1344,128]{1,0:T(8,128)(2,1)S(1)}, bf16[1344,128]{1,0:T(8,128)(2,1)S(1)}, u32[]{:S(2)}, u32[]{:S(2)}) collective-permute-start(bf16[1344,128]{1,0:T(8,128)(2,1)S(1)} %lane0_2.1.refs_2_), channel_id=1, source_target_pairs={{0,1},{3,2},{2,3},{1,0},{4,5},{7,6},{6,7},{5,4},{8,9},{11,10},{10,... | collective-permute-start | bytes 1032200 | tf_op jit(solution)/shard_map/ppermute | solution.py:351
  19.8 0.8 %lane1_2.1.refs_1_ = bf16[1376,128]{1,0:T(8,128)(2,1)S(1)} custom-call(s32[8,8]{1,0:T(8,128)S(1)} %copy-done.2, bf16[2,6,640,128]{3,2,1,0:T(8,128)(2,1)S(1)} %bitcast.16, bf16[2,16,128]{2,1,0:T(8,128)(2,1)S(1)} %pad.4.refs_0_.notes, bf16[1376,128]{1,0:T(8,128)(2,1)S(1)} %collective-permute-done.1.refs_1_.refs_2_.refs_0_.refs_3_, ...), custom_call_target="tpu_custom_call" | custom-call | flops 2000000000 | bytes 1024 | tf_op jit(solution)/shard_map/lane1_2/pallas_call | solution.py:93
  21.2 1.2 %lane0_3.1.refs_1_ = bf16[1408,128]{1,0:T(8,128)(2,1)S(1)} custom-call(s32[8,8]{1,0:T(8,128)S(1)} %copy-done.2, bf16[2,6,640,128]{3,2,1,0:T(8,128)(2,1)S(1)} %bitcast.17, bf16[1024,128]{1,0:T(8,128)(2,1)S(1)} %collective-permute-done.5.refs_0_.refs_1_, bf16[1376,128]{1,0:T(8,128)(2,1)S(1)} %lane1_2.1.refs_1_, ...), custom_call_target="tpu_custom_call" | custom-call | flops 1000000000 | bytes 1024 | tf_op jit(solution)/shard_map/lane0_3/pallas_call | solution.py:93
  22.4 5.2 %collective-permute-start.8 = (bf16[1408,128]{1,0:T(8,128)(2,1)S(1)}, bf16[1408,128]{1,0:T(8,128)(2,1)S(1)}, u32[]{:S(2)}, u32[]{:S(2)}) collective-permute-start(bf16[1408,128]{1,0:T(8,128)(2,1)S(1)} %lane0_3.1.refs_1_), channel_id=1, source_target_pairs={{0,1},{3,2},{2,3},{1,0},{4,5},{7,6},{6,7},{5,4},{8,9},{11,10},{10,... | collective-permute-start | bytes 1081352 | tf_op jit(solution)/shard_map/ppermute | solution.py:351
  29.0 1.2 %lane0_4.1.refs_1_ = bf16[1376,128]{1,0:T(8,128)(2,1)S(1)} custom-call(s32[8,8]{1,0:T(8,128)S(1)} %copy-done.2, bf16[2,6,640,128]{3,2,1,0:T(8,128)(2,1)S(1)} %bitcast.19, bf16[2,16,128]{2,1,0:T(8,128)(2,1)S(1)} %pad.4.refs_0_.notes, bf16[1376,128]{1,0:T(8,128)(2,1)S(1)} %collective-permute-done.3.refs_1_.refs_4_, bf16[1344,128]{1,0:T(8,128)(2,1)S(1)} %lane1_3.1.refs_2_, ...), custom_call_target="tpu_custom_call" | custom-call | flops 1000000000 | bytes 1024 | tf_op jit(solution)/shard_map/lane0_4/pallas_call | solution.py:93
  30.2 4.9 %collective-permute-start.6 = (bf16[1376,128]{1,0:T(8,128)(2,1)S(1)}, bf16[1376,128]{1,0:T(8,128)(2,1)S(1)}, u32[]{:S(2)}, u32[]{:S(2)}) collective-permute-start(bf16[1376,128]{1,0:T(8,128)(2,1)S(1)} %lane0_4.1.refs_1_), channel_id=1, source_target_pairs={{0,1},{3,2},{2,3},{1,0},{4,5},{7,6},{6,7},{5,4},{8,9},{11,10},{10,... | collective-permute-start | bytes 1056776 | tf_op jit(solution)/shard_map/ppermute | solution.py:351
  36.5 1.1 %lane0_5.1.refs_1_ = bf16[1344,128]{1,0:T(8,128)(2,1)S(1)} custom-call(s32[8,8]{1,0:T(8,128)S(1)} %copy-done.2, bf16[2,6,640,128]{3,2,1,0:T(8,128)(2,1)S(1)} %bitcast.21, bf16[1344,128]{1,0:T(8,128)(2,1)S(1)} %collective-permute-done.7.refs_0_.refs_7_, bf16[1408,128]{1,0:T(8,128)(2,1)S(1)} %lane1_4.1.refs_1_, ...), custom_call_target="tpu_custom_call" | custom-call | flops 1000000000 | bytes 1024 | tf_op jit(solution)/shard_map/lane0_5/pallas_call | solution.py:93
  37.6 5.3 %collective-permute-start.10 = (bf16[1344,128]{1,0:T(8,128)(2,1)S(1)}, bf16[1344,128]{1,0:T(8,128)(2,1)S(1)}, u32[]{:S(2)}, u32[]{:S(2)}) collective-permute-start(bf16[1344,128]{1,0:T(8,128)(2,1)S(1)} %lane0_5.1.refs_1_), channel_id=1, source_target_pairs={{0,1},{3,2},{2,3},{1,0},{4,5},{7,6},{6,7},{5,4},{8,9},{11,10},{10,... | collective-permute-start | bytes 1032200 | tf_op jit(solution)/shard_map/ppermute | solution.py:351
  44.3 1.1 %make_plan.1.refs_3_.plan = s32[16,128]{1,0:T(8,128)S(1)} custom-call(s32[8,8]{1,0:T(8,128)S(1)} %copy-done.2, s32[48]{0:T(128)S(1)} %copy-done.3, s32[6,8]{1,0:T(8,128)S(1)} %bitcast.34, s32[6,8]{1,0:T(8,128)S(1)} %bitcast.36, s32[6,6]{1,0:T(8,128)S(1)} %bitcast.35, bf16[2,16,128]{2,1,0:T(8,128)(2,1)S(1)} %pad.4.refs_0_.notes, ...), custom_call_target="tpu_custom_call" | custom-call | flops 1000000000 | bytes 1024 | tf_op jit(solution)/shard_map/make_plan/pallas_call | solution.py:175
  46.1 6.2 %collective-permute-start.14 = (bf16[1408,128]{1,0:T(8,128)(2,1)S(1)}, bf16[1408,128]{1,0:T(8,128)(2,1)S(1)}, u32[]{:S(2)}, u32[]{:S(2)}) collective-permute-start(bf16[1408,128]{1,0:T(8,128)(2,1)S(1)} %lane0_6.1.refs_1_), channel_id=1, source_target_pairs={{0,1},{3,2},{2,3},{1,0},{4,5},{7,6},{6,7},{5,4},{8,9},{11,10},{10,... | collective-permute-start | bytes 1081352 | tf_op jit(solution)/shard_map/ppermute | solution.py:351
  54.4 4.1 %collective-permute-start.16 = (bf16[1280,128]{1,0:T(8,128)(2,1)S(1)}, bf16[1280,128]{1,0:T(8,128)(2,1)S(1)}, u32[]{:S(2)}, u32[]{:S(2)}) collective-permute-start(bf16[1280,128]{1,0:T(8,128)(2,1)S(1)} %lane0_7.1.refs_1_), channel_id=1, source_target_pairs={{0,1},{3,2},{2,3},{1,0},{4,5},{7,6},{6,7},{5,4},{8,9},{11,10},{10,... | collective-permute-start | bytes 983048 | tf_op jit(solution)/shard_map/ppermute | solution.py:351
  58.6 1.5 %collective-permute-done.14.refs_2_.refs_11_ = bf16[1408,128]{1,0:T(8,128)(2,1)S(1)} collective-permute-done((bf16[1408,128]{1,0:T(8,128)(2,1)S(1)}, bf16[1408,128]{1,0:T(8,128)(2,1)S(1)}, u32[]{:S(2)}, u32[]{:S(2)}) %collective-permute-start.14) | collective-permute-done | bytes 360480 | tf_op jit(solution)/shard_map/ppermute | solution.py:351
  60.8 2.8 %collective-permute-start.15 = (bf16[1280,128]{1,0:T(8,128)(2,1)S(1)}, bf16[1280,128]{1,0:T(8,128)(2,1)S(1)}, u32[]{:S(2)}, u32[]{:S(2)}) collective-permute-start(bf16[1280,128]{1,0:T(8,128)(2,1)S(1)} %lane0_8.1), channel_id=1, source_target_pairs={{0,1},{3,2},{2,3},{1,0},{4,5},{7,6},{6,7},{5,4},{8,9},{11,10},{10,... | collective-permute-start | bytes 983048 | tf_op jit(solution)/shard_map/ppermute | solution.py:351
  63.6 4.3 %multiply_rows.3.refs_3_ = bf16[6,6,128,128]{3,2,1,0:T(8,128)(2,1)} custom-call(s32[8,8]{1,0:T(8,128)S(1)} %copy-done.2, s32[16,128]{1,0:T(8,128)S(1)} %make_plan.1.refs_3_.plan, bf16[6,8,128,128]{3,2,1,0:T(8,128)(2,1)S(1)} %bitcast.31, bf16[6,8,128,128]{3,2,1,0:T(8,128)(2,1)S(1)} %collective-permute-done.9.refs_2_.b1, ...), custom_call_target="tpu_custom_call" | custom-call | flops 2013265920 | bytes 4194304 | tf_op jit(solution)/shard_map/multiply_rows/pallas_call | solution.py:277
  67.9 2.2 %multiply_rows.4.refs_3_ = bf16[6,6,128,128]{3,2,1,0:T(8,128)(2,1)} custom-call(s32[8,8]{1,0:T(8,128)S(1)} %copy-done.2, s32[16,128]{1,0:T(8,128)S(1)} %make_plan.1.refs_3_.plan, bf16[6,8,128,128]{3,2,1,0:T(8,128)(2,1)S(1)} %bitcast.32, bf16[6,8,128,128]{3,2,1,0:T(8,128)(2,1)S(1)} %collective-permute-done.9.refs_2_.b1, ...), custom_call_target="tpu_custom_call", output_to_operand_aliasing={{}: (8, {})} | custom-call | flops 503316480 | bytes 4194304 | tf_op jit(solution)/shard_map/multiply_rows/pallas_call | solution.py:277
  70.1 1.7 %collective-permute-done.15.refs_2_ = bf16[1280,128]{1,0:T(8,128)(2,1)S(1)} collective-permute-done((bf16[1280,128]{1,0:T(8,128)(2,1)S(1)}, bf16[1280,128]{1,0:T(8,128)(2,1)S(1)}, u32[]{:S(2)}, u32[]{:S(2)}) %collective-permute-start.15) | collective-permute-done | bytes 327712 | tf_op jit(solution)/shard_map/ppermute | solution.py:351
  71.8 2.1 %multiply_rows.5 = bf16[6,6,128,128]{3,2,1,0:T(8,128)(2,1)} custom-call(s32[8,8]{1,0:T(8,128)S(1)} %copy-done.2, s32[16,128]{1,0:T(8,128)S(1)} %make_plan.1.refs_3_.plan, bf16[6,8,128,128]{3,2,1,0:T(8,128)(2,1)S(1)} %bitcast.33, bf16[6,8,128,128]{3,2,1,0:T(8,128)(2,1)S(1)} %collective-permute-done.9.refs_2_.b1, ...), custom_call_target="tpu_custom_call", output_to_operand_aliasing={{}: (8, {})} | custom-call | flops 503316480 | bytes 4194304 | tf_op jit(solution)/shard_map/multiply_rows/pallas_call | solution.py:277
  (49 shorter events, 10.5 us)
Async XLA Ops:
  0.0 4.7 %copy-start.5 = (s32[1,1,2,6,5]{3,2,4,1,0:T(2,128)S(1)}, s32[1,1,2,6,5]{3,2,4,1,0:T(2,128)}, u32[]{:S(2)}) copy-start(s32[1,1,2,6,5]{3,2,4,1,0:T(2,128)} %param.8) | copy-start | bytes 724
  0.0 4.9 %copy-start = (bf16[1,1,2,6,5,128,128]{6,5,4,3,2,1,0:T(8,128)(2,1)S(1)}, bf16[1,1,2,6,5,128,128]{6,5,4,3,2,1,0:T(8,128)(2,1)}, u32[]{:S(2)}) copy-start(bf16[1,1,2,6,5,128,128]{6,5,4,3,2,1,0:T(8,128)(2,1)} %param.7) | copy-start | bytes 5898244
  0.0 4.9 %copy-start.2 = (s32[8,8]{1,0:T(8,128)S(1)}, s32[8,8]{1,0:T(8,128)}, u32[]{:S(2)}) copy-start(s32[8,8]{1,0:T(8,128)} %owner.37) | copy-start | bytes 772
  2.6 9.4 %collective-permute-start.2 = (bf16[1024,128]{1,0:T(8,128)(2,1)}, bf16[1024,128]{1,0:T(8,128)(2,1)S(1)}, u32[]{:S(2)}, u32[]{:S(2)}) collective-permute-start(bf16[1024,128]{1,0:T(8,128)(2,1)} %lane0_0.1), channel_id=1, source_target_pairs={{0,1},{3,2},{2,3},{1,0},{4,5},{7,6},{6,7},{5,4},{8,9},{11,10},{10,... | collective-permute-start | bytes 786440 | tf_op jit(solution)/shard_map/ppermute | solution.py:351
  4.9 1.2 %copy-start.4 = (s32[1,1,6,8]{3,1,2,0:T(1,128)S(1)}, s32[1,1,6,8]{3,1,2,0:T(1,128)}, u32[]{:S(2)}) copy-start(s32[1,1,6,8]{3,1,2,0:T(1,128)} %param.10) | copy-start | bytes 580
  4.9 4.2 %copy-start.1 = (bf16[1,1,6,8,128,128]{5,4,3,2,1,0:T(8,128)(2,1)S(1)}, bf16[1,1,6,8,128,128]{5,4,3,2,1,0:T(8,128)(2,1)}, u32[]{:S(2)}) copy-start(bf16[1,1,6,8,128,128]{5,4,3,2,1,0:T(8,128)(2,1)} %param.9) | copy-start | bytes 4718596
  6.1 3.0 %collective-permute-start = (s32[1,1,6,8]{3,2,1,0:T(8,128)S(1)}, s32[1,1,6,8]{3,2,1,0:T(8,128)S(1)}, u32[]{:S(2)}, u32[]{:S(2)}) collective-permute-start(s32[1,1,6,8]{3,2,1,0:T(8,128)S(1)} %copy.11), channel_id=1, source_target_pairs={{4,0},{8,4},{12,8},{16,12},{20,16},{24,20},{28,24},{0,28},{5,1},{9... | collective-permute-start | bytes 584 | tf_op jit(solution)/shard_map/ppermute | solution.py:345
  7.8 12.0 %collective-permute-start.1 = (bf16[1376,128]{1,0:T(8,128)(2,1)S(1)}, bf16[1376,128]{1,0:T(8,128)(2,1)S(1)}, u32[]{:S(2)}, u32[]{:S(2)}) collective-permute-start(bf16[1376,128]{1,0:T(8,128)(2,1)S(1)} %lane0_1.1), channel_id=1, source_target_pairs={{0,1},{3,2},{2,3},{1,0},{4,5},{7,6},{6,7},{5,4},{8,9},{11,10},{10,... | collective-permute-start | bytes 1056776 | tf_op jit(solution)/shard_map/ppermute | solution.py:351
  9.1 43.3 %collective-permute-start.9 = (bf16[6,8,128,128]{3,2,1,0:T(8,128)(2,1)S(1)}, bf16[6,8,128,128]{3,2,1,0:T(8,128)(2,1)S(1)}, u32[]{:S(2)}, u32[]{:S(2)}) collective-permute-start(bf16[6,8,128,128]{3,2,1,0:T(8,128)(2,1)S(1)} %bitcast.30), channel_id=1, source_target_pairs={{4,0},{8,4},{12,8},{16,12},{20,16},{24,20},{28,24},{0,28},{5,1},{9... | collective-permute-start | bytes 4718600 | tf_op jit(solution)/shard_map/ppermute | solution.py:347
  12.7 8.5 %collective-permute-start.5 = (bf16[1024,128]{1,0:T(8,128)(2,1)S(1)}, bf16[1024,128]{1,0:T(8,128)(2,1)S(1)}, u32[]{:S(2)}, u32[]{:S(2)}) collective-permute-start(bf16[1024,128]{1,0:T(8,128)(2,1)S(1)} %lane1_1.1.refs_0_), channel_id=1, source_target_pairs={{1,2},{2,1},{5,6},{6,5},{9,10},{10,9},{13,14},{14,13},{17,18},{18,... | collective-permute-start | bytes 786440 | tf_op jit(solution)/shard_map/ppermute | solution.py:351
  14.5 13.0 %collective-permute-start.4 = (bf16[1344,128]{1,0:T(8,128)(2,1)S(1)}, bf16[1344,128]{1,0:T(8,128)(2,1)S(1)}, u32[]{:S(2)}, u32[]{:S(2)}) collective-permute-start(bf16[1344,128]{1,0:T(8,128)(2,1)S(1)} %lane0_2.1.refs_2_), channel_id=1, source_target_pairs={{0,1},{3,2},{2,3},{1,0},{4,5},{7,6},{6,7},{5,4},{8,9},{11,10},{10,... | collective-permute-start | bytes 1032200 | tf_op jit(solution)/shard_map/ppermute | solution.py:351
  20.5 8.4 %collective-permute-start.3 = (bf16[1376,128]{1,0:T(8,128)(2,1)S(1)}, bf16[1376,128]{1,0:T(8,128)(2,1)S(1)}, u32[]{:S(2)}, u32[]{:S(2)}) collective-permute-start(bf16[1376,128]{1,0:T(8,128)(2,1)S(1)} %lane1_2.1.refs_1_), channel_id=1, source_target_pairs={{1,2},{2,1},{5,6},{6,5},{9,10},{10,9},{13,14},{14,13},{17,18},{18,... | collective-permute-start | bytes 1056776 | tf_op jit(solution)/shard_map/ppermute | solution.py:351
  22.4 12.6 %collective-permute-start.8 = (bf16[1408,128]{1,0:T(8,128)(2,1)S(1)}, bf16[1408,128]{1,0:T(8,128)(2,1)S(1)}, u32[]{:S(2)}, u32[]{:S(2)}) collective-permute-start(bf16[1408,128]{1,0:T(8,128)(2,1)S(1)} %lane0_3.1.refs_1_), channel_id=1, source_target_pairs={{0,1},{3,2},{2,3},{1,0},{4,5},{7,6},{6,7},{5,4},{8,9},{11,10},{10,... | collective-permute-start | bytes 1081352 | tf_op jit(solution)/shard_map/ppermute | solution.py:351
  28.3 8.2 %collective-permute-start.7 = (bf16[1344,128]{1,0:T(8,128)(2,1)S(1)}, bf16[1344,128]{1,0:T(8,128)(2,1)S(1)}, u32[]{:S(2)}, u32[]{:S(2)}) collective-permute-start(bf16[1344,128]{1,0:T(8,128)(2,1)S(1)} %lane1_3.1.refs_2_), channel_id=1, source_target_pairs={{1,2},{2,1},{5,6},{6,5},{9,10},{10,9},{13,14},{14,13},{17,18},{18,... | collective-permute-start | bytes 1032200 | tf_op jit(solution)/shard_map/ppermute | solution.py:351
  30.2 12.7 %collective-permute-start.6 = (bf16[1376,128]{1,0:T(8,128)(2,1)S(1)}, bf16[1376,128]{1,0:T(8,128)(2,1)S(1)}, u32[]{:S(2)}, u32[]{:S(2)}) collective-permute-start(bf16[1376,128]{1,0:T(8,128)(2,1)S(1)} %lane0_4.1.refs_1_), channel_id=1, source_target_pairs={{0,1},{3,2},{2,3},{1,0},{4,5},{7,6},{6,7},{5,4},{8,9},{11,10},{10,... | collective-permute-start | bytes 1056776 | tf_op jit(solution)/shard_map/ppermute | solution.py:351
  35.8 7.1 %copy-start.6 = (s32[1,1,6,6]{3,1,2,0:T(1,128)S(1)}, s32[1,1,6,6]{3,1,2,0:T(1,128)}, u32[]{:S(2)}) copy-start(s32[1,1,6,6]{3,1,2,0:T(1,128)} %param.11) | copy-start | bytes 436
  35.8 9.6 %collective-permute-start.11 = (bf16[1408,128]{1,0:T(8,128)(2,1)S(1)}, bf16[1408,128]{1,0:T(8,128)(2,1)S(1)}, u32[]{:S(2)}, u32[]{:S(2)}) collective-permute-start(bf16[1408,128]{1,0:T(8,128)(2,1)S(1)} %lane1_4.1.refs_1_), channel_id=1, source_target_pairs={{1,2},{2,1},{5,6},{6,5},{9,10},{10,9},{13,14},{14,13},{17,18},{18,... | collective-permute-start | bytes 1081352 | tf_op jit(solution)/shard_map/ppermute | solution.py:351
  37.6 14.7 %collective-permute-start.10 = (bf16[1344,128]{1,0:T(8,128)(2,1)S(1)}, bf16[1344,128]{1,0:T(8,128)(2,1)S(1)}, u32[]{:S(2)}, u32[]{:S(2)}) collective-permute-start(bf16[1344,128]{1,0:T(8,128)(2,1)S(1)} %lane0_5.1.refs_1_), channel_id=1, source_target_pairs={{0,1},{3,2},{2,3},{1,0},{4,5},{7,6},{6,7},{5,4},{8,9},{11,10},{10,... | collective-permute-start | bytes 1032200 | tf_op jit(solution)/shard_map/ppermute | solution.py:351
  42.9 1.4 %copy-start.3 = (s32[48]{0:T(128)S(1)}, s32[48]{0:T(128)}, u32[]{:S(2)}) copy-start(s32[48]{0:T(128)} %atoms.1) | copy-start | bytes 580
  43.6 10.1 %collective-permute-start.13 = (bf16[1280,128]{1,0:T(8,128)(2,1)S(1)}, bf16[1280,128]{1,0:T(8,128)(2,1)S(1)}, u32[]{:S(2)}, u32[]{:S(2)}) collective-permute-start(bf16[1280,128]{1,0:T(8,128)(2,1)S(1)} %lane1_5.1.refs_3_.refs_1_), channel_id=1, source_target_pairs={{1,2},{2,1},{5,6},{6,5},{9,10},{10,9},{13,14},{14,13},{17,18},{18,... | collective-permute-start | bytes 983048 | tf_op jit(solution)/shard_map/ppermute | solution.py:351
  46.1 13.9 %collective-permute-start.14 = (bf16[1408,128]{1,0:T(8,128)(2,1)S(1)}, bf16[1408,128]{1,0:T(8,128)(2,1)S(1)}, u32[]{:S(2)}, u32[]{:S(2)}) collective-permute-start(bf16[1408,128]{1,0:T(8,128)(2,1)S(1)} %lane0_6.1.refs_1_), channel_id=1, source_target_pairs={{0,1},{3,2},{2,3},{1,0},{4,5},{7,6},{6,7},{5,4},{8,9},{11,10},{10,... | collective-permute-start | bytes 1081352 | tf_op jit(solution)/shard_map/ppermute | solution.py:351
  53.1 7.0 %collective-permute-start.12 = (bf16[1280,128]{1,0:T(8,128)(2,1)S(1)}, bf16[1280,128]{1,0:T(8,128)(2,1)S(1)}, u32[]{:S(2)}, u32[]{:S(2)}) collective-permute-start(bf16[1280,128]{1,0:T(8,128)(2,1)S(1)} %lane1_6.1.refs_1_), channel_id=1, source_target_pairs={{1,2},{2,1},{5,6},{6,5},{9,10},{10,9},{13,14},{14,13},{17,18},{18,... | collective-permute-start | bytes 983048 | tf_op jit(solution)/shard_map/ppermute | solution.py:351
  54.4 13.5 %collective-permute-start.16 = (bf16[1280,128]{1,0:T(8,128)(2,1)S(1)}, bf16[1280,128]{1,0:T(8,128)(2,1)S(1)}, u32[]{:S(2)}, u32[]{:S(2)}) collective-permute-start(bf16[1280,128]{1,0:T(8,128)(2,1)S(1)} %lane0_7.1.refs_1_), channel_id=1, source_target_pairs={{0,1},{3,2},{2,3},{1,0},{4,5},{7,6},{6,7},{5,4},{8,9},{11,10},{10,... | collective-permute-start | bytes 983048 | tf_op jit(solution)/shard_map/ppermute | solution.py:351
  60.8 11.0 %collective-permute-start.15 = (bf16[1280,128]{1,0:T(8,128)(2,1)S(1)}, bf16[1280,128]{1,0:T(8,128)(2,1)S(1)}, u32[]{:S(2)}, u32[]{:S(2)}) collective-permute-start(bf16[1280,128]{1,0:T(8,128)(2,1)S(1)} %lane0_8.1), channel_id=1, source_target_pairs={{0,1},{3,2},{2,3},{1,0},{4,5},{7,6},{6,7},{5,4},{8,9},{11,10},{10,... | collective-permute-start | bytes 983048 | tf_op jit(solution)/shard_map/ppermute | solution.py:351

commit v5 on v1

--- a/solution.py
+++ b/solution.py
@@ -330,7 +330,7 @@
             before = slot - 2
             if lane == 0 and before > 0 and before in edges:
                 after.append(edges[before])
-            if slot == plan_slot and lane == 0:
+            if slot == plan_slot and lane == 1:
                 plan = make_plan(
                     panel_owner, atom_size, stored_bc, moved_bc[0, 0], targets, notes, arrived[NOTED], nz, spots, newest
                 )

time: 72.3 us -> 73 us (level)
  Pallas kernels: 24.1 us -> 25.3 us
    pallas_call x3, Pallas kernels: 8.6 us -> 9.81 us  [multiply_rows(): pl.pallas_call(functools.partial(rows_kernel, first, count, hops, tuple(s...]
  transfers between devices with their start and end apart: 17 -> 17, of which waited for: 3 -> 2; matrix products, arithmetic and copies ran while one was open for 0% -> 0% of each run, Pallas kernels for 27% -> 28%
where the time goes in v5:
time: 73 us; the launch traced here: 72.9 us
  starting transfers between devices  44.9 us (62%)
  Pallas kernels  25.3 us (35%)
  waiting for transfers between devices  2.15 us (3%)
    ppermute x15, starting transfers between devices, local(): got = lax.ppermute(newest, 'col', route)  40.7 us
    pallas_call x15, Pallas kernels, relay(): pl.pallas_call(functools.partial(relay_kernel, roles, len(after)), out_sh...  14.4 us
    pallas_call x3, Pallas kernels, multiply_rows(): pl.pallas_call(functools.partial(rows_kernel, first, count, hops, tuple(s...  9.81 us
    ppermute x1, starting transfers between devices, local(): moved_b = lax.ppermute(behind_b, 'row', from_next)  2.6 us
    ppermute x15, waiting for transfers between devices, local(): got = lax.ppermute(newest, 'col', route)  1.82 us
    ppermute x1, starting transfers between devices, local(): moved_bc = lax.ppermute(behind_bc, 'row', from_next)  1.66 us
  transfers between devices with their start and end apart: 17, of which 2 were waited for; matrix products, arithmetic and copies ran while one was open for 0% of the time, Pallas kernels for 28%

profile of v5, /device:TPU:0, one launch (start us, length us, event | category | flops | bytes accessed | tf_op | source)
XLA Modules:
  0.0 72.9 jit_solution(10156958104376104221)
XLA Ops:
  0.0 2.6 %lane0_0.1 = bf16[1280,128]{1,0:T(8,128)(2,1)} custom-call(s32[8,8]{1,0:T(8,128)} %owner.37, bf16[2,6,640,128]{3,2,1,0:T(8,128)(2,1)} %bitcast.12), custom_call_target="tpu_custom_call" | custom-call | flops 1000000000 | bytes 1024 | tf_op jit(solution)/shard_map/lane0_0/pallas_call | solution.py:93
  2.6 2.1 %collective-permute-start.2 = (bf16[1280,128]{1,0:T(8,128)(2,1)}, bf16[1280,128]{1,0:T(8,128)(2,1)S(1)}, u32[]{:S(2)}, u32[]{:S(2)}) collective-permute-start(bf16[1280,128]{1,0:T(8,128)(2,1)} %lane0_0.1), channel_id=1, source_target_pairs={{0,1},{3,2},{2,3},{1,0},{4,5},{7,6},{6,7},{5,4},{8,9},{11,10},{10,... | collective-permute-start | bytes 983048 | tf_op jit(solution)/shard_map/ppermute | solution.py:351
  4.9 1.1 %lane0_1.1 = bf16[1312,128]{1,0:T(8,128)(2,1)S(1)} custom-call(s32[8,8]{1,0:T(8,128)S(1)} %copy-done.2, bf16[2,6,640,128]{3,2,1,0:T(8,128)(2,1)S(1)} %bitcast.13, bf16[2,16,128]{2,1,0:T(8,128)(2,1)S(1)} %pad.4.refs_0_.notes), custom_call_target="tpu_custom_call" | custom-call | flops 1000000000 | bytes 1024 | tf_op jit(solution)/shard_map/lane0_1/pallas_call | solution.py:93
  6.1 1.7 %collective-permute-start = (s32[1,1,6,8]{3,2,1,0:T(8,128)S(1)}, s32[1,1,6,8]{3,2,1,0:T(8,128)S(1)}, u32[]{:S(2)}, u32[]{:S(2)}) collective-permute-start(s32[1,1,6,8]{3,2,1,0:T(8,128)S(1)} %copy.11), channel_id=1, source_target_pairs={{4,0},{8,4},{12,8},{16,12},{20,16},{24,20},{28,24},{0,28},{5,1},{9... | collective-permute-start | bytes 584 | tf_op jit(solution)/shard_map/ppermute | solution.py:345
  7.7 1.0 %collective-permute-start.1 = (bf16[1312,128]{1,0:T(8,128)(2,1)S(1)}, bf16[1312,128]{1,0:T(8,128)(2,1)S(1)}, u32[]{:S(2)}, u32[]{:S(2)}) collective-permute-start(bf16[1312,128]{1,0:T(8,128)(2,1)S(1)} %lane0_1.1), channel_id=1, source_target_pairs={{0,1},{3,2},{2,3},{1,0},{4,5},{7,6},{6,7},{5,4},{8,9},{11,10},{10,... | collective-permute-start | bytes 1007624 | tf_op jit(solution)/shard_map/ppermute | solution.py:351
  9.1 2.6 %collective-permute-start.10 = (bf16[6,8,128,128]{3,2,1,0:T(8,128)(2,1)S(1)}, bf16[6,8,128,128]{3,2,1,0:T(8,128)(2,1)S(1)}, u32[]{:S(2)}, u32[]{:S(2)}) collective-permute-start(bf16[6,8,128,128]{3,2,1,0:T(8,128)(2,1)S(1)} %bitcast.30), channel_id=1, source_target_pairs={{4,0},{8,4},{12,8},{16,12},{20,16},{24,20},{28,24},{0,28},{5,1},{9... | collective-permute-start | bytes 4718600 | tf_op jit(solution)/shard_map/ppermute | solution.py:347
  11.7 1.8 %collective-permute-done.2.refs_0_ = bf16[1280,128]{1,0:T(8,128)(2,1)S(1)} collective-permute-done((bf16[1280,128]{1,0:T(8,128)(2,1)}, bf16[1280,128]{1,0:T(8,128)(2,1)S(1)}, u32[]{:S(2)}, u32[]{:S(2)}) %collective-permute-start.2) | collective-permute-done | bytes 327712 | tf_op jit(solution)/shard_map/ppermute | solution.py:351
  14.8 1.1 %lane0_2.1.refs_2_ = bf16[1280,128]{1,0:T(8,128)(2,1)S(1)} custom-call(s32[8,8]{1,0:T(8,128)S(1)} %copy-done.2, bf16[2,6,640,128]{3,2,1,0:T(8,128)(2,1)S(1)} %bitcast.15, bf16[1280,128]{1,0:T(8,128)(2,1)S(1)} %lane1_1.1.refs_0_), custom_call_target="tpu_custom_call" | custom-call | flops 3000000000 | bytes 1024 | tf_op jit(solution)/shard_map/lane0_2/pallas_call | solution.py:93
  15.9 5.3 %collective-permute-start.4 = (bf16[1280,128]{1,0:T(8,128)(2,1)S(1)}, bf16[1280,128]{1,0:T(8,128)(2,1)S(1)}, u32[]{:S(2)}, u32[]{:S(2)}) collective-permute-start(bf16[1280,128]{1,0:T(8,128)(2,1)S(1)} %lane0_2.1.refs_2_), channel_id=1, source_target_pairs={{0,1},{3,2},{2,3},{1,0},{4,5},{7,6},{6,7},{5,4},{8,9},{11,10},{10,... | collective-permute-start | bytes 983048 | tf_op jit(solution)/shard_map/ppermute | solution.py:351
  21.2 0.7 %lane1_2.1.refs_1_ = bf16[1312,128]{1,0:T(8,128)(2,1)S(1)} custom-call(s32[8,8]{1,0:T(8,128)S(1)} %copy-done.2, bf16[2,6,640,128]{3,2,1,0:T(8,128)(2,1)S(1)} %bitcast.16, bf16[2,16,128]{2,1,0:T(8,128)(2,1)S(1)} %pad.4.refs_0_.notes, bf16[1312,128]{1,0:T(8,128)(2,1)S(1)} %collective-permute-done.1.refs_1_.refs_2_.refs_0_.refs_3_, ...), custom_call_target="tpu_custom_call" | custom-call | flops 2000000000 | bytes 1024 | tf_op jit(solution)/shard_map/lane1_2/pallas_call | solution.py:93
  21.9 0.7 collective-permute-start.3
  22.6 1.1 %lane0_3.1.refs_1_ = bf16[1280,128]{1,0:T(8,128)(2,1)S(1)} custom-call(s32[8,8]{1,0:T(8,128)S(1)} %copy-done.2, bf16[2,6,640,128]{3,2,1,0:T(8,128)(2,1)S(1)} %bitcast.17, bf16[1280,128]{1,0:T(8,128)(2,1)S(1)} %collective-permute-done.5.refs_0_.refs_1_, bf16[1312,128]{1,0:T(8,128)(2,1)S(1)} %lane1_2.1.refs_1_, ...), custom_call_target="tpu_custom_call" | custom-call | flops 1000000000 | bytes 1024 | tf_op jit(solution)/shard_map/lane0_3/pallas_call | solution.py:93
  23.7 4.7 %collective-permute-start.7 = (bf16[1280,128]{1,0:T(8,128)(2,1)S(1)}, bf16[1280,128]{1,0:T(8,128)(2,1)S(1)}, u32[]{:S(2)}, u32[]{:S(2)}) collective-permute-start(bf16[1280,128]{1,0:T(8,128)(2,1)S(1)} %lane0_3.1.refs_1_), channel_id=1, source_target_pairs={{0,1},{3,2},{2,3},{1,0},{4,5},{7,6},{6,7},{5,4},{8,9},{11,10},{10,... | collective-permute-start | bytes 983048 | tf_op jit(solution)/shard_map/ppermute | solution.py:351
  29.9 1.2 %lane0_4.1.refs_1_ = bf16[1312,128]{1,0:T(8,128)(2,1)S(1)} custom-call(s32[8,8]{1,0:T(8,128)S(1)} %copy-done.2, bf16[2,6,640,128]{3,2,1,0:T(8,128)(2,1)S(1)} %bitcast.19, bf16[2,16,128]{2,1,0:T(8,128)(2,1)S(1)} %pad.4.refs_0_.notes, bf16[1312,128]{1,0:T(8,128)(2,1)S(1)} %collective-permute-done.3.refs_1_.refs_4_, bf16[1280,128]{1,0:T(8,128)(2,1)S(1)} %lane1_3.1.refs_2_, ...), custom_call_target="tpu_custom_call" | custom-call | flops 1000000000 | bytes 1024 | tf_op jit(solution)/shard_map/lane0_4/pallas_call | solution.py:93
  31.1 4.5 %collective-permute-start.6 = (bf16[1312,128]{1,0:T(8,128)(2,1)S(1)}, bf16[1312,128]{1,0:T(8,128)(2,1)S(1)}, u32[]{:S(2)}, u32[]{:S(2)}) collective-permute-start(bf16[1312,128]{1,0:T(8,128)(2,1)S(1)} %lane0_4.1.refs_1_), channel_id=1, source_target_pairs={{0,1},{3,2},{2,3},{1,0},{4,5},{7,6},{6,7},{5,4},{8,9},{11,10},{10,... | collective-permute-start | bytes 1007624 | tf_op jit(solution)/shard_map/ppermute | solution.py:351
  36.9 1.1 %lane0_5.1.refs_1_ = bf16[1280,128]{1,0:T(8,128)(2,1)S(1)} custom-call(s32[8,8]{1,0:T(8,128)S(1)} %copy-done.2, bf16[2,6,640,128]{3,2,1,0:T(8,128)(2,1)S(1)} %bitcast.21, bf16[1280,128]{1,0:T(8,128)(2,1)S(1)} %collective-permute-done.9.refs_0_.refs_7_, bf16[1280,128]{1,0:T(8,128)(2,1)S(1)} %lane1_4.1.refs_1_, ...), custom_call_target="tpu_custom_call" | custom-call | flops 1000000000 | bytes 1024 | tf_op jit(solution)/shard_map/lane0_5/pallas_call | solution.py:93
  38.0 5.2 %collective-permute-start.11 = (bf16[1280,128]{1,0:T(8,128)(2,1)S(1)}, bf16[1280,128]{1,0:T(8,128)(2,1)S(1)}, u32[]{:S(2)}, u32[]{:S(2)}) collective-permute-start(bf16[1280,128]{1,0:T(8,128)(2,1)S(1)} %lane0_5.1.refs_1_), channel_id=1, source_target_pairs={{0,1},{3,2},{2,3},{1,0},{4,5},{7,6},{6,7},{5,4},{8,9},{11,10},{10,... | collective-permute-start | bytes 983048 | tf_op jit(solution)/shard_map/ppermute | solution.py:351
  45.3 4.7 %collective-permute-start.14 = (bf16[1280,128]{1,0:T(8,128)(2,1)S(1)}, bf16[1280,128]{1,0:T(8,128)(2,1)S(1)}, u32[]{:S(2)}, u32[]{:S(2)}) collective-permute-start(bf16[1280,128]{1,0:T(8,128)(2,1)S(1)} %lane0_6.1.refs_3_.refs_1_), channel_id=1, source_target_pairs={{0,1},{3,2},{2,3},{1,0},{4,5},{7,6},{6,7},{5,4},{8,9},{11,10},{10,... | collective-permute-start | bytes 983048 | tf_op jit(solution)/shard_map/ppermute | solution.py:351
  50.0 1.1 %make_plan.1.refs_3_.plan = s32[16,128]{1,0:T(8,128)S(1)} custom-call(s32[8,8]{1,0:T(8,128)S(1)} %copy-done.2, s32[48]{0:T(128)S(1)} %copy-done.3, s32[6,8]{1,0:T(8,128)S(1)} %bitcast.34, s32[6,8]{1,0:T(8,128)S(1)} %bitcast.36, s32[6,6]{1,0:T(8,128)S(1)} %bitcast.35, bf16[2,16,128]{2,1,0:T(8,128)(2,1)S(1)} %pad.4.refs_0_.notes, ...), custom_call_target="tpu_custom_call" | custom-call | flops 1000000000 | bytes 1024 | tf_op jit(solution)/shard_map/make_plan/pallas_call | solution.py:175
  53.2 4.3 %collective-permute-start.16 = (bf16[1280,128]{1,0:T(8,128)(2,1)S(1)}, bf16[1280,128]{1,0:T(8,128)(2,1)S(1)}, u32[]{:S(2)}, u32[]{:S(2)}) collective-permute-start(bf16[1280,128]{1,0:T(8,128)(2,1)S(1)} %lane0_7.1.refs_1_), channel_id=1, source_target_pairs={{0,1},{3,2},{2,3},{1,0},{4,5},{7,6},{6,7},{5,4},{8,9},{11,10},{10,... | collective-permute-start | bytes 983048 | tf_op jit(solution)/shard_map/ppermute | solution.py:351
  58.2 4.8 %collective-permute-start.15 = (bf16[1280,128]{1,0:T(8,128)(2,1)S(1)}, bf16[1280,128]{1,0:T(8,128)(2,1)S(1)}, u32[]{:S(2)}, u32[]{:S(2)}) collective-permute-start(bf16[1280,128]{1,0:T(8,128)(2,1)S(1)} %lane0_8.1), channel_id=1, source_target_pairs={{0,1},{3,2},{2,3},{1,0},{4,5},{7,6},{6,7},{5,4},{8,9},{11,10},{10,... | collective-permute-start | bytes 983048 | tf_op jit(solution)/shard_map/ppermute | solution.py:351
  63.1 5.1 %multiply_rows.3.refs_3_ = bf16[6,6,128,128]{3,2,1,0:T(8,128)(2,1)} custom-call(s32[8,8]{1,0:T(8,128)S(1)} %copy-done.2, s32[16,128]{1,0:T(8,128)S(1)} %make_plan.1.refs_3_.plan, bf16[6,8,128,128]{3,2,1,0:T(8,128)(2,1)S(1)} %bitcast.31, bf16[6,8,128,128]{3,2,1,0:T(8,128)(2,1)S(1)} %collective-permute-done.10.refs_2_.b1, ...), custom_call_target="tpu_custom_call" | custom-call | flops 2013265920 | bytes 4194304 | tf_op jit(solution)/shard_map/multiply_rows/pallas_call | solution.py:277
  68.2 2.4 %multiply_rows.4.refs_3_ = bf16[6,6,128,128]{3,2,1,0:T(8,128)(2,1)} custom-call(s32[8,8]{1,0:T(8,128)S(1)} %copy-done.2, s32[16,128]{1,0:T(8,128)S(1)} %make_plan.1.refs_3_.plan, bf16[6,8,128,128]{3,2,1,0:T(8,128)(2,1)S(1)} %bitcast.32, bf16[6,8,128,128]{3,2,1,0:T(8,128)(2,1)S(1)} %collective-permute-done.10.refs_2_.b1, ...), custom_call_target="tpu_custom_call", output_to_operand_aliasing={{}: (8, {})} | custom-call | flops 503316480 | bytes 4194304 | tf_op jit(solution)/shard_map/multiply_rows/pallas_call | solution.py:277
  70.5 2.4 %multiply_rows.5 = bf16[6,6,128,128]{3,2,1,0:T(8,128)(2,1)} custom-call(s32[8,8]{1,0:T(8,128)S(1)} %copy-done.2, s32[16,128]{1,0:T(8,128)S(1)} %make_plan.1.refs_3_.plan, bf16[6,8,128,128]{3,2,1,0:T(8,128)(2,1)S(1)} %bitcast.33, bf16[6,8,128,128]{3,2,1,0:T(8,128)(2,1)S(1)} %collective-permute-done.10.refs_2_.b1, ...), custom_call_target="tpu_custom_call", output_to_operand_aliasing={{}: (8, {})} | custom-call | flops 503316480 | bytes 4194304 | tf_op jit(solution)/shard_map/multiply_rows/pallas_call | solution.py:277
  (49 shorter events, 9.4 us)
Async XLA Ops:
  0.0 4.7 %copy-start.5 = (s32[1,1,2,6,5]{3,2,4,1,0:T(2,128)S(1)}, s32[1,1,2,6,5]{3,2,4,1,0:T(2,128)}, u32[]{:S(2)}) copy-start(s32[1,1,2,6,5]{3,2,4,1,0:T(2,128)} %param.8) | copy-start | bytes 724
  0.0 4.9 %copy-start = (bf16[1,1,2,6,5,128,128]{6,5,4,3,2,1,0:T(8,128)(2,1)S(1)}, bf16[1,1,2,6,5,128,128]{6,5,4,3,2,1,0:T(8,128)(2,1)}, u32[]{:S(2)}) copy-start(bf16[1,1,2,6,5,128,128]{6,5,4,3,2,1,0:T(8,128)(2,1)} %param.7) | copy-start | bytes 5898244
  0.0 4.9 %copy-start.2 = (s32[8,8]{1,0:T(8,128)S(1)}, s32[8,8]{1,0:T(8,128)}, u32[]{:S(2)}) copy-start(s32[8,8]{1,0:T(8,128)} %owner.37) | copy-start | bytes 772
  2.6 10.8 %collective-permute-start.2 = (bf16[1280,128]{1,0:T(8,128)(2,1)}, bf16[1280,128]{1,0:T(8,128)(2,1)S(1)}, u32[]{:S(2)}, u32[]{:S(2)}) collective-permute-start(bf16[1280,128]{1,0:T(8,128)(2,1)} %lane0_0.1), channel_id=1, source_target_pairs={{0,1},{3,2},{2,3},{1,0},{4,5},{7,6},{6,7},{5,4},{8,9},{11,10},{10,... | collective-permute-start | bytes 983048 | tf_op jit(solution)/shard_map/ppermute | solution.py:351
  4.9 1.2 %copy-start.4 = (s32[1,1,6,8]{3,1,2,0:T(1,128)S(1)}, s32[1,1,6,8]{3,1,2,0:T(1,128)}, u32[]{:S(2)}) copy-start(s32[1,1,6,8]{3,1,2,0:T(1,128)} %param.10) | copy-start | bytes 580
  4.9 4.2 %copy-start.1 = (bf16[1,1,6,8,128,128]{5,4,3,2,1,0:T(8,128)(2,1)S(1)}, bf16[1,1,6,8,128,128]{5,4,3,2,1,0:T(8,128)(2,1)}, u32[]{:S(2)}) copy-start(bf16[1,1,6,8,128,128]{5,4,3,2,1,0:T(8,128)(2,1)} %param.9) | copy-start | bytes 4718596
  6.1 3.0 %collective-permute-start = (s32[1,1,6,8]{3,2,1,0:T(8,128)S(1)}, s32[1,1,6,8]{3,2,1,0:T(8,128)S(1)}, u32[]{:S(2)}, u32[]{:S(2)}) collective-permute-start(s32[1,1,6,8]{3,2,1,0:T(8,128)S(1)} %copy.11), channel_id=1, source_target_pairs={{4,0},{8,4},{12,8},{16,12},{20,16},{24,20},{28,24},{0,28},{5,1},{9... | collective-permute-start | bytes 584 | tf_op jit(solution)/shard_map/ppermute | solution.py:345
  7.7 13.5 %collective-permute-start.1 = (bf16[1312,128]{1,0:T(8,128)(2,1)S(1)}, bf16[1312,128]{1,0:T(8,128)(2,1)S(1)}, u32[]{:S(2)}, u32[]{:S(2)}) collective-permute-start(bf16[1312,128]{1,0:T(8,128)(2,1)S(1)} %lane0_1.1), channel_id=1, source_target_pairs={{0,1},{3,2},{2,3},{1,0},{4,5},{7,6},{6,7},{5,4},{8,9},{11,10},{10,... | collective-permute-start | bytes 1007624 | tf_op jit(solution)/shard_map/ppermute | solution.py:351
  9.1 42.1 %collective-permute-start.10 = (bf16[6,8,128,128]{3,2,1,0:T(8,128)(2,1)S(1)}, bf16[6,8,128,128]{3,2,1,0:T(8,128)(2,1)S(1)}, u32[]{:S(2)}, u32[]{:S(2)}) collective-permute-start(bf16[6,8,128,128]{3,2,1,0:T(8,128)(2,1)S(1)} %bitcast.30), channel_id=1, source_target_pairs={{4,0},{8,4},{12,8},{16,12},{20,16},{24,20},{28,24},{0,28},{5,1},{9... | collective-permute-start | bytes 4718600 | tf_op jit(solution)/shard_map/ppermute | solution.py:347
  14.1 8.5 %collective-permute-start.5 = (bf16[1280,128]{1,0:T(8,128)(2,1)S(1)}, bf16[1280,128]{1,0:T(8,128)(2,1)S(1)}, u32[]{:S(2)}, u32[]{:S(2)}) collective-permute-start(bf16[1280,128]{1,0:T(8,128)(2,1)S(1)} %lane1_1.1.refs_0_), channel_id=1, source_target_pairs={{1,2},{2,1},{5,6},{6,5},{9,10},{10,9},{13,14},{14,13},{17,18},{18,... | collective-permute-start | bytes 983048 | tf_op jit(solution)/shard_map/ppermute | solution.py:351
  15.9 12.6 %collective-permute-start.4 = (bf16[1280,128]{1,0:T(8,128)(2,1)S(1)}, bf16[1280,128]{1,0:T(8,128)(2,1)S(1)}, u32[]{:S(2)}, u32[]{:S(2)}) collective-permute-start(bf16[1280,128]{1,0:T(8,128)(2,1)S(1)} %lane0_2.1.refs_2_), channel_id=1, source_target_pairs={{0,1},{3,2},{2,3},{1,0},{4,5},{7,6},{6,7},{5,4},{8,9},{11,10},{10,... | collective-permute-start | bytes 983048 | tf_op jit(solution)/shard_map/ppermute | solution.py:351
  21.9 7.9 %collective-permute-start.3 = (bf16[1312,128]{1,0:T(8,128)(2,1)S(1)}, bf16[1312,128]{1,0:T(8,128)(2,1)S(1)}, u32[]{:S(2)}, u32[]{:S(2)}) collective-permute-start(bf16[1312,128]{1,0:T(8,128)(2,1)S(1)} %lane1_2.1.refs_1_), channel_id=1, source_target_pairs={{1,2},{2,1},{5,6},{6,5},{9,10},{10,9},{13,14},{14,13},{17,18},{18,... | collective-permute-start | bytes 1007624 | tf_op jit(solution)/shard_map/ppermute | solution.py:351
  23.7 11.8 %collective-permute-start.7 = (bf16[1280,128]{1,0:T(8,128)(2,1)S(1)}, bf16[1280,128]{1,0:T(8,128)(2,1)S(1)}, u32[]{:S(2)}, u32[]{:S(2)}) collective-permute-start(bf16[1280,128]{1,0:T(8,128)(2,1)S(1)} %lane0_3.1.refs_1_), channel_id=1, source_target_pairs={{0,1},{3,2},{2,3},{1,0},{4,5},{7,6},{6,7},{5,4},{8,9},{11,10},{10,... | collective-permute-start | bytes 983048 | tf_op jit(solution)/shard_map/ppermute | solution.py:351
  29.2 7.7 %collective-permute-start.9 = (bf16[1280,128]{1,0:T(8,128)(2,1)S(1)}, bf16[1280,128]{1,0:T(8,128)(2,1)S(1)}, u32[]{:S(2)}, u32[]{:S(2)}) collective-permute-start(bf16[1280,128]{1,0:T(8,128)(2,1)S(1)} %lane1_3.1.refs_2_), channel_id=1, source_target_pairs={{1,2},{2,1},{5,6},{6,5},{9,10},{10,9},{13,14},{14,13},{17,18},{18,... | collective-permute-start | bytes 983048 | tf_op jit(solution)/shard_map/ppermute | solution.py:351
  31.1 12.2 %collective-permute-start.6 = (bf16[1312,128]{1,0:T(8,128)(2,1)S(1)}, bf16[1312,128]{1,0:T(8,128)(2,1)S(1)}, u32[]{:S(2)}, u32[]{:S(2)}) collective-permute-start(bf16[1312,128]{1,0:T(8,128)(2,1)S(1)} %lane0_4.1.refs_1_), channel_id=1, source_target_pairs={{0,1},{3,2},{2,3},{1,0},{4,5},{7,6},{6,7},{5,4},{8,9},{11,10},{10,... | collective-permute-start | bytes 1007624 | tf_op jit(solution)/shard_map/ppermute | solution.py:351
  36.2 7.0 %copy-start.6 = (s32[1,1,6,6]{3,1,2,0:T(1,128)S(1)}, s32[1,1,6,6]{3,1,2,0:T(1,128)}, u32[]{:S(2)}) copy-start(s32[1,1,6,6]{3,1,2,0:T(1,128)} %param.11) | copy-start | bytes 436
  36.2 8.4 %collective-permute-start.8 = (bf16[1280,128]{1,0:T(8,128)(2,1)S(1)}, bf16[1280,128]{1,0:T(8,128)(2,1)S(1)}, u32[]{:S(2)}, u32[]{:S(2)}) collective-permute-start(bf16[1280,128]{1,0:T(8,128)(2,1)S(1)} %lane1_4.1.refs_1_), channel_id=1, source_target_pairs={{1,2},{2,1},{5,6},{6,5},{9,10},{10,9},{13,14},{14,13},{17,18},{18,... | collective-permute-start | bytes 983048 | tf_op jit(solution)/shard_map/ppermute | solution.py:351
  38.0 13.1 %collective-permute-start.11 = (bf16[1280,128]{1,0:T(8,128)(2,1)S(1)}, bf16[1280,128]{1,0:T(8,128)(2,1)S(1)}, u32[]{:S(2)}, u32[]{:S(2)}) collective-permute-start(bf16[1280,128]{1,0:T(8,128)(2,1)S(1)} %lane0_5.1.refs_1_), channel_id=1, source_target_pairs={{0,1},{3,2},{2,3},{1,0},{4,5},{7,6},{6,7},{5,4},{8,9},{11,10},{10,... | collective-permute-start | bytes 983048 | tf_op jit(solution)/shard_map/ppermute | solution.py:351
  43.9 6.1 %copy-start.3 = (s32[48]{0:T(128)S(1)}, s32[48]{0:T(128)}, u32[]{:S(2)}) copy-start(s32[48]{0:T(128)} %atoms.1) | copy-start | bytes 580
  43.9 8.6 %collective-permute-start.13 = (bf16[1280,128]{1,0:T(8,128)(2,1)S(1)}, bf16[1280,128]{1,0:T(8,128)(2,1)S(1)}, u32[]{:S(2)}, u32[]{:S(2)}) collective-permute-start(bf16[1280,128]{1,0:T(8,128)(2,1)S(1)} %lane1_5.1.refs_1_), channel_id=1, source_target_pairs={{1,2},{2,1},{5,6},{6,5},{9,10},{10,9},{13,14},{14,13},{17,18},{18,... | collective-permute-start | bytes 983048 | tf_op jit(solution)/shard_map/ppermute | solution.py:351
  45.3 12.2 %collective-permute-start.14 = (bf16[1280,128]{1,0:T(8,128)(2,1)S(1)}, bf16[1280,128]{1,0:T(8,128)(2,1)S(1)}, u32[]{:S(2)}, u32[]{:S(2)}) collective-permute-start(bf16[1280,128]{1,0:T(8,128)(2,1)S(1)} %lane0_6.1.refs_3_.refs_1_), channel_id=1, source_target_pairs={{0,1},{3,2},{2,3},{1,0},{4,5},{7,6},{6,7},{5,4},{8,9},{11,10},{10,... | collective-permute-start | bytes 983048 | tf_op jit(solution)/shard_map/ppermute | solution.py:351
  51.8 5.7 %collective-permute-start.12 = (bf16[1280,128]{1,0:T(8,128)(2,1)S(1)}, bf16[1280,128]{1,0:T(8,128)(2,1)S(1)}, u32[]{:S(2)}, u32[]{:S(2)}) collective-permute-start(bf16[1280,128]{1,0:T(8,128)(2,1)S(1)} %lane1_6.1.refs_1_), channel_id=1, source_target_pairs={{1,2},{2,1},{5,6},{6,5},{9,10},{10,9},{13,14},{14,13},{17,18},{18,... | collective-permute-start | bytes 983048 | tf_op jit(solution)/shard_map/ppermute | solution.py:351
  53.2 14.9 %collective-permute-start.16 = (bf16[1280,128]{1,0:T(8,128)(2,1)S(1)}, bf16[1280,128]{1,0:T(8,128)(2,1)S(1)}, u32[]{:S(2)}, u32[]{:S(2)}) collective-permute-start(bf16[1280,128]{1,0:T(8,128)(2,1)S(1)} %lane0_7.1.refs_1_), channel_id=1, source_target_pairs={{0,1},{3,2},{2,3},{1,0},{4,5},{7,6},{6,7},{5,4},{8,9},{11,10},{10,... | collective-permute-start | bytes 983048 | tf_op jit(solution)/shard_map/ppermute | solution.py:351
  58.2 12.3 %collective-permute-start.15 = (bf16[1280,128]{1,0:T(8,128)(2,1)S(1)}, bf16[1280,128]{1,0:T(8,128)(2,1)S(1)}, u32[]{:S(2)}, u32[]{:S(2)}) collective-permute-start(bf16[1280,128]{1,0:T(8,128)(2,1)S(1)} %lane0_8.1), channel_id=1, source_target_pairs={{0,1},{3,2},{2,3},{1,0},{4,5},{7,6},{6,7},{5,4},{8,9},{11,10},{10,... | collective-permute-start | bytes 983048 | tf_op jit(solution)/shard_map/ppermute | solution.py:351
